TPU v7x, 32 devices: a whole 2x2x4 slice. The times are simulated.
32 devices in a mesh: batch: 16 (over z, x, core), seq: 2 (over y).
Axes of the slice: x: 2, y: 2, z: 4, core: 2. Of those that a mesh axis runs over, the one named last changes fastest.
Arguments:
- inputs: bfloat16 [64, 128, 768], P('batch', 'seq'), may hold values from -6 to 6
- time_embed: bfloat16 [64, 768], P('batch'), may hold values from -3 to 3
- segment_ids: int32 [64, 128], P('batch'), may hold values from 0 to 3, never falling along the last dimension, each value on 1 to 64 neighbouring positions
- cotangent: bfloat16 [64, 128, 768], P('batch', 'seq'), may hold values from -6 to 6
- first_gain: bfloat16 [768], P(('batch', 'seq')), may hold values from 0.5 to 1.5
- first_shift: bfloat16 [768], P(('batch', 'seq')), may hold values from -1.5 to 1.5
- mix_weight: bfloat16 [768, 2304], P(('batch', 'seq')), may hold values from -0.21875 to 0.21875
- mix_bias: bfloat16 [1536], P(('batch', 'seq')), may hold values from -1.5 to 1.5
- out_weight: bfloat16 [768, 768], P(('batch', 'seq')), may hold values from -1.25 to 1.25
- out_bias: bfloat16 [768], P(('batch', 'seq')), may hold values from -1.5 to 1.5
- second_gain: bfloat16 [768], P(('batch', 'seq')), may hold values from 0.5 to 1.5
- second_shift: bfloat16 [768], P(('batch', 'seq')), may hold values from -1.5 to 1.5
- up_weight: bfloat16 [768, 3072], P(('batch', 'seq')), may hold values from -0.21875 to 0.21875
- up_bias: bfloat16 [3072], P(('batch', 'seq')), may hold values from -1.5 to 1.5
- down_weight: bfloat16 [3072, 768], P(('batch', 'seq')), may hold values from -0.109375 to 0.109375
- down_bias: bfloat16 [768], P(('batch', 'seq')), may hold values from -1.5 to 1.5
Outputs:
- layer_out: bfloat16 [64, 128, 768], P('batch', 'seq')
- inputs_grad: float32 [64, 128, 768], P('batch', 'seq')
- time_grad: float32 [64, 768], P('batch', 'seq')
- first_gain_grad: float32 [768], P(('batch', 'seq'))
- first_shift_grad: float32 [768], P(('batch', 'seq'))
- mix_weight_grad: float32 [768, 2304], P(('batch', 'seq'))
- mix_bias_grad: float32 [1536], P(('batch', 'seq'))
- out_weight_grad: float32 [768, 768], P(('batch', 'seq'))
- out_bias_grad: float32 [768], P(('batch', 'seq'))
- second_gain_grad: float32 [768], P(('batch', 'seq'))
- second_shift_grad: float32 [768], P(('batch', 'seq'))
- up_weight_grad: float32 [768, 3072], P(('batch', 'seq'))
- up_bias_grad: float32 [3072], P(('batch', 'seq'))
- down_weight_grad: float32 [3072, 768], P(('batch', 'seq'))
- down_bias_grad: float32 [768], P(('batch', 'seq'))
Inputs may be any that keep to these rules, and one draw needn't show every extreme that they name: `segment_ids`: in each row of 128 positions the ids never fall, every id appears, and a document spans 1 to 64 positions.
All inputs are finite; a program needn't handle non-finite values.
Results may differ from a plain program's by a relative error of at most 0.0096.
Values may be sent and summed in bfloat16 or wider, within the bound.
A program may use at most 192 MiB of HBM per device.

v0:
```python
from functools import partial
import math

import jax
import jax.numpy as jnp
from jax import lax
from jax.sharding import PartitionSpec as P

HEAD_DIM = 64


EPSILON = 1e-05
NEG_FILL = -1e30


def layer_norm(hidden, norm_gain, norm_shift):
    average = jnp.mean(hidden, axis=-1, keepdims=True)
    centred = hidden - average
    spread = jnp.mean(centred * centred, axis=-1, keepdims=True)
    return centred * lax.rsqrt(spread + EPSILON) * norm_gain + norm_shift


def row_block(row_count, per_row):
    row_limit = min(max(1, 1024 // per_row), row_count)
    return max((divisor for divisor in range(1, row_limit + 1) if row_count % divisor == 0))


def split_rows(tensor, block_rows):
    return tensor.reshape((tensor.shape[0] // block_rows, block_rows) + tensor.shape[1:])


def masked_scores(query_blk, key_blk, query_seg, key_seg, scale_factor):
    scores = (
        jnp.einsum("rqhe,rkhe->rhqk", query_blk, key_blk, preferred_element_type=jnp.float32)
        * scale_factor
    )
    same_segment = query_seg[:, None, :, None] == key_seg[:, None, None, :]
    return jnp.where(same_segment, scores, NEG_FILL)


def attend_forward(queries, key_rows, values, query_ids, key_ids, scale_factor):
    row_count = queries.shape[0]
    block_rows = row_block(row_count, queries.shape[1])

    def one_block(pieces):
        query_blk, key_blk, value_blk, query_seg, key_seg = pieces
        masked = masked_scores(query_blk, key_blk, query_seg, key_seg, scale_factor)
        largest = jnp.max(masked, axis=-1, keepdims=True)
        log_total = largest + jnp.log(jnp.sum(jnp.exp(masked - largest), axis=-1, keepdims=True))
        weights_low = jnp.exp(masked - log_total).astype(jnp.bfloat16)
        attended = jnp.einsum(
            "rhqk,rkhe->rqhe", weights_low, value_blk, preferred_element_type=jnp.float32
        )
        return (attended, log_total[..., 0])

    attended, log_total = lax.map(
        one_block,
        tuple(
            (
                split_rows(tensor, block_rows)
                for tensor in (queries, key_rows, values, query_ids, key_ids)
            )
        ),
    )
    return (attended.reshape(queries.shape), log_total.reshape((row_count,) + log_total.shape[2:]))


def attend_backward(
    queries, key_rows, values, grad_out, log_total, query_ids, key_ids, scale_factor
):
    row_count = queries.shape[0]
    block_rows = row_block(row_count, queries.shape[1])

    def one_block(pieces):
        query_blk, key_blk, value_blk, grad_blk, total_blk, query_seg, key_seg = pieces
        masked = masked_scores(query_blk, key_blk, query_seg, key_seg, scale_factor)
        weights_soft = jnp.exp(masked - total_blk[..., None])
        d_weights = jnp.einsum(
            "rqhe,rkhe->rhqk", grad_blk, value_blk, preferred_element_type=jnp.float32
        )
        centre = jnp.sum(weights_soft * d_weights, axis=-1, keepdims=True)
        d_scores = (weights_soft * (d_weights - centre)).astype(jnp.bfloat16)
        grad_query = (
            jnp.einsum("rhqk,rkhe->rqhe", d_scores, key_blk, preferred_element_type=jnp.float32)
            * scale_factor
        )
        grad_key = (
            jnp.einsum("rhqk,rqhe->rkhe", d_scores, query_blk, preferred_element_type=jnp.float32)
            * scale_factor
        )
        grad_value = jnp.einsum(
            "rhqk,rqhe->rkhe",
            weights_soft.astype(jnp.bfloat16),
            grad_blk,
            preferred_element_type=jnp.float32,
        )
        return (grad_query, grad_key, grad_value)

    grad_query, grad_key, grad_value = lax.map(
        one_block,
        tuple(
            (
                split_rows(tensor, block_rows)
                for tensor in (queries, key_rows, values, grad_out, log_total, query_ids, key_ids)
            )
        ),
    )
    return (
        grad_query.reshape(queries.shape),
        grad_key.reshape(key_rows.shape),
        grad_value.reshape(values.shape),
    )


def to_heads_shape(tensor):
    return tensor.reshape(tensor.shape[:2] + (tensor.shape[2] // HEAD_DIM, HEAD_DIM))


def forward_state(params, inputs, time_embed, segment_ids):
    (
        first_gain,
        first_shift,
        mix_weight,
        mix_bias,
        out_weight,
        out_bias,
        second_gain,
        second_shift,
        up_weight,
        up_bias,
        down_weight,
        down_bias,
    ) = params
    scale_factor = 1.0 / math.sqrt(HEAD_DIM)
    model_width = inputs.shape[-1]
    residual_in = inputs.astype(jnp.float32) + time_embed.astype(jnp.float32)[:, None, :]
    normed_one, norm_one_back = jax.vjp(
        layer_norm, residual_in, first_gain.astype(jnp.float32), first_shift.astype(jnp.float32)
    )
    normed_one = normed_one.astype(jnp.bfloat16)
    projected = jnp.einsum(
        "rtd,de->rte", normed_one, mix_weight, preferred_element_type=jnp.float32
    )
    bias_float = mix_bias.astype(jnp.float32)
    queries = (projected[..., :model_width] + bias_float[:model_width]).astype(jnp.bfloat16)
    key_rows = projected[..., model_width : 2 * model_width].astype(jnp.bfloat16)
    values = (projected[..., 2 * model_width :] + bias_float[model_width:]).astype(jnp.bfloat16)
    head_query, head_key, head_value = (
        lax.all_to_all(queries, "seq", split_axis=2, concat_axis=1, tiled=True),
        lax.all_to_all(key_rows, "seq", split_axis=2, concat_axis=1, tiled=True),
        lax.all_to_all(values, "seq", split_axis=2, concat_axis=1, tiled=True),
    )
    attended, log_total = attend_forward(
        to_heads_shape(head_query),
        to_heads_shape(head_key),
        to_heads_shape(head_value),
        segment_ids,
        segment_ids,
        scale_factor,
    )
    attended_heads = attended.reshape(head_query.shape).astype(jnp.bfloat16)
    attended_rows = lax.all_to_all(attended_heads, "seq", split_axis=1, concat_axis=2, tiled=True)
    kept_attention = (head_query, head_key, head_value, log_total, segment_ids)
    branch = jnp.einsum(
        "rtc,cd->rtd", attended_rows, out_weight, preferred_element_type=jnp.float32
    ) + out_bias.astype(jnp.float32)
    residual_mid = residual_in + branch
    normed_two, norm_two_back = jax.vjp(
        layer_norm, residual_mid, second_gain.astype(jnp.float32), second_shift.astype(jnp.float32)
    )
    normed_two = normed_two.astype(jnp.bfloat16)
    hidden_up = jnp.einsum(
        "rtd,df->rtf", normed_two, up_weight, preferred_element_type=jnp.float32
    ) + up_bias.astype(jnp.float32)
    activation, gelu_back = jax.vjp(partial(jax.nn.gelu, approximate=False), hidden_up)
    activation = activation.astype(jnp.bfloat16)
    return (
        residual_mid,
        normed_one,
        norm_one_back,
        kept_attention,
        attended_rows,
        norm_two_back,
        normed_two,
        gelu_back,
        activation,
    )


def attend_grads(d_attended, kept_attention):
    scale_factor = 1.0 / math.sqrt(HEAD_DIM)
    head_query, head_key, head_value, log_total, key_ids = kept_attention
    grad_heads = lax.all_to_all(d_attended, "seq", split_axis=2, concat_axis=1, tiled=True)
    grad_query, grad_key, grad_value = attend_backward(
        to_heads_shape(head_query),
        to_heads_shape(head_key),
        to_heads_shape(head_value),
        to_heads_shape(grad_heads),
        log_total,
        key_ids,
        key_ids,
        scale_factor,
    )
    return (
        lax.all_to_all(
            grad_query.reshape(head_query.shape).astype(jnp.bfloat16),
            "seq",
            split_axis=1,
            concat_axis=2,
            tiled=True,
        ),
        lax.all_to_all(
            grad_key.reshape(head_key.shape).astype(jnp.bfloat16),
            "seq",
            split_axis=1,
            concat_axis=2,
            tiled=True,
        ),
        lax.all_to_all(
            grad_value.reshape(head_value.shape).astype(jnp.bfloat16),
            "seq",
            split_axis=1,
            concat_axis=2,
            tiled=True,
        ),
    )


def shards(
    inputs,
    time_embed,
    segment_ids,
    cotangent,
    first_gain,
    first_shift,
    mix_weight,
    mix_bias,
    out_weight,
    out_bias,
    second_gain,
    second_shift,
    up_weight,
    up_bias,
    down_weight,
    down_bias,
):
    params = (
        lax.all_gather(first_gain, ("batch", "seq"), axis=0, tiled=True),
        lax.all_gather(first_shift, ("batch", "seq"), axis=0, tiled=True),
        lax.all_gather(mix_weight, ("batch", "seq"), axis=0, tiled=True),
        lax.all_gather(mix_bias, ("batch", "seq"), axis=0, tiled=True),
        lax.all_gather(out_weight, ("batch", "seq"), axis=0, tiled=True),
        lax.all_gather(out_bias, ("batch", "seq"), axis=0, tiled=True),
        lax.all_gather(second_gain, ("batch", "seq"), axis=0, tiled=True),
        lax.all_gather(second_shift, ("batch", "seq"), axis=0, tiled=True),
        lax.all_gather(up_weight, ("batch", "seq"), axis=0, tiled=True),
        lax.all_gather(up_bias, ("batch", "seq"), axis=0, tiled=True),
        lax.all_gather(down_weight, ("batch", "seq"), axis=0, tiled=True),
        lax.all_gather(down_bias, ("batch", "seq"), axis=0, tiled=True),
    )
    layer_state = forward_state(params, inputs, time_embed, segment_ids)
    layer_out = (
        layer_state[0]
        + jnp.einsum("rtf,fd->rtd", layer_state[8], params[10], preferred_element_type=jnp.float32)
        + params[11].astype(jnp.float32)
    ).astype(jnp.bfloat16)
    fenced = lax.optimization_barrier(
        (
            first_gain,
            first_shift,
            mix_weight,
            mix_bias,
            out_weight,
            out_bias,
            second_gain,
            second_shift,
            up_weight,
            up_bias,
            down_weight,
            down_bias,
            inputs,
            time_embed,
            layer_out,
        )
    )
    params = (
        lax.all_gather(fenced[0], ("batch", "seq"), axis=0, tiled=True),
        lax.all_gather(fenced[1], ("batch", "seq"), axis=0, tiled=True),
        lax.all_gather(fenced[2], ("batch", "seq"), axis=0, tiled=True),
        lax.all_gather(fenced[3], ("batch", "seq"), axis=0, tiled=True),
        lax.all_gather(fenced[4], ("batch", "seq"), axis=0, tiled=True),
        lax.all_gather(fenced[5], ("batch", "seq"), axis=0, tiled=True),
        lax.all_gather(fenced[6], ("batch", "seq"), axis=0, tiled=True),
        lax.all_gather(fenced[7], ("batch", "seq"), axis=0, tiled=True),
        lax.all_gather(fenced[8], ("batch", "seq"), axis=0, tiled=True),
        lax.all_gather(fenced[9], ("batch", "seq"), axis=0, tiled=True),
        lax.all_gather(fenced[10], ("batch", "seq"), axis=0, tiled=True),
        lax.all_gather(fenced[11], ("batch", "seq"), axis=0, tiled=True),
    )
    layer_state = forward_state(params, fenced[12], fenced[13], segment_ids)
    (
        residual_mid,
        normed_one,
        norm_one_back,
        kept_attention,
        attended_rows,
        norm_two_back,
        normed_two,
        gelu_back,
        activation,
    ) = layer_state
    mix_full = params[2]
    out_full = params[4]
    up_full = params[8]
    down_full = params[10]
    grad_out = cotangent.astype(jnp.float32)
    down_bias_grad = jnp.sum(grad_out, axis=(0, 1))
    down_weight_grad = jnp.einsum(
        "rtf,rtd->fd", activation, cotangent, preferred_element_type=jnp.float32
    )
    d_activation = jnp.einsum(
        "rtd,fd->rtf", cotangent, down_full, preferred_element_type=jnp.float32
    )
    d_hidden = gelu_back(d_activation)[0].astype(jnp.bfloat16)
    up_bias_grad = jnp.sum(d_hidden.astype(jnp.float32), axis=(0, 1))
    up_weight_grad = jnp.einsum(
        "rtd,rtf->df", normed_two, d_hidden, preferred_element_type=jnp.float32
    )
    d_normed_two = jnp.einsum("rtf,df->rtd", d_hidden, up_full, preferred_element_type=jnp.float32)
    d_mid, second_gain_grad, second_shift_grad = norm_two_back(d_normed_two)
    d_mid = d_mid + grad_out
    d_branch = d_mid.astype(jnp.bfloat16)
    out_bias_grad = jnp.sum(d_branch.astype(jnp.float32), axis=(0, 1))
    out_weight_grad = jnp.einsum(
        "rtc,rtd->cd", attended_rows, d_branch, preferred_element_type=jnp.float32
    )
    d_attended = jnp.einsum(
        "rtd,cd->rtc", d_branch, out_full, preferred_element_type=jnp.float32
    ).astype(jnp.bfloat16)
    grad_query, grad_key, grad_value = attend_grads(d_attended, kept_attention)
    d_projected = jnp.concatenate([grad_query, grad_key, grad_value], axis=-1)
    mix_bias_grad = jnp.concatenate(
        [
            jnp.sum(grad_query.astype(jnp.float32), axis=(0, 1)),
            jnp.sum(grad_value.astype(jnp.float32), axis=(0, 1)),
        ]
    )
    mix_weight_grad = jnp.einsum(
        "rtd,rte->de", normed_one, d_projected, preferred_element_type=jnp.float32
    )
    d_normed_one = jnp.einsum(
        "rte,de->rtd", d_projected, mix_full, preferred_element_type=jnp.float32
    )
    d_input_norm, first_gain_grad, first_shift_grad = norm_one_back(d_normed_one)
    inputs_grad = d_input_norm + d_mid
    time_grad = lax.psum_scatter(
        jnp.sum(inputs_grad, axis=1), "seq", scatter_dimension=1, tiled=True
    )
    weight_grads = (
        lax.psum_scatter(first_gain_grad, ("batch", "seq"), scatter_dimension=0, tiled=True),
        lax.psum_scatter(first_shift_grad, ("batch", "seq"), scatter_dimension=0, tiled=True),
        lax.psum_scatter(mix_weight_grad, ("batch", "seq"), scatter_dimension=0, tiled=True),
        lax.psum_scatter(mix_bias_grad, ("batch", "seq"), scatter_dimension=0, tiled=True),
        lax.psum_scatter(out_weight_grad, ("batch", "seq"), scatter_dimension=0, tiled=True),
        lax.psum_scatter(out_bias_grad, ("batch", "seq"), scatter_dimension=0, tiled=True),
        lax.psum_scatter(second_gain_grad, ("batch", "seq"), scatter_dimension=0, tiled=True),
        lax.psum_scatter(second_shift_grad, ("batch", "seq"), scatter_dimension=0, tiled=True),
        lax.psum_scatter(up_weight_grad, ("batch", "seq"), scatter_dimension=0, tiled=True),
        lax.psum_scatter(up_bias_grad, ("batch", "seq"), scatter_dimension=0, tiled=True),
        lax.psum_scatter(down_weight_grad, ("batch", "seq"), scatter_dimension=0, tiled=True),
        lax.psum_scatter(down_bias_grad, ("batch", "seq"), scatter_dimension=0, tiled=True),
    )
    return (layer_out, inputs_grad, time_grad) + tuple(weight_grads)


def solution(mesh):
    return jax.shard_map(
        shards,
        mesh=mesh,
        in_specs=(
            P("batch", "seq", None),
            P("batch", None),
            P("batch", None),
            P("batch", "seq", None),
            P(("batch", "seq")),
            P(("batch", "seq")),
            P(("batch", "seq"), None),
            P(("batch", "seq")),
            P(("batch", "seq"), None),
            P(("batch", "seq")),
            P(("batch", "seq")),
            P(("batch", "seq")),
            P(("batch", "seq"), None),
            P(("batch", "seq")),
            P(("batch", "seq"), None),
            P(("batch", "seq")),
        ),
        out_specs=(
            P("batch", "seq", None),
            P("batch", "seq", None),
            P("batch", "seq"),
            P(("batch", "seq")),
            P(("batch", "seq")),
            P(("batch", "seq"), None),
            P(("batch", "seq")),
            P(("batch", "seq"), None),
            P(("batch", "seq")),
            P(("batch", "seq")),
            P(("batch", "seq")),
            P(("batch", "seq"), None),
            P(("batch", "seq")),
            P(("batch", "seq"), None),
            P(("batch", "seq")),
        ),
        check_vma=False,
    )
```

profile of v0, /device:TPU:0, one launch (start us, length us, event | category | flops | bytes accessed | tf_op | source)
XLA Modules:
  0.0 1135.3 jit_solution(13876450463464012679)
XLA Ops:
  16.7 42.7 %all-reduce.25 = (bf16[768]{0:T(1024)(128)(2,1)S(1)}, bf16[768]{0:T(1024)(128)(2,1)S(1)}, bf16[1536]{0:T(1024)(128)(2,1)S(1)}, bf16[768]{0:T(1024)(128)(2,1)}, b...) all-reduce(bf16[768]{0:T(1024)(128)(2,1)S(1)} %dynamic-update-slice, ...), channel_id=1, replica_groups=mesh['batch'=16,'seq'=2] {'batch','seq'}, use_global_device_ids=true, to_apply=%add.1 | all-reduce | flops 9216 | bytes 36864
  62.5 11.4 all-gather.9.cloned.1.call-done
  73.9 3.3 fusion.23
  80.9 4.2 all-to-all-start.2
  87.0 5.4 all-to-all-done.2
  92.4 3.5 all-to-all-start
  97.9 4.4 all-to-all-done
  102.3 3.5 all-to-all-start.1
  115.6 3.7 all-to-all-start.3
  119.4 5.7 all-to-all-done.3
  125.2 5.2 all-gather.11.cloned.1.call-done
  132.6 63.4 %all-gather.13.cloned.1.call-done = bf16[768,3072]{1,0:T(8,128)(2,1)} async-done(((bf16[24,3072]{1,0:T(8,128)(2,1)}), bf16[768,3072]{1,0:T(8,128)(2,1)}) %all-gather.13.cloned.1.call-update) | async-done | bytes 4718608 | tf_op jit(solution)/shard_map/all_gather | solution.py:256
  196.0 6.4 fusion.110
  202.4 58.9 %all-gather.15.cloned.1.call-done = bf16[3072,768]{1,0:T(8,128)(2,1)} async-done(((bf16[96,768]{1,0:T(8,128)(2,1)}), bf16[3072,768]{1,0:T(8,128)(2,1)}) %all-gather.15.cloned.1.call-update) | async-done | bytes 4718608 | tf_op jit(solution)/shard_map/all_gather | solution.py:258
  261.3 11.9 %fusion.89 = bf16[4,64,768]{2,1,0:T(8,128)(2,1)} fusion(f32[4,64,768]{2,1,0:T(8,128)S(1)} %get-tuple-element.220, bf16[3072,768]{1,0:T(8,128)(2,1)} %all-gather.15.cloned.1.call-done, f32[4,64,3072]{2,1,0:T(8,128)} %get-tuple-element.221, u8[64,3072]{1,0:T(8,128)(4,1)S(1)} %get-tuple-element.171, u8[64,3072]{1,0:T(8,128)(4,1)S(1)} %get-tuple-element.170, ...), kind=kOutput, calls=%fused_computation.120 | convolution fusion | flops 1263599616 | bytes 9440256 | tf_op jit(solution)/shard_map/rtf,fd->rtd/dot_general | solution.py:264
  277.0 40.9 %all-reduce.24 = (bf16[3072]{0:T(1024)(128)(2,1)}, bf16[768]{0:T(1024)(128)(2,1)S(1)}, bf16[768]{0:T(1024)(128)(2,1)S(1)}, bf16[1536]{0:T(1024)(128)(2,1)S(1)}, ...) all-reduce(bf16[3072]{0:T(1024)(128)(2,1)S(1)} %dynamic-update-slic, ...), channel_id=1, replica_groups=mesh['batch'=16,'seq'=2] {'batch','seq'}, use_global_device_ids=true, to_apply=%add.14 | all-reduce | flops 8448 | bytes 33792
  318.3 14.2 %all-gather.17.cloned.1.call-done = bf16[768,2304]{1,0:T(8,128)(2,1)} async-done(((bf16[24,2304]{1,0:T(8,128)(2,1)}), bf16[768,2304]{1,0:T(8,128)(2,1)}) %all-gather.17.cloned.1.call-update) | async-done | bytes 3538960 | tf_op jit(solution)/shard_map/all_gather | solution.py:289
  332.5 3.2 fusion.21
  339.6 4.2 all-to-all-start.6
  346.6 4.5 all-to-all-done.6
  351.1 3.5 all-to-all-start.4
  356.6 4.4 all-to-all-done.4
  361.0 3.5 all-to-all-start.5
  374.3 3.6 all-to-all-start.7
  379.8 4.0 all-to-all-done.7
  384.6 4.3 all-gather.19.cloned.1.call-done
  392.7 61.7 %all-gather.21.cloned.1.call-done = bf16[768,3072]{1,0:T(8,128)(2,1)} async-done(((bf16[24,3072]{1,0:T(8,128)(2,1)}), bf16[768,3072]{1,0:T(8,128)(2,1)}) %all-gather.21.cloned.1.call-update) | async-done | bytes 4718608 | tf_op jit(solution)/shard_map/all_gather | solution.py:295
  454.5 7.2 fusion.111
  461.7 58.2 %all-gather.23.cloned.1.call-done = bf16[3072,768]{1,0:T(8,128)(2,1)} async-done(((bf16[96,768]{1,0:T(8,128)(2,1)}), bf16[3072,768]{1,0:T(8,128)(2,1)}) %all-gather.23.cloned.1.call-update) | async-done | bytes 4718608 | tf_op jit(solution)/shard_map/all_gather | solution.py:297
  519.9 11.7 %convert_reduce_fusion = (f32[3072]{0:T(1024)}, bf16[4,64,3072]{2,1,0:T(8,128)(2,1)S(1)}) fusion(u8[64,3072]{1,0:T(8,128)(4,1)} %get-tuple-element.169, u8[64,3072]{1,0:T(8,128)(4,1)} %get-tuple-element.168, f32[4,64,3072]{2,1,0:T(8,128)} %get-tuple-element.226, bf16[4,64,768]{2,1,0:T(8,128)(2,1)S(1)} %copy-done.7, ...), kind=kOutput, calls=%fused_computation.38 | convolution fusion | flops 1270084608 | bytes 10235904 | tf_op jit(solution)/shard_map/rtd,fd->rtf/dot_general | solution.py:321
  540.4 10.6 all_to_all.195
  553.3 2.8 copy.123
  563.1 4.2 all-to-all-start.9
  567.3 2.4 fusion.87
  573.9 3.5 all-to-all-start.10
  580.0 3.2 all-to-all-done.10
  583.2 3.5 all-to-all-start.11
  588.8 3.8 all-to-all-done.11
  594.3 4.2 fusion.162
  603.2 3.0 convolution_bitcast_fusion.3
  606.3 4.2 convolution_bitcast_fusion.2
  611.7 6.7 convolution_bitcast_fusion.1
  619.4 11.9 %convolution_bitcast_fusion = f32[3072,768]{1,0:T(8,128)} fusion(bf16[4,64,768]{2,1,0:T(8,128)(2,1)S(1)} %copy-done.8, f32[4,64,3072]{2,1,0:T(8,128)} %get-tuple-element.226, u8[64,3072]{1,0:T(8,128)(4,1)S(1)} %copy-done.67, u8[64,3072]{1,0:T(8,128)(4,1)S(1)} %copy-done.66), kind=kOutput, calls=%fused_computation | convolution fusion | flops 1263009792 | bytes 13369344 | tf_op jit(solution)/shard_map/rtf,rtd->fd/dot_general | solution.py:318
  632.1 40.5 %all-reduce.23 = (f32[768]{0:T(1024)S(1)}, f32[768]{0:T(1024)S(1)}, f32[1536]{0:T(1024)S(1)}, f32[768]{0:T(1024)S(1)}, f32[768]{0:T(1024)S(1)}, /*index=5*/f32[7...) all-reduce(f32[768]{0:T(1024)S(1)} %copy-done.39, ...), channel_id=3, replica_groups=mesh['batch'=16,'seq'=2] {'batch','seq'}, use_global_device_ids=true, to_apply=%region_20.21.clone | all-reduce | flops 9216 | bytes 73728
  678.8 41.9 %reduce-scatter.10.cloned.1.call-done = f32[24,768]{1,0:T(8,128)} async-done(((f32[768,768]{1,0:T(8,128)}), f32[24,768]{1,0:T(8,128)}) %reduce-scatter.10.cloned.1.call-update) | async-done | bytes 73744 | tf_op jit(solution)/shard_map/reduce_scatter | solution.py:364
  720.7 124.5 %reduce-scatter.8.cloned.1.call-done = f32[24,2304]{1,0:T(8,128)} async-done(((f32[768,2304]{1,0:T(8,128)}), f32[24,2304]{1,0:T(8,128)}) %reduce-scatter.8.cloned.1.call-update) | async-done | bytes 221200 | tf_op jit(solution)/shard_map/reduce_scatter | solution.py:362
  845.2 142.1 %reduce-scatter.12.cloned.1.call-done = f32[24,3072]{1,0:T(8,128)} async-done(((f32[768,3072]{1,0:T(8,128)}), f32[24,3072]{1,0:T(8,128)}) %reduce-scatter.12.cloned.1.call-update) | async-done | bytes 294928 | tf_op jit(solution)/shard_map/reduce_scatter | solution.py:368
  987.4 141.0 %reduce-scatter.14.cloned.1.call-done = f32[96,768]{1,0:T(8,128)} async-done(((f32[3072,768]{1,0:T(8,128)}), f32[96,768]{1,0:T(8,128)}) %reduce-scatter.14.cloned.1.call-update) | async-done | bytes 294928 | tf_op jit(solution)/shard_map/reduce_scatter | solution.py:370
  (323 shorter events, 103.4 us)
Async XLA Ops:
  7.2 66.7 %all-gather.9.cloned.1.call-start = ((), (), s32[]{:S(2)}) async-start(), calls=%async_computation.17 | async-start | bytes 3649536 | tf_op jit(solution)/shard_map/all_gather | solution.py:250
  7.9 122.6 %all-gather.11.cloned.1.call-start = ((), (), s32[]{:S(2)}) async-start(), calls=%async_computation.18 | async-start | bytes 1216512 | tf_op jit(solution)/shard_map/all_gather | solution.py:252
  8.7 187.4 %all-gather.13.cloned.1.call-start = ((), (), s32[]{:S(2)}) async-start(), calls=%async_computation.19 | async-start | bytes 4866048 | tf_op jit(solution)/shard_map/all_gather | solution.py:256
  9.4 251.9 %all-gather.15.cloned.1.call-start = ((), (), s32[]{:S(2)}) async-start(), calls=%async_computation.20 | async-start | bytes 4866048 | tf_op jit(solution)/shard_map/all_gather | solution.py:258
  80.9 11.5 %all-to-all-start.2 = ((bf16[2,2,49152]{2,1,0:T(2,128)(2,1)}), bf16[2,2,49152]{2,1,0:T(2,128)(2,1)}, u32[]{:S(2)}, u32[]{:S(2)}) async-start(bf16[2,2,49152]{2,1,0:T(2,128)(2,1)} %reshape.278), calls=%async_computation.2 | async-start | bytes 786432 | tf_op jit(solution)/shard_map/all_to_all | solution.py:151
  85.6 20.2 %copy-start.44 = (s32[4,128]{1,0:T(4,128)S(1)}, s32[4,128]{1,0:T(4,128)}, u32[]{:S(2)}) copy-start(s32[4,128]{1,0:T(4,128)} %param.18) | copy-start | bytes 6148
  92.4 9.9 all-to-all-start
  102.3 9.3 all-to-all-start.1
  106.0 7.5 copy-start.12
  114.3 16.2 %copy-start = (bf16[4,64,768]{2,1,0:T(8,128)(2,1)S(1)}, bf16[4,64,768]{2,1,0:T(8,128)(2,1)}, u32[]{:S(2)}) copy-start(bf16[4,64,768]{2,1,0:T(8,128)(2,1)} %param.16) | copy-start | bytes 1179652
  115.6 9.5 all-to-all-start.3
  119.3 213.2 %all-gather.17.cloned.1.call-start = ((), (), s32[]{:S(2)}) async-start(), calls=%async_computation.21 | async-start | bytes 3649536 | tf_op jit(solution)/shard_map/all_gather | solution.py:289
  261.3 14.0 %copy-start.58 = (bf16[96]{0:T(256)(128)(2,1)S(1)}, bf16[96]{0:T(256)(128)(2,1)}, u32[]{:S(2)}) copy-start(bf16[96]{0:T(256)(128)(2,1)} %param.29) | copy-start | bytes 580
  261.3 14.3 %copy-start.59 = (bf16[24]{0:T(256)(128)(2,1)S(1)}, bf16[24]{0:T(256)(128)(2,1)}, u32[]{:S(2)}) copy-start(bf16[24]{0:T(256)(128)(2,1)} %param.21) | copy-start | bytes 148
  261.3 14.5 %copy-start.60 = (bf16[24]{0:T(256)(128)(2,1)S(1)}, bf16[24]{0:T(256)(128)(2,1)}, u32[]{:S(2)}) copy-start(bf16[24]{0:T(256)(128)(2,1)} %param.20) | copy-start | bytes 148
  261.3 14.8 %copy-start.61 = (bf16[48]{0:T(256)(128)(2,1)S(1)}, bf16[48]{0:T(256)(128)(2,1)}, u32[]{:S(2)}) copy-start(bf16[48]{0:T(256)(128)(2,1)} %param.23) | copy-start | bytes 292
  261.3 15.0 %copy-start.62 = (bf16[24]{0:T(256)(128)(2,1)S(1)}, bf16[24]{0:T(256)(128)(2,1)}, u32[]{:S(2)}) copy-start(bf16[24]{0:T(256)(128)(2,1)} %param.25) | copy-start | bytes 148
  261.3 15.2 %copy-start.63 = (bf16[24]{0:T(256)(128)(2,1)S(1)}, bf16[24]{0:T(256)(128)(2,1)}, u32[]{:S(2)}) copy-start(bf16[24]{0:T(256)(128)(2,1)} %param.27) | copy-start | bytes 148
  261.3 15.5 %copy-start.64 = (bf16[24]{0:T(256)(128)(2,1)S(1)}, bf16[24]{0:T(256)(128)(2,1)}, u32[]{:S(2)}) copy-start(bf16[24]{0:T(256)(128)(2,1)} %param.26) | copy-start | bytes 148
  261.3 56.5 %copy-start.26 = (bf16[4,768]{1,0:T(4,128)(2,1)S(1)}, bf16[4,768]{1,0:T(4,128)(2,1)}, u32[]{:S(2)}) copy-start(bf16[4,768]{1,0:T(4,128)(2,1)} %param.17) | copy-start | bytes 18436
  273.2 115.7 %all-gather.19.cloned.1.call-start = ((), (), s32[]{:S(2)}) async-start(), calls=%async_computation.22 | async-start | bytes 1216512 | tf_op jit(solution)/shard_map/all_gather | solution.py:291
  273.8 180.7 %all-gather.21.cloned.1.call-start = ((), (), s32[]{:S(2)}) async-start(), calls=%async_computation.23 | async-start | bytes 4866048 | tf_op jit(solution)/shard_map/all_gather | solution.py:295
  274.5 245.4 %all-gather.23.cloned.1.call-start = ((), (), s32[]{:S(2)}) async-start(), calls=%async_computation.24 | async-start | bytes 4866048 | tf_op jit(solution)/shard_map/all_gather | solution.py:297
  317.8 17.8 %copy-start.17 = (f32[768]{0:T(1024)}, f32[768]{0:T(1024)S(1)}, u32[]{:S(2)}) copy-start(f32[768]{0:T(1024)S(1)} %convert_element_type.204) | copy-start | bytes 9220
  318.0 17.6 %copy-start.19 = (f32[4,64]{1,0:T(4,128)}, f32[4,64]{1,0:T(4,128)S(1)}, u32[]{:S(2)}) copy-start(f32[4,64]{1,0:T(4,128)S(1)} %broadcast_multiply_fusion.1) | copy-start | bytes 3076
  318.3 17.4 %copy-start.30 = (f32[4,64]{1,0:T(4,128)}, f32[4,64]{1,0:T(4,128)S(1)}, u32[]{:S(2)}) copy-start(f32[4,64]{1,0:T(4,128)S(1)} %multiply_reduce_fusion.6) | copy-start | bytes 3076
  318.3 17.4 %copy-start.23 = (f32[4,64]{1,0:T(4,128)}, f32[4,64]{1,0:T(4,128)S(1)}, u32[]{:S(2)}) copy-start(f32[4,64]{1,0:T(4,128)S(1)} %fusion.127) | copy-start | bytes 3076
  339.6 11.5 %all-to-all-start.6 = ((bf16[2,2,49152]{2,1,0:T(2,128)(2,1)}), bf16[2,2,49152]{2,1,0:T(2,128)(2,1)}, u32[]{:S(2)}, u32[]{:S(2)}) async-start(bf16[2,2,49152]{2,1,0:T(2,128)(2,1)} %reshape.284), calls=%async_computation.6 | async-start | bytes 786432 | tf_op jit(solution)/shard_map/all_to_all | solution.py:151
  351.1 9.9 all-to-all-start.4
  361.0 9.3 all-to-all-start.5
  372.6 6.5 copy-start.54
  373.0 17.9 %copy-start.14 = (f32[4,6,128]{2,1,0:T(8,128)}, f32[4,6,128]{2,1,0:T(8,128)S(1)}, u32[]{:S(2)}) copy-start(f32[4,6,128]{2,1,0:T(8,128)S(1)} %log_add_fusion) | copy-start | bytes 36868
  374.3 9.5 all-to-all-start.7
  390.9 140.7 %copy-start.5 = (f32[4,64,768]{2,1,0:T(8,128)}, f32[4,64,768]{2,1,0:T(8,128)S(1)}, u32[]{:S(2)}) copy-start(f32[4,64,768]{2,1,0:T(8,128)S(1)} %get-tuple-element.225) | copy-start | bytes 2359300
  392.7 127.2 %copy-start.7 = (bf16[4,64,768]{2,1,0:T(8,128)(2,1)S(1)}, bf16[4,64,768]{2,1,0:T(8,128)(2,1)}, u32[]{:S(2)}) copy-start(bf16[4,64,768]{2,1,0:T(8,128)(2,1)} %param.19) | copy-start | bytes 1179652
  519.9 11.7 %copy-start.28 = (f32[4,64]{1,0:T(4,128)S(1)}, f32[4,64]{1,0:T(4,128)}, u32[]{:S(2)}) copy-start(f32[4,64]{1,0:T(4,128)} %copy-done.27) | copy-start | bytes 3076
  519.9 11.7 %copy-start.36 = (f32[768]{0:T(1024)S(1)}, f32[768]{0:T(1024)}, u32[]{:S(2)}) copy-start(f32[768]{0:T(1024)} %convert_element_type.214) | copy-start | bytes 9220
  519.9 11.7 %copy-start.42 = (f32[4,64]{1,0:T(4,128)S(1)}, f32[4,64]{1,0:T(4,128)}, u32[]{:S(2)}) copy-start(f32[4,64]{1,0:T(4,128)} %fusion.128) | copy-start | bytes 3076
  519.9 11.7 %copy-start.57 = (bf16[768,3072]{1,0:T(8,128)(2,1)S(1)}, bf16[768,3072]{1,0:T(8,128)(2,1)}, u32[]{:S(2)}) copy-start(bf16[768,3072]{1,0:T(8,128)(2,1)} %all-gather.21.cloned.1.call-done) | copy-start | bytes 14155780
  563.1 10.7 all-to-all-start.9
  573.9 9.3 all-to-all-start.10
  583.2 9.3 all-to-all-start.11
  586.7 90.5 %reduce-scatter.16.cloned.1.call-start = ((), (), s32[]{:S(2)}) async-start(), calls=%async_computation.29 | async-start | bytes 589824
  587.8 6.5 copy-start.20
  603.2 117.6 %reduce-scatter.10.cloned.1.call-start = ((), (), s32[]{:S(2)}) async-start(), calls=%async_computation.26 | async-start | bytes 2433024 | tf_op jit(solution)/shard_map/reduce_scatter | solution.py:364
  606.2 239.0 %reduce-scatter.8.cloned.1.call-start = ((), (), s32[]{:S(2)}) async-start(), calls=%async_computation.25 | async-start | bytes 7299072 | tf_op jit(solution)/shard_map/reduce_scatter | solution.py:362
  610.6 376.8 %reduce-scatter.12.cloned.1.call-start = ((), (), s32[]{:S(2)}) async-start(), calls=%async_computation.27 | async-start | bytes 9732096 | tf_op jit(solution)/shard_map/reduce_scatter | solution.py:368
  618.4 510.0 %reduce-scatter.14.cloned.1.call-start = ((), (), s32[]{:S(2)}) async-start(), calls=%async_computation.28 | async-start | bytes 9732096 | tf_op jit(solution)/shard_map/reduce_scatter | solution.py:370
  (44 other events, 115.7 us)
Sparse Core Ops, SparseCore 0:
  10.9 62.8 all-gather.8
  76.8 53.6 all-gather.10
  133.4 62.5 all-gather.12
  198.8 62.4 all-gather.14
  273.3 59.1 all-gather.16
  335.3 53.6 all-gather.18
  391.8 62.6 all-gather.20
  457.4 62.4 all-gather.22
  603.3 11.8 reduce-scatter.15
  621.7 98.9 reduce-scatter.9
  727.0 118.2 reduce-scatter.7
  852.6 134.7 reduce-scatter.11
  993.8 134.4 reduce-scatter.13
where the time goes:
time: 1150 us; the launch traced here: 1140 us
  waiting for transfers between devices  772 us (67%)
  blocking collectives  135 us (12%)
  matrix products  88.2 us (8%)
  local copies, waits for them, and re-layouts  69.1 us (6%)
  starting transfers between devices  41.4 us (4%)
  between operations  15.6 us (1%)
  other arithmetic  14.8 us (1%)
    reduce_scatter x1, waiting for transfers between devices, shards(): lax.psum_scatter(up_weight_grad, ('batch', 'seq'), scatter_dimension=0, t...  142 us
    reduce_scatter x1, waiting for transfers between devices, shards(): lax.psum_scatter(down_weight_grad, ('batch', 'seq'), scatter_dimension=0,...  141 us
    reduce_scatter x1, waiting for transfers between devices, shards(): lax.psum_scatter(mix_weight_grad, ('batch', 'seq'), scatter_dimension=0,...  125 us
    unnamed x3, blocking collectives  124 us
    all_gather x1, waiting for transfers between devices, shards(): lax.all_gather(up_weight, ('batch', 'seq'), axis=0, tiled=True)  63.4 us
    all_gather x1, waiting for transfers between devices, shards(): lax.all_gather(fenced[8], ('batch', 'seq'), axis=0, tiled=True)  61.7 us
    all_gather x1, waiting for transfers between devices, shards(): lax.all_gather(down_weight, ('batch', 'seq'), axis=0, tiled=True)  58.9 us
    all_gather x1, waiting for transfers between devices, shards(): lax.all_gather(fenced[10], ('batch', 'seq'), axis=0, tiled=True)  58.2 us
  transfers between devices with their start and end apart: 24, of which 23 were waited for; matrix products, arithmetic and copies ran while one was open for 10% of the time, Pallas kernels for 0%

commit v1 on v0

v1 whole, which is shorter than its diff:
```python
from functools import partial
import math

import jax
import jax.numpy as jnp
from jax import lax
from jax.experimental import pallas as pl
from jax.experimental.pallas import tpu as pltpu
from jax.sharding import PartitionSpec as P

HEAD_DIM = 64
EPSILON = 1e-05
NEG_FILL = -1e30
BATCH, SEQ = "batch", "seq"
AXES = (BATCH, SEQ)
F32, BF16 = jnp.float32, jnp.bfloat16


def norm_back(d_out, normal, inv, gain):
    g = d_out * gain
    return inv * (g - jnp.mean(g, -1, keepdims=True) - normal * jnp.mean(g * normal, -1, keepdims=True))


def normal_part(hidden):
    centred = hidden - jnp.mean(hidden, -1, keepdims=True)
    inv = lax.rsqrt(jnp.mean(centred * centred, -1, keepdims=True) + EPSILON)
    return centred * inv, inv


def contract(a, b, over_a, over_b, batch=((), ())):
    return lax.dot_general(a, b, ((over_a, over_b), batch), preferred_element_type=F32)


def layer(inputs, time, ids, cot, params):
    (gain1, shift1, mix, mbias, out, obias, gain2, shift2, up, ubias, down, dbias) = params
    gain1, shift1, mbias, obias, gain2, shift2, ubias, dbias = (
        v.astype(F32) for v in (gain1, shift1, mbias, obias, gain2, shift2, ubias, dbias))
    rows, length, width = inputs.shape
    heads = width // HEAD_DIM
    scale = 1.0 / math.sqrt(HEAD_DIM)
    flat = lambda t: t.reshape(rows * length, -1)
    by_head = lambda t: t.reshape(rows, length, heads, HEAD_DIM).transpose(0, 2, 1, 3).reshape(rows * heads, length, HEAD_DIM)
    unhead = lambda t: flat(t.reshape(rows, heads, length, HEAD_DIM).transpose(0, 2, 1, 3))
    each = ((0,), (0,))
    cot = flat(cot)
    res_in = flat(inputs.astype(F32) + time.astype(F32)[:, None, :])
    norm1, inv1 = normal_part(res_in)
    normed1 = (norm1 * gain1 + shift1).astype(BF16)
    proj = contract(normed1, mix, (1,), (0,))
    q = by_head((proj[:, :width] + mbias[:width]).astype(BF16))
    k = by_head(proj[:, width:2 * width].astype(BF16))
    v = by_head((proj[:, 2 * width:] + mbias[width:]).astype(BF16))
    scores = contract(q, k, (2,), (2,), each) * scale
    same = jnp.repeat(ids[:, :, None] == ids[:, None, :], heads, axis=0)
    masked = jnp.where(same, scores, NEG_FILL)
    top = jnp.max(masked, -1, keepdims=True)
    log_total = top + jnp.log(jnp.sum(jnp.exp(masked - top), -1, keepdims=True))
    probs = jnp.exp(masked - log_total)
    probs16 = probs.astype(BF16)
    att = unhead(contract(probs16, v, (2,), (1,), each).astype(BF16))
    res_mid = res_in + (contract(att, out, (1,), (0,)) + obias)
    norm2, inv2 = normal_part(res_mid)
    normed2 = (norm2 * gain2 + shift2).astype(BF16)
    hid = contract(normed2, up, (1,), (0,)) + ubias
    cdf = 0.5 * (1.0 + lax.erf(hid * math.sqrt(0.5)))
    act = (hid * cdf).astype(BF16)
    layer_out = (res_mid + contract(act, down, (1,), (0,)) + dbias).astype(BF16)

    cot32 = cot.astype(F32)
    slope = cdf + hid * jnp.exp(-0.5 * hid * hid) * (1.0 / math.sqrt(2 * math.pi))
    d_hid = (contract(cot, down, (1,), (1,)) * slope).astype(BF16)
    d_n2 = contract(d_hid, up, (1,), (1,))
    d_mid = cot32 + norm_back(d_n2, norm2, inv2, gain2)
    d_br = d_mid.astype(BF16)
    d_att = by_head(contract(d_br, out, (1,), (1,)).astype(BF16))
    d_pr = contract(d_att, v, (2,), (2,), each)
    d_sc = (probs * (d_pr - jnp.sum(probs * d_pr, -1, keepdims=True))).astype(BF16)
    d_q = unhead((contract(d_sc, k, (2,), (1,), each) * scale).astype(BF16))
    d_k = unhead((contract(d_sc, q, (1,), (1,), each) * scale).astype(BF16))
    d_v = unhead(contract(probs16, d_att, (1,), (1,), each).astype(BF16))
    d_proj = jnp.concatenate([d_q, d_k, d_v], -1)
    d_n1 = contract(d_proj, mix, (1,), (1,))
    x_grad = d_mid + norm_back(d_n1, norm1, inv1, gain1)

    def col(t):
        return jnp.sum(t.astype(F32), axis=0)

    weigh = lambda a, b: contract(a, b, (0,), (0,))
    grads = (col(d_n1 * norm1), col(d_n1), weigh(normed1, d_proj), jnp.concatenate([col(d_q), col(d_v)]),
             weigh(att, d_br), col(d_br), col(d_n2 * norm2), col(d_n2), weigh(normed2, d_hid), col(d_hid),
             weigh(act, cot), col(cot32))
    return layer_out.reshape(inputs.shape), x_grad.reshape(inputs.shape), grads


def gather_all(shard):
    return lax.all_gather(shard, AXES, axis=0, tiled=True)


def scatter_sum(grad):
    return lax.psum_scatter(grad, AXES, scatter_dimension=0, tiled=True)


def rows_whole(tensor):
    return lax.all_to_all(tensor, SEQ, split_axis=0, concat_axis=1, tiled=True)


def rows_split(tensor):
    return lax.all_to_all(tensor, SEQ, split_axis=1, concat_axis=0, tiled=True)


def any_mesh(inputs, time_embed, segment_ids, cotangent, *shards):
    y, count = lax.axis_index(SEQ), inputs.shape[0] // lax.axis_size(SEQ)
    mine = [lax.dynamic_slice_in_dim(t, y * count, count, 0) for t in (time_embed, segment_ids)]
    layer_out, x_grad, grads = layer(
        rows_whole(inputs), mine[0], mine[1], rows_whole(cotangent), [gather_all(w) for w in shards])
    time_grad = lax.all_to_all(jnp.sum(x_grad, 1), SEQ, split_axis=1, concat_axis=0, tiled=True)
    return (rows_split(layer_out), rows_split(x_grad), time_grad) + tuple(scatter_sum(g) for g in grads)


MESH = pl.DeviceIdType.MESH
Z_CHIPS = 4


class Place:
    def __init__(self):
        b, self.y = lax.axis_index(BATCH), lax.axis_index(SEQ)
        self.z, self.x, self.c = b // 4, (b // 2) % 2, b % 2
        z, x, c, y = self.z, self.x, self.c, self.y
        self.x2, self.y2 = x + (1 - 2 * x) * (1 - c), y + (1 - 2 * y) * c
        self.x3, self.y3 = x + (1 - 2 * x) * c, y + (1 - 2 * y) * (1 - c)
        self.near = self.at(z, self.x2, c, self.y2)
        self.far = self.at(z, self.x3, c, self.y3)
        self.twin = self.at(z, x, 1 - c, y)
        self.x_peer = self.at(z, 1 - x, c, y)
        self.y_peer = self.at(z, x, c, 1 - y)
        self.z_slots = [lax.rem(z + d, Z_CHIPS) for d in (1, 2, 3)]
        self.z_from = [lax.rem(z + Z_CHIPS - d, Z_CHIPS) for d in (1, 2, 3)]
        self.z_peers = [self.at(q, x, c, y) for q in self.z_slots]

    @staticmethod
    def at(z, x, c, y):
        return ((z * 2 + x) * 2 + c, y)

    def greet(self):
        barrier = pltpu.get_barrier_semaphore()
        partners = self.z_peers + [self.near, self.far, self.twin]
        for partner in partners:
            pl.semaphore_signal(barrier, inc=1, device_id=partner, device_id_type=MESH)
        pl.semaphore_wait(barrier, len(partners))


class Wires:
    def __init__(self, send_sem, recv_sem, place):
        self.send_sem, self.recv_sem, self.place, self.sent = send_sem, recv_sem, place, []

    def start(self, src, dst, slot, device):
        copy = pltpu.make_async_remote_copy(
            src_ref=src, dst_ref=dst, send_sem=self.send_sem.at[slot], recv_sem=self.recv_sem.at[slot],
            device_id=device, device_id_type=MESH,
        )
        copy.start()
        self.sent.append(copy)

    def arrived(self, dst, slot):
        pltpu.make_async_remote_copy(
            src_ref=dst, dst_ref=dst, send_sem=self.send_sem.at[slot], recv_sem=self.recv_sem.at[slot],
            device_id=self.place.twin, device_id_type=MESH,
        ).wait_recv()

    def finish(self):
        for copy in self.sent:
            copy.wait_send()


class Gather:
    SLOTS = 10

    def __init__(self, wires, place, own, buf, at, wide, base):
        self.w, self.p, self.own, self.buf, self.cols, self.base = wires, place, own, buf, pl.ds(at, wide), base

    def mine(self):
        p = self.p
        return self.buf.at[p.z, p.x, p.c, p.y, :, self.cols]

    def block(self, x, y, c):
        return self.buf.at[:, x, c, y, :, self.cols]

    def begin(self):
        for j, peer in enumerate(self.p.z_peers):
            self.w.start(self.own.at[:, self.cols], self.mine(), self.base + j, peer)

    def after_z(self):
        p, w, base = self.p, self.w, self.base
        for j in range(3):
            w.arrived(self.mine(), base + j)
        b = self.block(p.x, p.y, p.c)
        w.start(b, b, base + 3, p.near)
        w.start(b, b, base + 4, p.far)
        w.start(b, b, base + 6, p.twin)

    def after_near(self):
        p, w, base = self.p, self.w, self.base
        b = self.block(p.x2, p.y2, p.c)
        w.arrived(b, base + 3)
        w.start(b, b, base + 5, p.far)
        w.start(b, b, base + 7, p.twin)

    def after_far(self):
        p, w, base = self.p, self.w, self.base
        b = self.block(p.x3, p.y3, p.c)
        w.arrived(b, base + 4)
        w.start(b, b, base + 8, p.twin)
        b = self.block(1 - p.x, 1 - p.y, p.c)
        w.arrived(b, base + 5)
        w.start(b, b, base + 9, p.twin)

    def complete(self):
        p = self.p
        for j in range(6, 10):
            self.w.arrived(self.block(p.x, p.y, 1 - p.c), self.base + j)


def butterfly(wires, place, value, send, recv, base):
    peers = [place.twin, place.y_peer, place.x_peer]
    peers.append(place.at(place.z + 1 - 2 * (place.z % 2), place.x, place.c, place.y))
    peers.append(place.at(lax.rem(place.z + 2, Z_CHIPS), place.x, place.c, place.y))
    for step, peer in enumerate(peers):
        send[step] = value.astype(send.dtype)
        wires.start(send.at[step], recv.at[step], base + step, peer)
        wires.arrived(recv.at[step], base + step)
        value = value + recv[step].astype(F32)
    return value


def gather_kernel(chunks, w1, w2, w3, small, xin, cot, b1, b2, b3, total, xfull, cfull,
                  sm_send, sm_recv, send_sem, recv_sem, local_sem):
    p = Place()
    p.greet()
    wires = Wires(send_sem, recv_sem, p)
    own, bufs = (w1, w2, w3), (b1, b2, b3)
    locs = []
    for w in range(3):
        locs.append(pltpu.make_async_copy(own[w], bufs[w].at[p.z, p.x, p.c, p.y], local_sem.at[w]))
    for i, (src, dst) in enumerate(((xin, xfull), (cot, cfull))):
        locs.append(pltpu.make_async_copy(src.at[pl.ds(2 * p.y, 2)], dst.at[:, p.y], local_sem.at[3 + i]))
    for copy in locs:
        copy.start()
    base = len(chunks) * Gather.SLOTS
    for i, (src, dst) in enumerate(((xin, xfull), (cot, cfull))):
        wires.start(src.at[pl.ds(2 - 2 * p.y, 2)], dst.at[:, p.y], base + i, p.y_peer)
    gathers = [Gather(wires, p, own[w], bufs[w], at, wide, Gather.SLOTS * k) for k, (w, at, wide) in enumerate(chunks)]
    gathers[0].begin()
    gathers[1].begin()
    total[...] = butterfly(wires, p, small[...].astype(F32), sm_send, sm_recv, base + 2)
    for copy in locs:
        copy.wait()
    count = len(gathers)
    for k in range(count + 2):
        if k < count:
            gathers[k].after_z()
        if k + 2 < count:
            gathers[k + 2].begin()
        if 0 <= k - 1 < count:
            gathers[k - 1].after_near()
        if 0 <= k - 2 < count:
            gathers[k - 2].after_far()
            gathers[k - 2].complete()
    for i, dst in enumerate((xfull, cfull)):
        wires.arrived(dst.at[:, p.y], base + i)
    wires.finish()


class Scatter:
    SLOTS = 6

    def __init__(self, wires, place, grads, out, bufs, at, wide, base):
        self.w, self.p, self.grads, self.out, self.base = wires, place, grads, out, base
        self.cols = pl.ds(at, wide)
        self.s1, self.r1, self.s2, self.r2, self.sz, self.rz = bufs

    def part(self, ref, *index):
        return ref.at[index + (slice(None), slice(None), self.cols)]

    def value(self, ref, *index):
        return ref[index + (slice(None), slice(None), self.cols)].astype(F32)

    def begin(self):
        p = self.p
        for j, (x, y) in enumerate(((p.x3, p.y3), (1 - p.x, 1 - p.y))):
            self.s1[j, :, :, self.cols] = self.value(self.grads, x, y).astype(BF16)
            self.w.start(self.part(self.s1, j), self.part(self.r1, j), self.base + j, p.far)

    def after_far(self):
        p = self.p
        self.w.arrived(self.part(self.r1, 1), self.base + 1)
        self.s2[:, :, self.cols] = (self.value(self.grads, p.x2, p.y2) + self.value(self.r1, 1)).astype(BF16)
        self.w.start(self.part(self.s2), self.part(self.r2), self.base + 2, p.near)
        self.w.arrived(self.part(self.r1, 0), self.base)

    def after_near(self):
        p = self.p
        self.w.arrived(self.part(self.r2), self.base + 2)
        for q in range(Z_CHIPS):
            total = (self.grads[p.x, p.y, q, :, self.cols] + self.r1[0, q, :, self.cols].astype(F32)
                     + self.r2[q, :, self.cols].astype(F32))
            self.sz[q, :, self.cols] = total.astype(BF16)

            @pl.when(q == p.z)
            def _():
                self.out[:, self.cols] = total
        for j, (q, peer) in enumerate(zip(p.z_slots, p.z_peers)):
            self.w.start(self.sz.at[q, :, self.cols], self.rz.at[j, :, self.cols], self.base + 3 + j, peer)

    def after_z(self):
        total = self.out[:, self.cols]
        for j in range(3):
            self.w.arrived(self.rz.at[j, :, self.cols], self.base + 3 + j)
            total = total + self.rz[j, :, self.cols].astype(F32)
        self.out[:, self.cols] = total


def scatter_kernel(chunks, g1, g2, g3, small, lout, igrad, tgrad, o1, o2, o3, total, lo_out, ig_out, tg_out, *scratch):
    bufs = [scratch[i * 6:(i + 1) * 6] for i in range(3)]
    sm_send, sm_recv, send_sem, recv_sem, local_sem = scratch[18:]
    p = Place()
    p.greet()
    wires = Wires(send_sem, recv_sem, p)
    grads, outs = (g1, g2, g3), (o1, o2, o3)
    base = len(chunks) * Scatter.SLOTS
    locs = []
    for i, (src, dst) in enumerate(((lout, lo_out), (igrad, ig_out))):
        locs.append(pltpu.make_async_copy(src.at[:, p.y], dst.at[pl.ds(2 * p.y, 2)], local_sem.at[i]))
        wires.start(src.at[:, 1 - p.y], dst.at[pl.ds(2 * p.y, 2)], base + i, p.y_peer)
    locs.append(pltpu.make_async_copy(tgrad.at[p.y], tg_out.at[p.y], local_sem.at[2]))
    wires.start(tgrad.at[1 - p.y], tg_out.at[p.y], base + 2, p.y_peer)
    for copy in locs:
        copy.start()
    scatters = [Scatter(wires, p, grads[w], outs[w], bufs[w], at, wide, Scatter.SLOTS * k)
                for k, (w, at, wide) in enumerate(chunks)]
    count = len(scatters)
    scatters[0].begin()
    scatters[1].begin()
    total[...] = butterfly(wires, p, small[...], sm_send, sm_recv, base + 3)
    for k in range(count + 2):
        if k < count:
            scatters[k].after_far()
        if k + 2 < count:
            scatters[k + 2].begin()
        if 0 <= k - 1 < count:
            scatters[k - 1].after_near()
        if 0 <= k - 2 < count:
            scatters[k - 2].after_z()
    for i, dst in enumerate((lo_out, ig_out)):
        wires.arrived(dst.at[pl.ds(2 * p.y, 2)], base + i)
    wires.arrived(tg_out.at[p.y], base + 2)
    for copy in locs:
        copy.wait()
    wires.finish()


def chunked(widths):
    chunks = []
    for w, pieces in enumerate(widths):
        at = 0
        for wide in pieces:
            chunks.append((w, at, wide))
            at += wide
    return chunks


ANY, VMEM = pl.BlockSpec(memory_space=pl.ANY), pl.BlockSpec(memory_space=pltpu.VMEM)
SMALL = (16, 768)


def run_gather(w1, w2, w3, small, xin, cot):
    chunks = chunked(((384,) * 4, (384,) * 4, (256,) * 3))
    slots = len(chunks) * Gather.SLOTS + 7
    shapes = [jax.ShapeDtypeStruct((4, 2, 2, 2) + w.shape, BF16) for w in (w1, w2, w3)]
    half = jax.ShapeDtypeStruct((2, 2) + xin.shape[1:], BF16)
    return pl.pallas_call(
        partial(gather_kernel, chunks),
        out_shape=shapes + [jax.ShapeDtypeStruct(small.shape, F32), half, half],
        in_specs=[ANY] * 3 + [VMEM] + [ANY] * 2,
        out_specs=[ANY] * 3 + [VMEM] + [ANY] * 2,
        scratch_shapes=[pltpu.VMEM((5,) + small.shape, BF16)] * 2
        + [pltpu.SemaphoreType.DMA((slots,))] * 2 + [pltpu.SemaphoreType.DMA((5,))],
        compiler_params=pltpu.CompilerParams(collective_id=0, has_side_effects=True),
    )(w1, w2, w3, small, xin, cot)


def run_scatter(grads, small, lout, igrad, tgrad):
    wide = [g.shape[-1] for g in grads]
    rows = [g.shape[-2] for g in grads]
    chunks = chunked([(n // 3,) * 3 if n % 384 == 0 and n < 1000 else (384,) * (n // 384) for n in wide])
    slots = len(chunks) * Scatter.SLOTS + 8
    scratch = []
    for r, n in zip(rows, wide):
        scratch += [pltpu.VMEM(s, BF16) for s in (
            (2, 4, r, n), (2, 4, r, n), (4, r, n), (4, r, n), (4, r, n), (3, r, n))]
    scratch += [pltpu.VMEM((5,) + SMALL, F32)] * 2
    scratch += [pltpu.SemaphoreType.DMA((slots,))] * 2 + [pltpu.SemaphoreType.DMA((3,))]
    out_shape = [jax.ShapeDtypeStruct((r, n), F32) for r, n in zip(rows, wide)]
    out_shape += [jax.ShapeDtypeStruct(SMALL, F32)]
    out_shape += [jax.ShapeDtypeStruct((4,) + lout.shape[2:], BF16), jax.ShapeDtypeStruct((4,) + lout.shape[2:], F32),
                  jax.ShapeDtypeStruct(tgrad.shape, F32)]
    return pl.pallas_call(
        partial(scatter_kernel, chunks),
        out_shape=out_shape,
        in_specs=[VMEM] * 4 + [ANY] * 3,
        out_specs=[VMEM] * 4 + [ANY] * 3,
        scratch_shapes=scratch,
        compiler_params=pltpu.CompilerParams(collective_id=1, has_side_effects=True, vmem_limit_bytes=56 * 2**20),
    )(*grads, small, lout, igrad, tgrad)


def pack_halves(shard):
    r, n = shard.shape
    return shard.reshape(r, 2, n // 2).transpose(1, 0, 2).reshape(2 * r, n // 2)


def unpack_halves(packed):
    r, n = packed.shape
    return packed.reshape(2, r // 2, n).transpose(1, 0, 2).reshape(r // 2, 2 * n)


def unpack_gathered(buf, at, wide):
    part = buf[..., at:at + wide].reshape(32, 2, 24, wide)
    return part.transpose(0, 2, 1, 3).reshape(768, 2 * wide)


def place_in_zeros(shard, index):
    n = shard.shape[0]
    return lax.dynamic_update_slice(jnp.zeros((32 * n,), shard.dtype), shard, (index * n,))


def split_grad(grad, c, packed):
    k, n = grad.shape
    g = grad.reshape(4, 2, 2, 2, k // 32, n)
    mine = lax.dynamic_index_in_dim(g, c, 2, keepdims=False)
    other = lax.dynamic_index_in_dim(g, 1 - c, 2, keepdims=False).astype(BF16)
    pairs = [(i, i ^ 1) for i in range(16)]
    total = mine + lax.ppermute(other, BATCH, pairs).astype(F32)
    total = total.transpose(1, 2, 0, 3, 4)
    if packed:
        r = k // 32
        total = total.reshape(2, 2, 4, r, 2, n // 2).transpose(0, 1, 2, 4, 3, 5).reshape(2, 2, 4, 2 * r, n // 2)
    return total


def whole_rows(inputs, time_embed, segment_ids, cotangent, first_gain, first_shift, mix_weight, mix_bias, out_weight,
               out_bias, second_gain, second_shift, up_weight, up_bias, down_weight, down_bias):
    b, y = lax.axis_index(BATCH), lax.axis_index(SEQ)
    c, index = b % 2, b * 2 + y
    smalls = [first_gain, first_shift, mix_bias, out_bias, second_gain, second_shift, up_bias, down_bias]
    flat = jnp.concatenate([place_in_zeros(v, index) for v in smalls] + [jnp.zeros((4 * 768,), BF16)]).reshape(SMALL)
    w1 = jnp.concatenate([pack_halves(mix_weight), pack_halves(out_weight)], axis=1)
    b1, b2, b3, total, xfull, cfull = run_gather(w1, pack_halves(up_weight), down_weight, flat, inputs, cotangent)
    mix, out, up = unpack_gathered(b1, 0, 1152), unpack_gathered(b1, 1152, 384), unpack_gathered(b2, 0, 1536)
    down = b3.reshape(3072, 768)
    gain1, shift1, mbias, obias = total[0], total[1], total[2:4].reshape(-1), total[4]
    gain2, shift2, ubias, dbias = total[5], total[6], total[7:11].reshape(-1), total[11]
    x = xfull.reshape(2, 128, 768)
    cot = cfull.reshape(2, 128, 768)
    time = lax.dynamic_slice_in_dim(time_embed, 2 * y, 2, 0)
    ids = lax.dynamic_slice_in_dim(segment_ids, 2 * y, 2, 0)
    params = (gain1, shift1, mix, mbias, out, obias, gain2, shift2, up, ubias, down, dbias)
    layer_out, x_grad, g = layer(x, time, ids, cot, params)
    g_mix, g_out, g_up, g_down = g[2], g[4], g[8], g[10]
    small_grads = jnp.concatenate([g[0], g[1], g[3], g[5], g[6], g[7], g[9], g[11], jnp.zeros((4 * 768,), F32)]).reshape(SMALL)
    grads = [split_grad(g_down, c, False), split_grad(g_up, c, True),
             jnp.concatenate([split_grad(g_out, c, True), split_grad(g_mix, c, True)], -1)]
    tg = jnp.sum(x_grad, 1).reshape(2, 2, 384).transpose(1, 0, 2)
    tg = jnp.pad(tg, ((0, 0), (0, 6), (0, 0)))
    o3, o2, o1, total, lo, ig, tg = run_scatter(
        grads, small_grads, layer_out.reshape(2, 2, 64, 768), x_grad.reshape(2, 2, 64, 768), tg)
    parts, at = [], 0
    flat = total.reshape(-1)
    for v in smalls:
        n = v.shape[0]
        parts.append(lax.dynamic_slice(flat, (at + index * n,), (n,)))
        at += 32 * n
    time_grad = tg[:, :2].reshape(4, 384)
    return (lo, ig, time_grad, parts[0], parts[1], unpack_halves(o1[:, 384:]), parts[2], unpack_halves(o1[:, :384]), parts[3],
            parts[4], parts[5], unpack_halves(o2), parts[6], o3, parts[7])


def solution(mesh):
    fits = mesh.shape[BATCH] == 16 and mesh.shape[SEQ] == 2
    tokens, rows, vector, matrix = P(BATCH, SEQ, None), P(BATCH, None), P(AXES), P(AXES, None)
    params = (vector, vector, matrix, vector, matrix, vector, vector, vector, matrix, vector, matrix, vector)
    return jax.shard_map(
        whole_rows if fits else any_mesh,
        mesh=mesh,
        in_specs=(tokens, rows, rows, tokens) + params,
        out_specs=(tokens, tokens, P(BATCH, SEQ)) + params,
        check_vma=False,
    )
```

time: 1150 us -> 410 us (0.36)
  waiting for transfers between devices: 772 us -> 0.01 us
  Pallas kernels: 0 us -> 193 us
  blocking collectives: 135 us -> 0 us
  local copies, waits for them, and re-layouts: 69.1 us -> 128 us
  matrix products: 88.2 us -> 42.1 us
  starting transfers between devices: 41.4 us -> 1.05 us
  other arithmetic: 14.8 us -> 39 us
  between operations: 15.6 us -> 1.82 us
    reduce_scatter x4 -> x0, waiting for transfers between devices: 450 us -> none  [the longest x1 142 us: shards(): lax.psum_scatter(up_weight_grad, ('batch', 'seq'), scatter_dimension=0, t...]
    all_gather x8 -> x0, waiting for transfers between devices: 277 us -> none  [the longest x1 63.4 us: shards(): lax.all_gather(up_weight, ('batch', 'seq'), axis=0, tiled=True)]
    pallas_call x0 -> x2, Pallas kernels: none -> 193 us  [the longest x1 96.3 us: run_gather(): pl.pallas_call(partial(gather_kernel, chunks), out_shape=shapes + [jax.Sh...]
    unnamed x3 -> x0, blocking collectives: 124 us -> none
    reshape x0 -> x29, local copies, waits for them, and re-layouts: none -> 47.8 us  [the longest x5 16 us: split_grad(): total.reshape(2, 2, 4, r, 2, n // 2).transpose(0, 1, 2, 4, 3, 5)]
    dot_general x23 -> x18, matrix products: 88.2 us -> 42.1 us  [contract(): lax.dot_general(a, b, ((over_a, over_b), batch), preferred_element_type=F32)]
    all_to_all x11 -> x0, starting transfers between devices: 40.6 us -> none  [the longest x2 8.32 us: forward_state(): lax.all_to_all(values, 'seq', split_axis=2, concat_axis=1, tiled=True)]
    all_to_all x11 -> x0, waiting for transfers between devices: 40.2 us -> none  [the longest x2 9.9 us: forward_state(): lax.all_to_all(values, 'seq', split_axis=2, concat_axis=1, tiled=True)]
  transfers between devices with their start and end apart: 24 -> 4, of which waited for: 23 -> 0; matrix products, arithmetic and copies ran while one was open for 10% -> 24% of each run, Pallas kernels for 0% -> 0%
where the time goes in v1:
time: 410 us; the launch traced here: 405 us
  Pallas kernels  193 us (47%)
  local copies, waits for them, and re-layouts  128 us (31%)
  matrix products  42.1 us (10%)
  other arithmetic  39 us (10%)
    pallas_call x1, Pallas kernels, run_gather(): pl.pallas_call(partial(gather_kernel, chunks), out_shape=shapes + [jax.Sh...  96.3 us
    pallas_call x1, Pallas kernels, run_scatter(): pl.pallas_call(partial(scatter_kernel, chunks), out_shape=out_shape, in_s...  96.2 us
    dot_general x18, matrix products, contract(): lax.dot_general(a, b, ((over_a, over_b), batch), preferred_element_type=F32)  42.1 us
    unnamed x165, local copies, waits for them, and re-layouts  38.4 us
    transpose x4, other arithmetic, split_grad(): total = total.transpose(1, 2, 0, 3, 4)  16.2 us
    reshape x5, local copies, waits for them, and re-layouts, split_grad(): total.reshape(2, 2, 4, r, 2, n // 2).transpose(0, 1, 2, 4, 3, 5)  16 us
    reshape x3, local copies, waits for them, and re-layouts, unpack_gathered(): part = buf[..., at:at + wide].reshape(32, 2, 24, wide)  12.9 us
  transfers between devices with their start and end apart: 4, of which 0 were waited for; matrix products, arithmetic and copies ran while one was open for 24% of the time, Pallas kernels for 0%

profile of v1, /device:TPU:0, one launch (start us, length us, event | category | flops | bytes accessed | tf_op | source)
XLA Modules:
  0.0 404.5 jit_solution(12761831736392327618)
XLA Ops:
  11.7 1.6 copy.171
  14.0 96.3 %shard_map.271 = (bf16[4,2,2,2,48,1536]{5,4,3,2,1,0:T(8,128)(2,1)}, bf16[4,2,2,2,48,1536]{5,4,3,2,1,0:T(8,128)(2,1)}, bf16[4,2,2,2,96,768]{5,4,3,2,1,0:T(8,128)(...) custom-call(bf16[48,1536]{1,0:T(8,128)(2,1)} %pad_maximum_fusion.4.w1, ...), custom_call_target="tpu_custom_call" | custom-call | tf_op jit(solution)/shard_map/pallas_call | solution.py:380
  110.3 2.3 slice.59
  112.6 2.4 slice.65
  115.7 1.7 add_reduce_fusion
  117.4 1.9 bitcast_add_fusion.5
  119.3 1.8 slice_reduce_fusion
  125.0 1.9 convert_reduce_fusion.1
  128.8 2.7 copy.91
  140.8 9.2 %copy.101 = bf16[32,2,24,1536]{3,1,2,0:T(2,128)(2,1)} copy(bf16[32,2,24,1536]{3,2,1,0:T(8,128)(2,1)} %bitcast.282) | data formatting | bytes 9437184 | tf_op jit(solution)/shard_map/reshape | solution.py:427
  150.0 5.7 %copy.143 = bf16[96,8,2,1536]{3,1,2,0:T(8,128)(2,1)} copy(bf16[96,8,2,1536]{3,2,1,0:T(2,128)(2,1)} %bitcast.273) | data formatting | bytes 9437184
  155.7 5.5 %fusion.11 = (bf16[3072,256]{0,1:T(8,128)(2,1)}, f32[256,3072]{1,0:T(8,128)S(1)}) fusion(f32[3072]{0:T(1024)S(1)} %add.295, bf16[768,3072]{1,0:T(8,128)(2,1)} %bitcast.283, f32[256,768]{1,0:T(8,128)S(1)} %get-tuple-element.73, f32[768]{0:T(1024)S(1)} %copy-done.35, f32[768]{0:T(1024)S(1)} %copy-done.34, f32[256]{0:T(256)S(1)} %add_rsqrt_fusion.1, ...), kind=kOutput, calls=%fused_computation.26 | convolution fusion | flops 1213661184 | bytes 10244096 | tf_op jit(solution)/shard_map/dot_general | solution.py:31
  161.2 6.0 %convert_reduce_fusion = (f32[3072]{0:T(1024)}, bf16[256,3072]{1,0:T(8,128)(2,1)S(1)}) fusion(f32[256,3072]{1,0:T(8,128)S(1)} %get-tuple-element.75, bf16[256,768]{1,0:T(8,128)(2,1)S(1)} %bitcast.289, bf16[3072,768]{1,0:T(8,128)(2,1)} %bitcast.336), kind=kOutput, calls=%fused_computation.24 | convolution fusion | flops 1217393664 | bytes 9842688 | tf_op jit(solution)/shard_map/dot_general | solution.py:31
  167.2 3.1 multiply_reduce_fusion.2
  171.5 2.1 convert_reduce_fusion.2
  173.6 3.2 fusion.35
  176.7 2.2 fusion.33
  182.0 2.0 multiply_reduce_fusion
  186.7 1.4 convolution_convert_fusion.1
  190.9 1.6 copy.115
  193.3 1.9 copy.119
  197.5 1.9 copy.120
  199.5 4.2 %multiply_reduce_fusion.1 = (f32[256]{0:T(256)}, f32[768]{0:T(1024)}, f32[256]{0:T(256)}, f32[768]{0:T(1024)}, bf16[256,768]{1,0:T(8,128)(2,1)}, /*index=5*/f32[256,768]{1,0:T(8,128)}) fusion(bf16[2,2,64,768]{3,2,1,0:T(8,128)(2,1)} %get-tuple-element.28, f32[768]{0:T(1024)S(1)} %copy-done.38, f32[256]{0:T(256)} %rsqrt.26, f32[256]{0:T(256)} %div.35, ...), kind=kOutput, calls=%fused_computation.69 | convolution fusion | flops 912259072 | bytes 6313984 | tf_op jit(solution)/shard_map/dot_general | solution.py:31
  204.8 2.3 fusion.23
  207.2 1.4 fusion.14
  208.6 2.3 copy-done.6
  211.0 1.6 fusion.43
  212.6 3.6 copy-done.5
  216.3 1.7 fusion.13
  218.4 1.9 copy.102
  221.7 3.6 copy-done.4
  225.4 1.7 fusion.12
  227.2 1.6 convert_reduce_fusion.4
  228.8 1.6 convert_reduce_fusion.3
  243.4 5.7 %fusion.21 = bf16[256,768]{1,0:T(8,128)(2,1)} fusion(f32[256,768]{1,0:T(8,128)S(1)} %copy-done.12, bf16[3072,768]{1,0:T(8,128)(2,1)} %bitcast.337, f32[256,3072]{1,0:T(8,128)} %copy-done.63, f32[768]{0:T(1024)S(1)} %copy-done.60), kind=kOutput, calls=%fused_computation.47 | convolution fusion | flops 1212481536 | bytes 9047040 | tf_op jit(solution)/shard_map/dot_general | solution.py:31
  249.7 1.5 reshape.428.small
  251.3 2.4 bitcast_reduce_fusion
  256.3 4.7 %fusion.3 = f32[2,2,4,24,2304]{4,3,1,0,2:T(8,128)} fusion(bf16[4,2,2,24,2304]{4,3,2,1,0:T(8,128)(2,1)} %collective-permute-done.3, f32[4,2,2,2,24,2304]{5,4,3,2,1,0:T(8,128)} %copy-done.6, s32[]{:T(128)S(6)} %select_n.75), kind=kLoop, calls=%fused_computation.12 | loop fusion | flops 1769472 | bytes 8847364 | tf_op jit(solution)/shard_map/transpose | solution.py:443
  261.0 5.5 %reshape.426 = f32[2,2,4,24,2,1152]{5,4,3,1,0,2:T(2,128)} reshape(f32[2,2,4,24,2304]{4,3,1,0,2:T(8,128)} %fusion.3) | data formatting | bytes 7077888 | tf_op jit(solution)/shard_map/reshape | solution.py:446
  266.5 2.4 copy.121
  269.0 2.9 pad_maximum_fusion.g3
  272.6 4.6 %fusion = f32[2,2,4,24,3072]{4,3,2,1,0:T(8,128)} fusion(bf16[4,2,2,24,3072]{4,3,0,2,1:T(8,128)(2,1)} %collective-permute-done.1, f32[4,2,2,2,24,3072]{5,4,3,2,1,0:T(8,128)S(1)} %bitcast.271, s32[]{:T(128)S(6)} %select_n.75), kind=kLoop, calls=%fused_computation.5 | loop fusion | flops 2359296 | bytes 11796484 | tf_op jit(solution)/shard_map/transpose | solution.py:443
  277.2 7.4 %reshape.414 = f32[2,2,4,24,2,1536]{5,4,3,2,1,0:T(2,128)} reshape(f32[2,2,4,24,3072]{4,3,2,1,0:T(8,128)} %fusion) | data formatting | bytes 9437184 | tf_op jit(solution)/shard_map/reshape | solution.py:446
  284.6 5.4 %copy.107 = f32[2,2,4,2,24,1536]{5,4,3,2,1,0:T(8,128)} copy(f32[2,2,4,2,24,1536]{5,3,4,2,1,0:T(2,128)} %bitcast.274) | data formatting | bytes 9437184 | tf_op jit(solution)/shard_map/transpose | solution.py:446
  290.0 5.7 %fusion.1.g1 = f32[2,2,4,96,768]{4,3,2,1,0:T(8,128)} fusion(bf16[4,2,2,96,768]{4,3,0,2,1:T(8,128)(2,1)} %collective-permute-done, f32[4,2,2,2,96,768]{5,4,3,2,1,0:T(8,128)} %copy-done.4, s32[]{:T(128)S(6)} %select_n.75), kind=kLoop, calls=%fused_computation.7 | loop fusion | flops 2359296 | bytes 11796484 | tf_op jit(solution)/shard_map/transpose | solution.py:443
  295.8 96.2 %shard_map.272 = (f32[96,768]{1,0:T(8,128)}, f32[48,1536]{1,0:T(8,128)}, f32[48,1536]{1,0:T(8,128)}, f32[16,768]{1,0:T(8,128)}, bf16[4,64,768]{2,1,0:T(8,128)(2,...) custom-call(f32[2,2,4,96,768]{4,3,2,1,0:T(8,128)} %fusion.1.g1, f32[2,2,4,48,1536]{4,3,2,1,0:T(8,128)} %bitcast.272, ...), custom_call_target="tpu_custom_call" | custom-call | tf_op jit(solution)/shard_map/pallas_call | solution.py:406
  394.7 1.7 copy.139
  400.9 1.8 copy.204
  (260 shorter events, 68.7 us)
Async XLA Ops:
  0.6 134.3 %copy-start = (s32[4,128]{1,0:T(4,128)S(1)}, s32[4,128]{1,0:T(4,128)}, u32[]{:S(2)}) copy-start(s32[4,128]{1,0:T(4,128)} %param.18) | copy-start | bytes 6148
  115.7 16.5 %copy-start.31 = (f32[2,768]{1,0:T(2,128)}, f32[2,768]{1,0:T(2,128)S(1)}, u32[]{:S(2)}) copy-start(f32[2,768]{1,0:T(2,128)S(1)} %dynamic-slice_convert_fusion.2) | copy-start | bytes 18436
  121.2 11.1 %copy-start.37 = (f32[768]{0:T(1024)}, f32[768]{0:T(1024)S(1)}, u32[]{:S(2)}) copy-start(f32[768]{0:T(1024)S(1)} %get-tuple-element.56) | copy-start | bytes 9220
  140.5 31.0 %copy-start.11 = (f32[256,768]{1,0:T(8,128)}, f32[256,768]{1,0:T(8,128)S(1)}, u32[]{:S(2)}) copy-start(f32[256,768]{1,0:T(8,128)S(1)} %get-tuple-element.73) | copy-start | bytes 2359300
  140.5 26.7 %copy-start.42 = (f32[256]{0:T(256)}, f32[256]{0:T(256)S(1)}, u32[]{:S(2)}) copy-start(f32[256]{0:T(256)S(1)} %broadcast_multiply_fusion.5) | copy-start | bytes 3076
  140.8 26.4 %copy-start.52 = (f32[256]{0:T(256)}, f32[256]{0:T(256)S(1)}, u32[]{:S(2)}) copy-start(f32[256]{0:T(256)S(1)} %add_rsqrt_fusion.1) | copy-start | bytes 3076
  150.0 5.7 %copy-start.39 = (f32[4,768]{1,0:T(4,128)S(1)}, f32[4,768]{1,0:T(4,128)}, u32[]{:S(2)}) copy-start(f32[4,768]{1,0:T(4,128)} %slice.69) | copy-start | bytes 36868
  150.0 5.7 %copy-start.34 = (f32[768]{0:T(1024)S(1)}, f32[768]{0:T(1024)}, u32[]{:S(2)}) copy-start(f32[768]{0:T(1024)} %get-tuple-element.51) | copy-start | bytes 9220
  150.0 5.7 %copy-start.35 = (f32[768]{0:T(1024)S(1)}, f32[768]{0:T(1024)}, u32[]{:S(2)}) copy-start(f32[768]{0:T(1024)} %get-tuple-element.50) | copy-start | bytes 9220
  155.7 5.5 %copy-start.17 = (bf16[2,2,64,768]{3,2,1,0:T(8,128)(2,1)S(1)}, bf16[2,2,64,768]{3,2,1,0:T(8,128)(2,1)}, u32[]{:S(2)}) copy-start(bf16[2,2,64,768]{3,2,1,0:T(8,128)(2,1)} %get-tuple-element.32) | copy-start | bytes 1179652
  155.7 11.5 %slice-start.3 = ((s8[4718592]{0:T(1024)(128)(4,1)}), s8[4194304]{0:T(1024)(128)(4,1)S(1)}, s32[]{:S(2)}) async-start(s8[4718592]{0:T(1024)(128)(4,1)} %bitcast.284), calls=%async_computation.3 | async-start | bytes 8388608
  161.2 6.0 %copy-start.63 = (f32[256,3072]{1,0:T(8,128)}, f32[256,3072]{1,0:T(8,128)S(1)}, u32[]{:S(2)}) copy-start(f32[256,3072]{1,0:T(8,128)S(1)} %get-tuple-element.75) | copy-start | bytes 9437188
  161.2 6.0 %slice-start.4 = ((s8[4718592]{0:T(1024)(128)(4,1)}), s8[524288]{0:T(1024)(128)(4,1)S(1)}, s32[]{:S(2)}) async-start(s8[4718592]{0:T(1024)(128)(4,1)} %bitcast.284), calls=%async_computation.4 | async-start | bytes 1048576
  173.6 5.8 %copy-start.9 = (f32[256,768]{1,0:T(8,128)}, f32[256,768]{1,0:T(8,128)S(1)}, u32[]{:S(2)}) copy-start(f32[256,768]{1,0:T(8,128)S(1)} %get-tuple-element.60) | copy-start | bytes 2359300
  173.6 5.8 %copy-start.14 = (bf16[96,8,2,384]{3,1,2,0:T(8,128)(2,1)S(1)}, bf16[96,8,2,384]{3,1,2,0:T(8,128)(2,1)}, u32[]{:S(2)}) copy-start(bf16[96,8,2,384]{3,1,2,0:T(8,128)(2,1)} %copy-done.13) | copy-start | bytes 3538948
  178.9 75.4 %collective-permute-start.2 = (bf16[4,2,2,24,768]{4,3,2,1,0:T(8,128)(2,1)}, bf16[4,2,2,24,768]{4,3,2,1,0:T(8,128)(2,1)}, u32[]{:S(2)}, u32[]{:S(2)}) collective-permute-start(bf16[4,2,2,24,768]{4,3,2,1,0:T(8,128)(2,1)} %fusion.33), channel_id=1, source_target_pairs={{0,2},{2,0},{4,6},{6,4},{8,10},{10,8},{12,14},{14,12},{16,18},{18,... | collective-permute-start | bytes 1769480 | tf_op jit(solution)/shard_map/ppermute | solution.py:442
  185.3 4.6 %copy-start.24 = (bf16[24,128,64]{1,2,0:T(8,128)(2,1)}, bf16[24,128,64]{1,2,0:T(8,128)(2,1)S(1)}, u32[]{:S(2)}) copy-start(bf16[24,128,64]{1,2,0:T(8,128)(2,1)S(1)} %fusion.20) | copy-start | bytes 1179652
  190.9 8.5 %copy-start.3 = (bf16[96,8,2,1152]{3,1,2,0:T(8,128)(2,1)S(1)}, bf16[96,8,2,1152]{3,1,2,0:T(8,128)(2,1)}, u32[]{:S(2)}) copy-start(bf16[96,8,2,1152]{3,1,2,0:T(8,128)(2,1)} %copy-done.2) | copy-start | bytes 10616836
  190.9 8.5 %copy-start.32 = (f32[2,768]{1,0:T(2,128)S(1)}, f32[2,768]{1,0:T(2,128)}, u32[]{:S(2)}) copy-start(f32[2,768]{1,0:T(2,128)} %copy-done.31) | copy-start | bytes 18436
  190.9 8.5 %copy-start.38 = (f32[768]{0:T(1024)S(1)}, f32[768]{0:T(1024)}, u32[]{:S(2)}) copy-start(f32[768]{0:T(1024)} %copy-done.37) | copy-start | bytes 9220
  207.1 3.8 copy-start.6
  207.2 3.8 copy-start.12
  207.2 3.8 copy-start.29
  207.2 3.8 copy-start.36
  207.2 3.8 copy-start.43
  207.2 3.8 copy-start.53
  210.9 45.3 %collective-permute-start.3 = (bf16[4,2,2,24,2304]{4,3,2,1,0:T(8,128)(2,1)}, bf16[4,2,2,24,2304]{4,3,2,1,0:T(8,128)(2,1)}, u32[]{:S(2)}, u32[]{:S(2)}) collective-permute-start(bf16[4,2,2,24,2304]{4,3,2,1,0:T(8,128)(2,1)} %fusion.14), channel_id=1, source_target_pairs={{0,2},{2,0},{4,6},{6,4},{8,10},{10,8},{12,14},{14,12},{16,18},{18,... | collective-permute-start | bytes 5308424 | tf_op jit(solution)/shard_map/ppermute | solution.py:442
  218.0 53.8 %collective-permute-start.1 = (bf16[4,2,2,24,3072]{4,3,0,2,1:T(8,128)(2,1)}, bf16[4,2,2,24,3072]{4,3,0,2,1:T(8,128)(2,1)}, u32[]{:S(2)}, u32[]{:S(2)}) collective-permute-start(bf16[4,2,2,24,3072]{4,3,0,2,1:T(8,128)(2,1)} %fusion.13), channel_id=1, source_target_pairs={{0,2},{2,0},{4,6},{6,4},{8,10},{10,8},{12,14},{14,12},{16,18},{18,... | collective-permute-start | bytes 7077896 | tf_op jit(solution)/shard_map/ppermute | solution.py:442
  225.3 5.2 %copy-start.51 = (f32[768]{0:T(1024)S(1)}, f32[768]{0:T(1024)}, u32[]{:S(2)}) copy-start(f32[768]{0:T(1024)} %get-tuple-element.44) | copy-start | bytes 9220
  225.3 6.5 %copy-start.50 = (f32[768]{0:T(1024)S(1)}, f32[768]{0:T(1024)}, u32[]{:S(2)}) copy-start(f32[768]{0:T(1024)} %get-tuple-element.47) | copy-start | bytes 9220
  225.3 10.4 %copy-start.49 = (f32[768]{0:T(1024)S(1)}, f32[768]{0:T(1024)}, u32[]{:S(2)}) copy-start(f32[768]{0:T(1024)} %get-tuple-element.59) | copy-start | bytes 9220
  225.3 11.7 %copy-start.62 = (f32[768]{0:T(1024)S(1)}, f32[768]{0:T(1024)}, u32[]{:S(2)}) copy-start(f32[768]{0:T(1024)} %get-tuple-element.41) | copy-start | bytes 9220
  225.4 13.0 %copy-start.61 = (f32[768]{0:T(1024)S(1)}, f32[768]{0:T(1024)}, u32[]{:S(2)}) copy-start(f32[768]{0:T(1024)} %get-tuple-element.48) | copy-start | bytes 9220
  225.4 14.3 %copy-start.59 = (f32[256]{0:T(256)S(1)}, f32[256]{0:T(256)}, u32[]{:S(2)}) copy-start(f32[256]{0:T(256)} %get-tuple-element.43) | copy-start | bytes 3076
  225.4 14.8 %copy-start.58 = (f32[256]{0:T(256)S(1)}, f32[256]{0:T(256)}, u32[]{:S(2)}) copy-start(f32[256]{0:T(256)} %get-tuple-element.46) | copy-start | bytes 3076
  225.4 15.4 %copy-start.54 = (f32[3072]{0:T(1024)S(1)}, f32[3072]{0:T(1024)}, u32[]{:S(2)}) copy-start(f32[3072]{0:T(1024)} %get-tuple-element.80) | copy-start | bytes 36868
  225.4 16.7 %copy-start.48 = (f32[768]{0:T(1024)S(1)}, f32[768]{0:T(1024)}, u32[]{:S(2)}) copy-start(f32[768]{0:T(1024)} %get-tuple-element.82) | copy-start | bytes 9220
  225.4 18.0 %copy-start.60 = (f32[768]{0:T(1024)S(1)}, f32[768]{0:T(1024)}, u32[]{:S(2)}) copy-start(f32[768]{0:T(1024)} %get-tuple-element.49) | copy-start | bytes 9220
  227.1 62.9 %collective-permute-start = (bf16[4,2,2,96,768]{4,3,0,2,1:T(8,128)(2,1)}, bf16[4,2,2,96,768]{4,3,0,2,1:T(8,128)(2,1)}, u32[]{:S(2)}, u32[]{:S(2)}) collective-permute-start(bf16[4,2,2,96,768]{4,3,0,2,1:T(8,128)(2,1)} %fusion.12), channel_id=1, source_target_pairs={{0,2},{2,0},{4,6},{6,4},{8,10},{10,8},{12,14},{14,12},{16,18},{18,... | collective-permute-start | bytes 7077896 | tf_op jit(solution)/shard_map/ppermute | solution.py:442
  243.4 7.8 %copy-start.8 = (bf16[2,2,64,768]{3,2,1,0:T(8,128)(2,1)S(1)}, bf16[2,2,64,768]{3,2,1,0:T(8,128)(2,1)}, u32[]{:S(2)}) copy-start(bf16[2,2,64,768]{3,2,1,0:T(8,128)(2,1)} %get-tuple-element.28) | copy-start | bytes 1179652
  243.4 7.8 %copy-start.10 = (f32[256,768]{1,0:T(8,128)S(1)}, f32[256,768]{1,0:T(8,128)}, u32[]{:S(2)}) copy-start(f32[256,768]{1,0:T(8,128)} %copy-done.9) | copy-start | bytes 2359300
  243.4 7.8 %copy-start.55 = (f32[256]{0:T(256)S(1)}, f32[256]{0:T(256)}, u32[]{:S(2)}) copy-start(f32[256]{0:T(256)} %rsqrt.26) | copy-start | bytes 3076
  249.1 5.2 %copy-start.15 = (f32[4,2,2,2,24,768]{5,4,3,2,1,0:T(8,128)S(1)}, f32[4,2,2,2,24,768]{5,4,3,2,1,0:T(8,128)}, u32[]{:S(2)}) copy-start(f32[4,2,2,2,24,768]{5,4,3,2,1,0:T(8,128)} %fusion.35) | copy-start | bytes 7077892
  261.0 10.9 %slice-start = ((s8[9437184]{0:T(1024)(128)(4,1)}), s8[1048576]{0:T(1024)(128)(4,1)S(1)}, s32[]{:S(2)}) async-start(s8[9437184]{0:T(1024)(128)(4,1)} %bitcast.269), calls=%async_computation | async-start | bytes 2097152
  266.5 5.3 %slice-start.1 = ((s8[9437184]{0:T(1024)(128)(4,1)}), s8[4194304]{0:T(1024)(128)(4,1)S(1)}, s32[]{:S(2)}) async-start(s8[9437184]{0:T(1024)(128)(4,1)} %bitcast.269), calls=%async_computation.1 | async-start | bytes 8388608
  392.0 10.7 %copy-start.30 = (f32[4,64,768]{2,1,0:T(8,128)S(1)}, f32[4,64,768]{2,1,0:T(8,128)}, u32[]{:S(2)}) copy-start(f32[4,64,768]{2,1,0:T(8,128)} %get-tuple-element.100) | copy-start | bytes 2359300
  392.0 11.6 %copy-start.33 = (f32[96,768]{1,0:T(8,128)S(1)}, f32[96,768]{1,0:T(8,128)}, u32[]{:S(2)}) copy-start(f32[96,768]{1,0:T(8,128)} %get-tuple-element.112) | copy-start | bytes 884740
  392.0 12.3 %copy-start.1 = (s32[4,128]{1,0:T(4,128)S(1)}, s32[4,128]{1,0:T(4,128)}, u32[]{:S(2)}) copy-start(s32[4,128]{1,0:T(4,128)} %param.18) | copy-start | bytes 6148
  (25 other events, 48.8 us)

commit v2 on v1

v2 whole, which is shorter than its diff:
```python
from functools import partial
import math
from types import SimpleNamespace

import jax
import jax.numpy as jnp
from jax import lax
from jax.experimental import pallas as pl
from jax.experimental.pallas import tpu as pltpu
from jax.sharding import PartitionSpec as P

HEAD_DIM = 64
EPSILON = 1e-05
NEG_FILL = -1e30
BATCH, SEQ = "batch", "seq"
AXES = (BATCH, SEQ)
F32, BF16 = jnp.float32, jnp.bfloat16


def norm_back(d_out, normal, inv, gain):
    g = d_out * gain
    return inv * (g - jnp.mean(g, -1, keepdims=True) - normal * jnp.mean(g * normal, -1, keepdims=True))


def normal_part(hidden):
    centred = hidden - jnp.mean(hidden, -1, keepdims=True)
    inv = lax.rsqrt(jnp.mean(centred * centred, -1, keepdims=True) + EPSILON)
    return centred * inv, inv


def contract(a, b, over_a, over_b, batch=((), ())):
    return lax.dot_general(a, b, ((over_a, over_b), batch), preferred_element_type=F32)


def layer(inputs, time, ids, cot, params):
    (gain1, shift1, mix, mbias, out, obias, gain2, shift2, up, ubias, down, dbias) = params
    gain1, shift1, mbias, obias, gain2, shift2, ubias, dbias = (
        v.astype(F32) for v in (gain1, shift1, mbias, obias, gain2, shift2, ubias, dbias))
    rows, length, width = inputs.shape
    heads = width // HEAD_DIM
    scale = 1.0 / math.sqrt(HEAD_DIM)
    flat = lambda t: t.reshape(rows * length, -1)
    by_head = lambda t: t.reshape(rows, length, heads, HEAD_DIM).transpose(0, 2, 1, 3).reshape(rows * heads, length, HEAD_DIM)
    unhead = lambda t: flat(t.reshape(rows, heads, length, HEAD_DIM).transpose(0, 2, 1, 3))
    each = ((0,), (0,))
    cot = flat(cot)
    res_in = flat(inputs.astype(F32) + time.astype(F32)[:, None, :])
    norm1, inv1 = normal_part(res_in)
    normed1 = (norm1 * gain1 + shift1).astype(BF16)
    proj = contract(normed1, mix, (1,), (0,))
    q = by_head((proj[:, :width] + mbias[:width]).astype(BF16))
    k = by_head(proj[:, width:2 * width].astype(BF16))
    v = by_head((proj[:, 2 * width:] + mbias[width:]).astype(BF16))
    scores = contract(q, k, (2,), (2,), each) * scale
    same = jnp.repeat(ids[:, :, None] == ids[:, None, :], heads, axis=0)
    masked = jnp.where(same, scores, NEG_FILL)
    top = jnp.max(masked, -1, keepdims=True)
    log_total = top + jnp.log(jnp.sum(jnp.exp(masked - top), -1, keepdims=True))
    probs = jnp.exp(masked - log_total)
    probs16 = probs.astype(BF16)
    att = unhead(contract(probs16, v, (2,), (1,), each).astype(BF16))
    res_mid = res_in + (contract(att, out, (1,), (0,)) + obias)
    norm2, inv2 = normal_part(res_mid)
    normed2 = (norm2 * gain2 + shift2).astype(BF16)
    hid = contract(normed2, up, (1,), (0,)) + ubias
    cdf = 0.5 * (1.0 + lax.erf(hid * math.sqrt(0.5)))
    act = (hid * cdf).astype(BF16)
    layer_out = (res_mid + contract(act, down, (1,), (0,)) + dbias).astype(BF16)

    cot32 = cot.astype(F32)
    slope = cdf + hid * jnp.exp(-0.5 * hid * hid) * (1.0 / math.sqrt(2 * math.pi))
    d_hid = (contract(cot, down, (1,), (1,)) * slope).astype(BF16)
    d_n2 = contract(d_hid, up, (1,), (1,))
    d_mid = cot32 + norm_back(d_n2, norm2, inv2, gain2)
    d_br = d_mid.astype(BF16)
    d_att = by_head(contract(d_br, out, (1,), (1,)).astype(BF16))
    d_pr = contract(d_att, v, (2,), (2,), each)
    d_sc = (probs * (d_pr - jnp.sum(probs * d_pr, -1, keepdims=True))).astype(BF16)
    d_q = unhead((contract(d_sc, k, (2,), (1,), each) * scale).astype(BF16))
    d_k = unhead((contract(d_sc, q, (1,), (1,), each) * scale).astype(BF16))
    d_v = unhead(contract(probs16, d_att, (1,), (1,), each).astype(BF16))
    d_proj = jnp.concatenate([d_q, d_k, d_v], -1)
    d_n1 = contract(d_proj, mix, (1,), (1,))
    x_grad = d_mid + norm_back(d_n1, norm1, inv1, gain1)

    def col(t):
        return jnp.sum(t.astype(F32), axis=0)

    weigh = lambda a, b: contract(a, b, (0,), (0,))
    grads = (col(d_n1 * norm1), col(d_n1), weigh(normed1, d_proj), jnp.concatenate([col(d_q), col(d_v)]),
             weigh(att, d_br), col(d_br), col(d_n2 * norm2), col(d_n2), weigh(normed2, d_hid), col(d_hid),
             weigh(act, cot), col(cot32))
    return layer_out.reshape(inputs.shape), x_grad.reshape(inputs.shape), grads


def gather_all(shard):
    return lax.all_gather(shard, AXES, axis=0, tiled=True)


def scatter_sum(grad):
    return lax.psum_scatter(grad, AXES, scatter_dimension=0, tiled=True)


def rows_whole(tensor):
    return lax.all_to_all(tensor, SEQ, split_axis=0, concat_axis=1, tiled=True)


def rows_split(tensor):
    return lax.all_to_all(tensor, SEQ, split_axis=1, concat_axis=0, tiled=True)


def any_mesh(inputs, time_embed, segment_ids, cotangent, *shards):
    y, count = lax.axis_index(SEQ), inputs.shape[0] // lax.axis_size(SEQ)
    mine = [lax.dynamic_slice_in_dim(t, y * count, count, 0) for t in (time_embed, segment_ids)]
    layer_out, x_grad, grads = layer(
        rows_whole(inputs), mine[0], mine[1], rows_whole(cotangent), [gather_all(w) for w in shards])
    time_grad = lax.all_to_all(jnp.sum(x_grad, 1), SEQ, split_axis=1, concat_axis=0, tiled=True)
    return (rows_split(layer_out), rows_split(x_grad), time_grad) + tuple(scatter_sum(g) for g in grads)


MESH = pl.DeviceIdType.MESH
Z_CHIPS = 4
TOKENS, WIDTH, HIDDEN, PART = 256, 768, 3072, 384
SMALL = (16, WIDTH)
TRANSPOSED = ((1,), (1,))
TOKEN_SUM = ((0,), (0,))


class Place:
    def __init__(self):
        b, self.y = lax.axis_index(BATCH), lax.axis_index(SEQ)
        self.z, self.x, self.c = b // 4, (b // 2) % 2, b % 2
        z, x, c, y = self.z, self.x, self.c, self.y
        self.x2, self.y2 = x + (1 - 2 * x) * (1 - c), y + (1 - 2 * y) * c
        self.x3, self.y3 = x + (1 - 2 * x) * c, y + (1 - 2 * y) * (1 - c)
        self.near = self.at(z, self.x2, c, self.y2)
        self.far = self.at(z, self.x3, c, self.y3)
        self.twin = self.at(z, x, 1 - c, y)
        self.x_peer = self.at(z, 1 - x, c, y)
        self.y_peer = self.at(z, x, c, 1 - y)
        self.z_slots = [lax.rem(z + d, Z_CHIPS) for d in (1, 2, 3)]
        self.z_peers = [self.at(q, x, c, y) for q in self.z_slots]

    @staticmethod
    def at(z, x, c, y):
        return ((z * 2 + x) * 2 + c, y)

    def role(self, c, x, y):
        dx, dy = (x + self.x) % 2, (y + self.y) % 2
        return (dx + 2 * dy) * (1 - c) + (dy + 2 * dx) * c

    def of_role(self, c, role):
        low, high = role % 2, role // 2
        dx, dy = low * (1 - c) + high * c, high * (1 - c) + low * c
        return (self.x + dx) % 2, (self.y + dy) % 2

    def greet(self):
        barrier = pltpu.get_barrier_semaphore()
        partners = self.z_peers + [self.near, self.far, self.twin]
        for partner in partners:
            pl.semaphore_signal(barrier, inc=1, device_id=partner, device_id_type=MESH)
        pl.semaphore_wait(barrier, len(partners))


class Wires:
    def __init__(self, send_sem, recv_sem, place):
        self.send_sem, self.recv_sem, self.place = send_sem, recv_sem, place
        self.sent, self.used = [], 0

    def slots(self, count):
        self.used += count
        return self.used - count

    def start(self, src, dst, slot, device):
        copy = pltpu.make_async_remote_copy(
            src_ref=src, dst_ref=dst, send_sem=self.send_sem.at[slot], recv_sem=self.recv_sem.at[slot],
            device_id=device, device_id_type=MESH,
        )
        copy.start()
        self.sent.append(copy)
        return copy

    def arrived(self, dst, slot):
        pltpu.make_async_remote_copy(
            src_ref=dst, dst_ref=dst, send_sem=self.send_sem.at[slot], recv_sem=self.recv_sem.at[slot],
            device_id=self.place.twin, device_id_type=MESH,
        ).wait_recv()

    def left(self, copies):
        for copy in copies:
            copy.wait_send()
        self.sent = [kept for kept in self.sent if all(kept is not copy for copy in copies)]

    def finish(self):
        for copy in self.sent:
            copy.wait_send()
        self.sent = []


class Gather:
    def __init__(self, wires, place, own, buf, at, wide):
        self.w, self.p, self.own, self.buf, self.cols = wires, place, own, buf, pl.ds(at, wide)
        self.base, self.copies = wires.slots(10), []

    def send(self, src, dst, slot, device):
        self.copies.append(self.w.start(src, dst, self.base + slot, device))

    def mine(self):
        p = self.p
        return self.buf.at[p.z, p.x, p.c, p.y, :, self.cols]

    def block(self, x, y, c):
        return self.buf.at[:, x, c, y, :, self.cols]

    def begin(self):
        for j, peer in enumerate(self.p.z_peers):
            self.send(self.own.at[:, self.cols], self.mine(), j, peer)

    def after_z(self):
        p = self.p
        for j in range(3):
            self.w.arrived(self.mine(), self.base + j)
        b = self.block(p.x, p.y, p.c)
        self.send(b, b, 3, p.near)
        self.send(b, b, 4, p.far)
        self.send(b, b, 6, p.twin)

    def after_near(self):
        p = self.p
        b = self.block(p.x2, p.y2, p.c)
        self.w.arrived(b, self.base + 3)
        self.send(b, b, 5, p.far)
        self.send(b, b, 7, p.twin)

    def after_far(self):
        p = self.p
        b = self.block(p.x3, p.y3, p.c)
        self.w.arrived(b, self.base + 4)
        self.send(b, b, 8, p.twin)
        b = self.block(1 - p.x, 1 - p.y, p.c)
        self.w.arrived(b, self.base + 5)
        self.send(b, b, 9, p.twin)
        for j in range(6, 10):
            self.w.arrived(self.block(p.x, p.y, 1 - p.c), self.base + j)

    def halves_in_place(self):
        self.w.left(self.copies)
        rows = self.buf.shape[-2] // 2

        @pl.loop(0, 16)
        def _(pair):
            z, x, c = pair // 4, (pair // 2) % 2, pair % 2
            v = [self.buf[z, x, c, y, :, self.cols].astype(F32) for y in (0, 1)]
            for h in (0, 1):
                part = slice(h * rows, h * rows + rows)
                self.buf[z, x, c, h, :, self.cols] = jnp.concatenate([v[0][part], v[1][part]], 0).astype(BF16)


class Scatter:
    def __init__(self, wires, place, rows, cols, keep, s1, r1, s2, r2, sz, rz, out, out_cols):
        self.w, self.p, self.rows, self.cols, self.out_cols = wires, place, rows, cols, out_cols
        self.keep, self.s1, self.r1, self.s2, self.r2, self.sz, self.rz, self.out = keep, s1, r1, s2, r2, sz, rz, out
        self.base, self.quarter, self.packed = wires.slots(5), Z_CHIPS * rows, rows % 16 != 0
        wide = cols.size // 2 if self.packed else cols.size
        self.z_cols = pl.ds(cols.start // 2 if self.packed else cols.start, wide)

    def begin(self, left, right):
        q = self.quarter
        for role in range(4):
            rows = slice(role * q, role * q + q)
            total = contract(left[0][rows], right[0], (1,), (0,)) + contract(left[1][rows], right[1], (1,), (0,))
            at = pl.ds((role % 2) * q, q)
            if role < 2:
                self.keep[at, self.cols] = total
            else:
                self.s1[at, self.cols] = total.astype(BF16)
        both = pl.ds(0, 2 * q)
        self.w.start(self.s1.at[both, self.cols], self.r1.at[both, self.cols], self.base, self.p.far)

    def after_far(self):
        q = self.quarter
        self.w.arrived(self.r1.at[pl.ds(0, 2 * q), self.cols], self.base)
        at = pl.ds(q, q)
        self.s2[:, self.cols] = (self.keep[at, self.cols] + self.r1[at, self.cols].astype(F32)).astype(BF16)
        self.w.start(self.s2.at[:, self.cols], self.r2.at[:, self.cols], self.base + 1, self.p.near)

    def after_near(self):
        q, n = self.quarter, self.rows
        self.w.arrived(self.r2.at[:, self.cols], self.base + 1)
        at = pl.ds(0, q)
        total = self.keep[at, self.cols] + self.r1[at, self.cols].astype(F32) + self.r2[:, self.cols].astype(F32)
        for z in range(Z_CHIPS):
            piece = total[z * n:z * n + n]

            @pl.when(z == self.p.z)
            def _():
                self.out[:, self.out_cols] = piece

            if self.packed:
                half = self.z_cols.size
                piece = jnp.concatenate([piece[:, :half], piece[:, half:]], 0)
            self.sz[z, :, self.z_cols] = piece.astype(BF16)
        for j, (z, peer) in enumerate(zip(self.p.z_slots, self.p.z_peers)):
            self.w.start(self.sz.at[z, :, self.z_cols], self.rz.at[j, :, self.z_cols], self.base + 2 + j, peer)

    def after_z(self):
        total = 0.0
        for j in range(3):
            self.w.arrived(self.rz.at[j, :, self.z_cols], self.base + 2 + j)
            total = total + self.rz[j, :, self.z_cols].astype(F32)
        if self.packed:
            total = jnp.concatenate([total[:self.rows], total[self.rows:]], 1)
        self.out[:, self.out_cols] = self.out[:, self.out_cols] + total


class Butterfly:
    def __init__(self, wires, place, send, recv):
        self.w, self.send, self.recv, self.base = wires, send, recv, wires.slots(5)
        self.peers = [place.twin, place.y_peer, place.x_peer]
        self.peers.append(place.at(place.z + 1 - 2 * (place.z % 2), place.x, place.c, place.y))
        self.peers.append(place.at(lax.rem(place.z + 2, Z_CHIPS), place.x, place.c, place.y))
        self.step = 0

    def begin(self, value):
        i = self.step
        self.send[i] = value.astype(self.send.dtype)
        self.w.start(self.send.at[i], self.recv.at[i], self.base + i, self.peers[i])

    def next(self):
        i = self.step
        self.w.arrived(self.recv.at[i], self.base + i)
        value = self.send[i].astype(F32) + self.recv[i].astype(F32)
        self.step += 1
        if self.step < 5:
            self.begin(value)
        return value


def merged(value):
    return value.reshape(-1, value.shape[-1])


def by_rows(step, body, *carry):
    return lax.fori_loop(0, TOKENS // step, lambda i, kept: body(i, pl.ds(pl.multiple_of(i * step, step), step), *kept), carry)


def folded(value):
    return jnp.sum(value.reshape(value.shape[0] // 8, 8, value.shape[1]), 0)


def column_sums(value):
    return contract(jnp.ones((8, value.shape[0]), BF16), value, (1,), (0,))[0:1]


def token_block(i):
    return i // 4, (i // 2) % 2, pl.ds(pl.multiple_of((i % 2) * 32, 32), 32)


def scratch_table(slots):
    k, w = WIDTH // 2, WIDTH
    return [
        ("par_send", (5,) + SMALL, BF16), ("par_recv", (5,) + SMALL, BF16), ("par", SMALL, F32),
        ("sum_send", (5,) + SMALL, F32), ("sum_recv", (5,) + SMALL, F32), ("sums", SMALL, F32),
        ("b1", (4, 2, 2, 2, 48, 1536), BF16), ("b2", (4, 2, 2, 2, 48, 1536), BF16), ("b3", (4, 2, 2, 2, 96, w), BF16),
        ("x0", (2, 2, 64, w), BF16), ("cot", (2, 2, 2, 64, w), BF16),
        ("res_in", (TOKENS, w), F32), ("normed1", (TOKENS, w), BF16), ("qkv", (TOKENS, 3 * w), BF16),
        ("probs", (12, TOKENS, 128), F32), ("att", (TOKENS, w), BF16), ("res_mid", (TOKENS, w), F32),
        ("normed2", (TOKENS, w), BF16), ("slope", (TOKENS, HIDDEN), F32), ("act", (TOKENS, HIDDEN), BF16),
        ("pick", (2, k, w), BF16), ("pick_act", (2, 192, PART), BF16),
        ("t1", (2, k, TOKENS), BF16), ("t1_send", (k, TOKENS), BF16),
        ("to", (2, k, TOKENS), BF16), ("to_send", (k, TOKENS), BF16),
        ("t2", (2, k, TOKENS), BF16), ("t2_send", (k, TOKENS), BF16),
        ("ta", (2, 4, 4, 96, TOKENS), BF16), ("ta_send", (4, 4, 96, TOKENS), BF16),
        ("d_hid", (2, TOKENS, HIDDEN), BF16), ("d_norm", (TOKENS, w), F32), ("d_mid", (TOKENS, w), F32),
        ("d_branch", (2, TOKENS, w), BF16), ("d_att", (TOKENS, w), BF16), ("d_proj", (2, TOKENS, 3 * w), BF16),
        ("lo", (2, 2, 64, w), BF16), ("ig", (2, 2, 64, w), F32), ("tg", (2, 8, PART), F32),
        ("keep_d", (768, w), F32), ("s1_d", (768, w), BF16), ("r1_d", (768, w), BF16), ("s2_d", (PART, w), BF16),
        ("r2_d", (PART, w), BF16), ("sz_d", (4, 96, w), BF16), ("rz_d", (3, 96, w), BF16),
        ("keep_u", (192, HIDDEN), F32), ("s1_u", (192, HIDDEN), BF16), ("r1_u", (192, HIDDEN), BF16),
        ("s2_u", (96, HIDDEN), BF16), ("r2_u", (96, HIDDEN), BF16), ("sz_u", (4, 48, 1536), BF16), ("rz_u", (3, 48, 1536), BF16),
        ("r1_m", (192, HIDDEN), BF16),
        ("s2_m", (96, HIDDEN), BF16), ("r2_m", (96, HIDDEN), BF16), ("sz_m", (4, 48, 1536), BF16), ("rz_m", (3, 48, 1536), BF16),
        ("send_sem", (slots,), None), ("recv_sem", (slots,), None), ("local_sem", (10,), None),
    ]


SLOTS = 240


def layer_kernel(names, w1, w2, w3, small, time, ids_down, ids_along, xin, cin,
                 o_mix, o_out, o_up, o_down, o_small, lo_out, ig_out, tg_out, *scratch):
    m = SimpleNamespace(**dict(zip(names, scratch)))
    p = Place()
    p.greet()
    wires = Wires(m.send_sem, m.recv_sem, p)
    me, twin = p.c, 1 - p.c
    scale = 1.0 / math.sqrt(HEAD_DIM)

    own, bufs = (w1, w2, w3), (m.b1, m.b2, m.b3)
    locs = [pltpu.make_async_copy(own[i], bufs[i].at[p.z, p.x, p.c, p.y], m.local_sem.at[i]) for i in range(3)]
    rows_own, rows_other = pl.ds(2 * p.y, 2), pl.ds(2 - 2 * p.y, 2)
    locs.append(pltpu.make_async_copy(xin.at[rows_own], m.x0.at[:, p.y], m.local_sem.at[3]))
    locs.append(pltpu.make_async_copy(cin.at[rows_own], m.cot.at[me, :, p.y], m.local_sem.at[4]))
    for copy in locs:
        copy.start()
    swap = wires.slots(3)
    wires.start(xin.at[rows_other], m.x0.at[:, p.y], swap, p.y_peer)
    params = Butterfly(wires, p, m.par_send, m.par_recv)
    params.begin(small[...].astype(F32))

    plan = [(0, PART * i, PART) for i in range(4)] + [(1, PART * i, PART) for i in range(4)] + [(2, 256 * i, 256) for i in range(3)]
    gathers = [Gather(wires, p, own[w], bufs[w], at, wide) for w, at, wide in plan]
    ahead = 3
    for g in gathers[:ahead]:
        g.begin()
    wires.start(cin.at[rows_other], m.cot.at[me, :, p.y], swap + 1, p.y_peer)

    def z_step(k):
        gathers[k].after_z()
        if k + ahead < len(gathers):
            gathers[k + ahead].begin()

    def near_step(k):
        gathers[k].after_near()

    def far_step(k):
        gathers[k].after_far()
        if plan[k][0] < 2:
            gathers[k].halves_in_place()

    lane, row = lax.broadcasted_iota(jnp.int32, (24, WIDTH), 1), lax.broadcasted_iota(jnp.int32, (24, WIDTH), 0)
    lane_a, row_a = lax.broadcasted_iota(jnp.int32, (192, PART), 1), lax.broadcasted_iota(jnp.int32, (192, PART), 0)
    for side, c in ((0, me), (1, twin)):
        pieces = []
        for role in range(4):
            x, y = p.of_role(c, role)
            for z in range(Z_CHIPS):
                first = (((z * 2 + x) * 2 + c) * 2 + y) * 24
                pieces.append((lane == row + first).astype(F32))
        m.pick[side] = jnp.concatenate(pieces, 0).astype(BF16)
        m.pick_act[side] = (lane_a == row_a + c * 192).astype(F32).astype(BF16)

    twin_base = wires.slots(16)

    def transposed(value, ref, send, slot):
        ref[me] = contract(m.pick[0], value, *TRANSPOSED).astype(BF16)
        send[...] = contract(m.pick[1], value, *TRANSPOSED).astype(BF16)
        wires.start(send, ref.at[me], twin_base + slot, p.twin)

    def left_of(ref):
        return [merged(ref[core]) for core in (0, 1)]

    def normal(h):
        centred = h - jnp.mean(h, -1, keepdims=True)
        inv = lax.rsqrt(jnp.mean(centred * centred, -1, keepdims=True) + EPSILON)
        return centred * inv, inv

    def first_norm():
        m.par[...] = params.next()
        for copy in locs[3:]:
            copy.wait()
        wires.arrived(m.x0.at[:, p.y], swap)

        def body(i, at):
            r, half, pos = token_block(i)
            h = m.x0[r, half, pos, :].astype(F32) + time[r]
            m.res_in[at, :] = h
            m.normed1[at, :] = (normal(h)[0] * m.par[0:1, :] + m.par[1:2, :]).astype(BF16)
            return ()

        by_rows(32, body)
        transposed(m.normed1[...], m.t1, m.t1_send, 0)

    def projected(k):
        for h in (0, 1):
            weight = merged(m.b1[:, :, :, h, :, pl.ds(PART * k, PART)])
            group, lanes = (3 * h + k) // 2, PART * ((3 * h + k) % 2)
            total = contract(m.normed1[...], weight, (1,), (0,))
            if group != 1:
                total = total + m.par[2 + group // 2:3 + group // 2, lanes:lanes + PART]
            m.qkv[:, WIDTH * group + lanes:WIDTH * group + lanes + PART] = total.astype(BF16)

    low = (lax.broadcasted_iota(jnp.int32, (1, 128), 1) < HEAD_DIM).astype(F32)
    heads_of = [low.astype(BF16), (1.0 - low).astype(BF16)]

    def two_heads(value):
        return jnp.concatenate([value * h for h in heads_of], 0)

    def side_by_side(value):
        return jnp.concatenate([value[:128], value[128:]], 1)

    def at_pair(i):
        return pl.ds(pl.multiple_of((i // 6) * 128, 128), 128), [
            pl.ds(pl.multiple_of((i % 6) * 128 + WIDTH * part, 128), 128) for part in range(3)]

    def attention(first, last):
        def body(i, _):
            rows, (cq, ck, cv) = at_pair(i)
            q2, k, v = two_heads(m.qkv[rows, cq]), m.qkv[rows, ck], m.qkv[rows, cv]
            scores = contract(q2, k, *TRANSPOSED) * scale
            same = ids_down[rows, :] == ids_along[i // 6]
            masked = jnp.where(jnp.concatenate([same, same], 0), scores, NEG_FILL)
            e = jnp.exp(masked - jnp.max(masked, -1, keepdims=True))
            probs = e / jnp.sum(e, -1, keepdims=True)
            m.probs[i] = probs
            m.att[rows, cq] = contract(side_by_side(probs.astype(BF16)), two_heads(v), (1,), (0,)).astype(BF16)
            return 0

        lax.fori_loop(first, last, body, 0)

    def out_half(h):
        return merged(m.b1[:, :, :, h, :, pl.ds(3 * PART, PART)])

    def branch():
        transposed(m.att[...], m.to, m.to_send, 1)
        for h in (0, 1):
            at = slice(PART * h, PART * h + PART)
            total = contract(m.att[...], out_half(h), (1,), (0,)) + m.par[4:5, at]
            m.res_mid[:, at] = m.res_in[:, at] + total

        def body(i, at):
            m.normed2[at, :] = (normal(m.res_mid[at, :])[0] * m.par[5:6, :] + m.par[6:7, :]).astype(BF16)
            return ()

        by_rows(32, body)
        transposed(m.normed2[...], m.t2, m.t2_send, 2)

    def up_part(k):
        for h in (0, 1):
            first = 1536 * h + PART * k
            cols, lanes = slice(first, first + PART), first % WIDTH
            weight = merged(m.b2[:, :, :, h, :, pl.ds(PART * k, PART)])
            bias = m.par[7 + first // WIDTH:8 + first // WIDTH, lanes:lanes + PART]
            m.slope[:, cols] = contract(m.normed2[...], weight, (1,), (0,)) + bias

            def body(i, at):
                v = m.slope[at, cols]
                cdf = 0.5 + 0.5 * lax.erf(v * math.sqrt(0.5))
                m.act[at, cols] = (v * cdf).astype(BF16)
                m.slope[at, cols] = cdf + v * jnp.exp(-0.5 * v * v) * (1.0 / math.sqrt(2 * math.pi))
                return ()

            by_rows(32, body)
            z, x = (first // PART) // 2, (first // PART) % 2
            act = m.act[:, cols]
            for side, c in ((0, me), (1, twin)):
                picked = contract(m.pick_act[side], act, *TRANSPOSED).astype(BF16)
                for y in (0, 1):
                    role = p.role(c, x, y)
                    piece = picked[96 * y:96 * y + 96]
                    if side == 0:
                        m.ta[me, role, z] = piece
                    else:
                        m.ta_send[role, z] = piece

    def cot_whole():
        wires.arrived(m.cot.at[me, :, p.y], swap + 1)
        wires.start(m.cot.at[me], m.cot.at[me], twin_base + 3, p.twin)

    def act_out():
        wires.start(m.ta_send, m.ta.at[me], twin_base + 4, p.twin)

    def scatter_of(kind, first, wide, out, out_first):
        cols, out_cols = pl.ds(first, wide), pl.ds(out_first, wide)
        if kind == 0:
            return Scatter(wires, p, 96, cols, m.keep_d, m.s1_d, m.r1_d, m.s2_d, m.r2_d, m.sz_d, m.rz_d, out, out_cols)
        if kind == 1:
            return Scatter(wires, p, 24, cols, m.keep_u, m.s1_u, m.r1_u, m.s2_u, m.r2_u, m.sz_u, m.rz_u, out, out_cols)
        return Scatter(wires, p, 24, cols, m.slope, m.act, m.r1_m, m.s2_m, m.r2_m, m.sz_m, m.rz_m, out, out_cols)

    down = [scatter_of(0, 256 * i, 256, o_down, 256 * i) for i in range(3)]
    ups = [scatter_of(1, WIDTH * i, WIDTH, o_up, WIDTH * i) for i in range(4)]
    mixes = [scatter_of(2, WIDTH * i, WIDTH, o_mix, WIDTH * i) for i in range(3)]
    outs = scatter_of(2, 3 * WIDTH, WIDTH, o_out, 0)

    def down_grad(i):
        if i == 0:
            wires.arrived(m.cot.at[twin], twin_base + 3)
            wires.arrived(m.ta.at[twin], twin_base + 4)
            m.sums[...] = jnp.zeros(SMALL, F32)
            m.sums[11:12, :] = column_sums(merged(m.cot[me]))
        cols = pl.ds(256 * i, 256)
        down[i].begin(left_of(m.ta), [merged(m.cot[core, :, :, :, cols]) for core in (0, 1)])

    def hidden_grad(i):
        cot = merged(m.cot[me])
        for part in (2 * i, 2 * i + 1):
            cols = slice(PART * part, PART * part + PART)
            d_act = contract(cot, merged(m.b3[part // 2, part % 2]), *TRANSPOSED)
            grad = (d_act * m.slope[:, cols]).astype(BF16)
            m.d_hid[me, :, cols] = grad
            lanes = PART * (part % 2)
            m.sums[7 + i:8 + i, lanes:lanes + PART] = column_sums(grad)
        at = m.d_hid.at[me, :, pl.ds(WIDTH * i, WIDTH)]
        wires.start(at, at, twin_base + 5 + i, p.twin)

    def up_grad(i):
        if i == 0:
            wires.arrived(m.t2.at[twin], twin_base + 2)
        cols = pl.ds(WIDTH * i, WIDTH)
        wires.arrived(m.d_hid.at[twin, :, cols], twin_base + 5 + i)
        ups[i].begin(left_of(m.t2), [m.d_hid[core, :, cols] for core in (0, 1)])

    def layer_result():
        for i in range(3):
            cols = slice(256 * i, 256 * i + 256)
            total = contract(m.act[...], merged(m.b3[:, :, :, :, :, cols]), (1,), (0,)) + m.par[11:12, cols]
            total = (m.res_mid[:, cols] + total).astype(BF16)
            for r in (0, 1):
                for half in (0, 1):
                    first = r * 128 + half * 64
                    m.lo[r, half, :, cols] = total[first:first + 64]

    back = wires.slots(3)
    lo_copy = pltpu.make_async_copy(m.lo.at[:, p.y], lo_out.at[rows_own], m.local_sem.at[5])
    ig_copy = pltpu.make_async_copy(m.ig.at[:, p.y], ig_out.at[rows_own], m.local_sem.at[6])
    tg_copy = pltpu.make_async_copy(m.tg.at[p.y], tg_out.at[p.y], m.local_sem.at[7])

    def result_out():
        lo_copy.start()
        wires.start(m.lo.at[:, 1 - p.y], lo_out.at[rows_own], back, p.y_peer)

    def second_norm_back():
        halves = [merged(m.b2[:, :, :, h]) for h in (0, 1)]
        m.d_norm[...] = contract(m.d_hid[me, :, 0:1536], halves[0], *TRANSPOSED)
        m.d_norm[...] += contract(m.d_hid[me, :, 1536:3072], halves[1], *TRANSPOSED)

        def body(i, at, gain_sum, shift_sum):
            r, half, pos = token_block(i)
            norm, inv = normal(m.res_mid[at, :])
            dn = m.d_norm[at, :]
            dn_norm = dn * norm
            g, gn = dn * m.par[5:6, :], dn_norm * m.par[5:6, :]
            back_in = inv * (g - jnp.mean(g, -1, keepdims=True) - norm * jnp.mean(gn, -1, keepdims=True))
            d_mid = m.cot[me, r, half, pos, :].astype(F32) + back_in
            m.d_mid[at, :] = d_mid
            m.d_branch[me, at, :] = d_mid.astype(BF16)
            return gain_sum + folded(dn_norm), shift_sum + folded(dn)

        zero = jnp.zeros((8, WIDTH), F32)
        gain_sum, shift_sum = by_rows(32, body, zero, zero)
        m.sums[5:6, :] = jnp.sum(gain_sum, 0, keepdims=True)
        m.sums[6:7, :] = jnp.sum(shift_sum, 0, keepdims=True)
        wires.start(m.d_branch.at[me], m.d_branch.at[me], twin_base + 9, p.twin)
        d_branch = m.d_branch[me]
        m.sums[4:5, :] = column_sums(d_branch)
        d_att = contract(d_branch[:, 0:PART], out_half(0), *TRANSPOSED) + contract(d_branch[:, PART:], out_half(1), *TRANSPOSED)
        m.d_att[...] = d_att.astype(BF16)

    def out_grad():
        wires.arrived(m.to.at[twin], twin_base + 1)
        wires.arrived(m.d_branch.at[twin], twin_base + 9)
        outs.begin(left_of(m.to), [m.d_branch[core] for core in (0, 1)])

    def attention_back(first, last):
        def body(i, _):
            rows, (cq, ck, cv) = at_pair(i)
            q2, k, v = two_heads(m.qkv[rows, cq]), m.qkv[rows, ck], m.qkv[rows, cv]
            da2 = two_heads(m.d_att[rows, cq])
            probs = m.probs[i]
            d_probs = contract(da2, v, *TRANSPOSED)
            delta = jnp.sum(probs * d_probs, -1, keepdims=True)
            d_scores = (probs * (d_probs - delta)).astype(BF16)
            m.d_proj[me, rows, cq] = (contract(side_by_side(d_scores), two_heads(k), (1,), (0,)) * scale).astype(BF16)
            m.d_proj[me, rows, ck] = (contract(d_scores, q2, *TOKEN_SUM) * scale).astype(BF16)
            m.d_proj[me, rows, cv] = contract(probs.astype(BF16), da2, *TOKEN_SUM).astype(BF16)
            return 0

        lax.fori_loop(first, last, body, 0)

    def proj_out():
        for i in range(3):
            at = m.d_proj.at[me, :, pl.ds(WIDTH * i, WIDTH)]
            wires.start(at, at, twin_base + 10 + i, p.twin)

    def mix_grad(i):
        if i == 0:
            wires.arrived(m.t1.at[twin], twin_base)
        cols = pl.ds(WIDTH * i, WIDTH)
        if i != 1:
            m.sums[2 + i // 2:3 + i // 2, :] = column_sums(m.d_proj[me, :, cols])
        wires.arrived(m.d_proj.at[twin, :, cols], twin_base + 10 + i)
        mixes[i].begin(left_of(m.t1), [m.d_proj[core, :, cols] for core in (0, 1)])

    def first_norm_back():
        halves = [merged(m.b1[:, :, :, h, :, 0:3 * PART]) for h in (0, 1)]
        m.d_norm[...] = contract(m.d_proj[me, :, 0:3 * PART], halves[0], *TRANSPOSED)
        m.d_norm[...] += contract(m.d_proj[me, :, 3 * PART:], halves[1], *TRANSPOSED)

        def body(i, at, gain_sum, shift_sum, row_sum):
            r, half, pos = token_block(i)
            norm, inv = normal(m.res_in[at, :])
            dn = m.d_norm[at, :]
            dn_norm = dn * norm
            g, gn = dn * m.par[0:1, :], dn_norm * m.par[0:1, :]
            grad = m.d_mid[at, :] + inv * (g - jnp.mean(g, -1, keepdims=True) - norm * jnp.mean(gn, -1, keepdims=True))
            m.ig[r, half, pos, :] = grad
            sums = folded(grad)
            first = (r == 0).astype(F32)
            return (gain_sum + folded(dn_norm), shift_sum + folded(dn),
                    row_sum + jnp.concatenate([sums * first, sums * (1.0 - first)], 0))

        zero = jnp.zeros((8, WIDTH), F32)
        gain_sum, shift_sum, row_sum = by_rows(32, body, zero, zero, jnp.zeros((16, WIDTH), F32))
        m.sums[0:1, :] = jnp.sum(gain_sum, 0, keepdims=True)
        m.sums[1:2, :] = jnp.sum(shift_sum, 0, keepdims=True)
        for r in (0, 1):
            total = jnp.sum(row_sum[8 * r:8 * r + 8], 0, keepdims=True)
            for half in (0, 1):
                m.tg[half, r:r + 1, :] = total[:, PART * half:PART * half + PART]
        ig_copy.start()
        wires.start(m.ig.at[:, 1 - p.y], ig_out.at[rows_own], back + 1, p.y_peer)
        tg_copy.start()
        wires.start(m.tg.at[1 - p.y], tg_out.at[p.y], back + 2, p.y_peer)

    totals = Butterfly(wires, p, m.sum_send, m.sum_recv)

    for copy in locs[:3]:
        copy.wait()
    z_step(0)
    params.next()
    z_step(1)
    near_step(0)
    params.next()
    z_step(2)
    near_step(1)
    params.next()
    params.next()
    first_norm()
    far_step(0)
    projected(0)
    z_step(3)
    near_step(2)
    far_step(1)
    projected(1)
    cot_whole()
    z_step(4)
    near_step(3)
    far_step(2)
    projected(2)
    attention(0, 4)
    z_step(5)
    near_step(4)
    attention(4, 8)
    far_step(3)
    attention(8, 12)
    z_step(6)
    near_step(5)
    branch()
    far_step(4)
    up_part(0)
    z_step(7)
    near_step(6)
    far_step(5)
    up_part(1)
    z_step(8)
    near_step(7)
    far_step(6)
    up_part(2)
    z_step(9)
    near_step(8)
    far_step(7)
    up_part(3)
    act_out()
    z_step(10)
    near_step(9)
    down_grad(0)
    far_step(8)
    near_step(10)
    down_grad(1)
    far_step(9)
    down_grad(2)
    down[0].after_far()
    far_step(10)
    hidden_grad(0)
    hidden_grad(1)
    down[1].after_far()
    down[0].after_near()
    up_grad(0)
    hidden_grad(2)
    up_grad(1)
    hidden_grad(3)
    up_grad(2)
    down[2].after_far()
    down[1].after_near()
    up_grad(3)
    layer_result()
    result_out()
    second_norm_back()
    ups[0].after_far()
    down[2].after_near()
    down[0].after_z()
    attention_back(0, 4)
    out_grad()
    ups[1].after_far()
    ups[0].after_near()
    attention_back(4, 8)
    ups[2].after_far()
    ups[1].after_near()
    attention_back(8, 12)
    proj_out()
    for i in range(3):
        mix_grad(i)
    first_norm_back()
    ups[3].after_far()
    ups[2].after_near()
    down[1].after_z()
    totals.begin(m.sums[...])
    outs.after_far()
    ups[3].after_near()
    down[2].after_z()
    totals.next()
    mixes[0].after_far()
    outs.after_near()
    ups[0].after_z()
    totals.next()
    mixes[1].after_far()
    mixes[0].after_near()
    ups[1].after_z()
    totals.next()
    mixes[2].after_far()
    mixes[1].after_near()
    ups[2].after_z()
    totals.next()
    ups[3].after_z()
    outs.after_z()
    mixes[2].after_near()
    o_small[...] = totals.next()
    for s in mixes:
        s.after_z()
    wires.arrived(lo_out.at[rows_own], back)
    wires.arrived(ig_out.at[rows_own], back + 1)
    wires.arrived(tg_out.at[p.y], back + 2)
    for copy in (lo_copy, ig_copy, tg_copy):
        copy.wait()
    wires.finish()


def pack_halves(shard):
    r, n = shard.shape
    return shard.reshape(r, 2, n // 2).transpose(1, 0, 2).reshape(2 * r, n // 2)


def place_in_zeros(shard, index):
    n = shard.shape[0]
    return lax.dynamic_update_slice(jnp.zeros((32 * n,), shard.dtype), shard, (index * n,))


def in_one_kernel(inputs, time_embed, segment_ids, cotangent, gain1, shift1, mix, mbias, out, obias, gain2, shift2, up, ubias,
                  down, dbias):
    y = lax.axis_index(SEQ)
    index = lax.axis_index(BATCH) * 2 + y
    smalls = (gain1, shift1, mbias, obias, gain2, shift2, ubias, dbias)
    flat = jnp.concatenate([place_in_zeros(v, index) for v in smalls] + [jnp.zeros((4 * WIDTH,), BF16)]).reshape(SMALL)
    w1 = jnp.concatenate([pack_halves(mix), pack_halves(out)], axis=1)
    time = lax.dynamic_slice_in_dim(time_embed, 2 * y, 2, 0).astype(F32).reshape(2, 1, WIDTH)
    ids = lax.dynamic_slice_in_dim(segment_ids, 2 * y, 2, 0)
    ids_down = jnp.broadcast_to(ids.reshape(TOKENS, 1), (TOKENS, 128))
    table = scratch_table(SLOTS)
    anywhere, vmem = pl.BlockSpec(memory_space=pl.ANY), pl.BlockSpec(memory_space=pltpu.VMEM)
    tokens = inputs.shape
    o_mix, o_out, o_up, o_down, sums, lo, ig, tg = pl.pallas_call(
        partial(layer_kernel, [name for name, _, _ in table]),
        out_shape=[jax.ShapeDtypeStruct(w.shape, F32) for w in (mix, out, up, down)]
        + [jax.ShapeDtypeStruct(SMALL, F32), jax.ShapeDtypeStruct(tokens, BF16), jax.ShapeDtypeStruct(tokens, F32),
           jax.ShapeDtypeStruct((2, 8, PART), F32)],
        in_specs=[vmem] * 7 + [anywhere] * 2,
        out_specs=[vmem] * 5 + [anywhere] * 3,
        scratch_shapes=[pltpu.SemaphoreType.DMA(shape) if kind is None else pltpu.VMEM(shape, kind) for _, shape, kind in table],
        compiler_params=pltpu.CompilerParams(collective_id=0, has_side_effects=True, vmem_limit_bytes=60 * 2**20),
    )(w1, pack_halves(up), down, flat, time, ids_down, ids.reshape(2, 1, 128), inputs, cotangent)
    parts, at = [], 0
    flat = sums.reshape(-1)
    for v in smalls:
        n = v.shape[0]
        parts.append(lax.dynamic_slice(flat, (at + index * n,), (n,)))
        at += 32 * n
    time_grad = tg[:, :2].reshape(4, PART)
    return (lo, ig, time_grad, parts[0], parts[1], o_mix, parts[2], o_out, parts[3], parts[4], parts[5], o_up, parts[6], o_down,
            parts[7])


def solution(mesh):
    fits = mesh.shape[BATCH] == 16 and mesh.shape[SEQ] == 2
    tokens, rows, vector, matrix = P(BATCH, SEQ, None), P(BATCH, None), P(AXES), P(AXES, None)
    params = (vector, vector, matrix, vector, matrix, vector, vector, vector, matrix, vector, matrix, vector)
    return jax.shard_map(
        in_one_kernel if fits else any_mesh,
        mesh=mesh,
        in_specs=(tokens, rows, rows, tokens) + params,
        out_specs=(tokens, tokens, P(BATCH, SEQ)) + params,
        check_vma=False,
    )
```

time: 410 us -> 200 us (0.49); the launches traced: 405 us -> 199 us
  local copies, waits for them, and re-layouts: 128 us -> 21.4 us
  matrix products: 42.1 us -> 0 us
  other arithmetic: 39 us -> 0.68 us
  Pallas kernels: 193 us -> 176 us
    dot_general x18 -> x0, matrix products: 42.1 us -> none  [contract(): lax.dot_general(a, b, ((over_a, over_b), batch), preferred_element_type=F32)]
    reshape x26 -> x4, local copies, waits for them, and re-layouts: 44.5 us -> 2.66 us  [the longest x1 0.8 us: in_one_kernel(): flat = sums.reshape(-1)]
    unnamed x165 -> x50, local copies, waits for them, and re-layouts: 38.4 us -> 12.6 us
    transpose x4 -> x0, other arithmetic: 16.2 us -> none  [split_grad(): total = total.transpose(1, 2, 0, 3, 4)]
    pallas_call x2 -> x1, Pallas kernels: 193 us -> 176 us  [in_one_kernel(): pl.pallas_call(partial(layer_kernel, [name for name, _, _ in table]), out...]
    reduce_sum x8 -> x0, other arithmetic: 11.7 us -> none  [the longest x4 7.15 us: col(): return jnp.sum(t.astype(F32), axis=0)]
    convert_element_type x8 -> x0, local copies, waits for them, and re-layouts: 10.3 us -> none  [the longest x4 6.96 us: split_grad(): other = lax.dynamic_index_in_dim(g, 1 - c, 2, keepdims=False).astype(BF16)]
    slice x9 -> x1, local copies, waits for them, and re-layouts: 10.8 us -> 0.81 us  [in_one_kernel(): time_grad = tg[:, :2].reshape(4, PART)]
  transfers between devices with their start and end apart: 4 -> 0, of which waited for: 0 -> 0; matrix products, arithmetic and copies ran while one was open for 24% -> 0% of each run, Pallas kernels for 0% -> 0%
where the time goes in v2:
time: 200 us; the launch traced here: 199 us
  Pallas kernels  176 us (88%)
  local copies, waits for them, and re-layouts  21.4 us (11%)
    pallas_call x1, Pallas kernels, in_one_kernel(): pl.pallas_call(partial(layer_kernel, [name for name, _, _ in table]), out...  176 us
    unnamed x50, local copies, waits for them, and re-layouts  12.6 us

profile of v2, /device:TPU:0, one launch (start us, length us, event | category | flops | bytes accessed | tf_op | source)
XLA Modules:
  0.0 199.2 jit_solution(18213717747830102592)
XLA Ops:
  0.6 0.0 copy-start
  0.7 0.7 copy-done
  1.3 0.6 constant_dynamic-slice_fusion
  1.9 0.6 copy-done.10
  2.6 0.2 dynamic_update_slice.29
  2.7 0.6 copy-done.11
  3.4 0.2 dynamic_update_slice.28
  3.6 0.6 copy-done.12
  4.2 0.2 dynamic_update_slice.27
  4.4 0.6 copy-done.13
  5.1 0.2 dynamic_update_slice.25
  5.2 0.6 copy-done.14
  5.9 0.2 dynamic_update_slice.24
  6.1 0.2 dynamic_update_slice.31
  6.3 0.6 copy-done.16
  7.0 0.2 dynamic_update_slice.26
  7.2 0.0 copy-start.8
  7.2 0.6 reshape.80.time
  7.8 0.0 copy-done.17
  7.8 0.2 dynamic_update_slice.30
  8.0 0.2 dynamic-update-slice
  8.2 0.2 dynamic-update-slice.1
  8.4 0.3 dynamic-update-slice.2
  8.7 0.2 dynamic-update-slice.3
  8.9 0.2 dynamic-update-slice.4
  9.1 0.2 dynamic-update-slice.5
  9.3 0.3 dynamic-update-slice.6
  9.6 0.2 dynamic-update-slice.7
  9.8 0.7 reshape.73.small
  10.5 0.7 pad_maximum_fusion.w1
  11.2 0.8 broadcast_in_dim.12.ids_down
  11.9 0.7 copy.40
  12.6 176.4 %shard_map.271 = (f32[24,2304]{1,0:T(8,128)}, f32[24,768]{1,0:T(8,128)}, f32[24,3072]{1,0:T(8,128)}, f32[96,768]{1,0:T(8,128)}, f32[16,768]{1,0:T(8,128)}, /*ind...) custom-call(bf16[48,1536]{1,0:T(8,128)(2,1)} %pad_maximum_fusion.w1, ...), custom_call_target="tpu_custom_call" | custom-call | tf_op jit(solution)/shard_map/pallas_call | solution.py:862
  189.0 0.8 slice.3
  189.8 0.6 reshape.77
  190.4 0.8 reshape.78
  191.2 0.6 dynamic_slice.34
  191.8 0.6 dynamic_slice.38
  192.4 0.6 fusion
  193.0 1.8 copy.66
  194.8 0.9 copy.67
  195.6 0.3 copy-done.4
  195.9 0.7 copy.68
  196.6 0.2 copy-done.7
  196.8 0.6 copy.69
  197.5 0.7 copy.70
  198.2 0.4 copy-done.2
  198.5 0.7 copy.71
  (37 shorter events, 0.1 us)
Async XLA Ops:
  0.6 0.7 copy-start
  1.9 0.7 copy-start.10
  2.7 0.7 copy-start.11
  3.6 0.7 copy-start.12
  4.4 0.7 copy-start.13
  5.2 0.7 copy-start.14
  5.2 0.8 copy-start.15
  5.9 1.3 copy-start.9
  6.3 0.7 copy-start.16
  7.1 0.7 copy-start.17
  7.2 3.3 %copy-start.8 = (bf16[24,768]{1,0:T(8,128)(2,1)S(1)}, bf16[24,768]{1,0:T(8,128)(2,1)}, u32[]{:S(2)}) copy-start(bf16[24,768]{1,0:T(8,128)(2,1)} %param.24) | copy-start | bytes 110596
  7.8 2.7 %copy-start.6 = (bf16[24,2304]{1,0:T(8,128)(2,1)S(1)}, bf16[24,2304]{1,0:T(8,128)(2,1)}, u32[]{:S(2)}) copy-start(bf16[24,2304]{1,0:T(8,128)(2,1)} %param.22) | copy-start | bytes 331780
  10.5 1.4 copy-start.5
  189.0 5.8 %copy-start.1 = (f32[4,64,768]{2,1,0:T(8,128)S(1)}, f32[4,64,768]{2,1,0:T(8,128)}, u32[]{:S(2)}) copy-start(f32[4,64,768]{2,1,0:T(8,128)} %get-tuple-element.53) | copy-start | bytes 2359300
  194.8 1.1 copy-start.4
  195.9 0.9 copy-start.7
  195.9 1.5 copy-start.3
  197.4 1.1 copy-start.2

commit v3 on v2

--- a/solution.py
+++ b/solution.py
@@ -122,6 +122,7 @@
 Z_CHIPS = 4
 TOKENS, WIDTH, HIDDEN, PART = 256, 768, 3072, 384
 SMALL = (16, WIDTH)
+PIECE = 24
 TRANSPOSED = ((1,), (1,))
 TOKEN_SUM = ((0,), (0,))
 
@@ -131,10 +132,6 @@
         b, self.y = lax.axis_index(BATCH), lax.axis_index(SEQ)
         self.z, self.x, self.c = b // 4, (b // 2) % 2, b % 2
         z, x, c, y = self.z, self.x, self.c, self.y
-        self.x2, self.y2 = x + (1 - 2 * x) * (1 - c), y + (1 - 2 * y) * c
-        self.x3, self.y3 = x + (1 - 2 * x) * c, y + (1 - 2 * y) * (1 - c)
-        self.near = self.at(z, self.x2, c, self.y2)
-        self.far = self.at(z, self.x3, c, self.y3)
         self.twin = self.at(z, x, 1 - c, y)
         self.x_peer = self.at(z, 1 - x, c, y)
         self.y_peer = self.at(z, x, c, 1 - y)
@@ -145,6 +142,14 @@
     def at(z, x, c, y):
         return ((z * 2 + x) * 2 + c, y)
 
+    def routes(self, turn):
+        c = 1 if turn else self.c
+        x, y = self.x, self.y
+        return (x + (1 - 2 * x) * (1 - c), y + (1 - 2 * y) * c), (x + (1 - 2 * x) * c, y + (1 - 2 * y) * (1 - c))
+
+    def on_chip(self, chip):
+        return self.at(self.z, chip[0], self.c, chip[1])
+
     def role(self, c, x, y):
         dx, dy = (x + self.x) % 2, (y + self.y) % 2
         return (dx + 2 * dy) * (1 - c) + (dy + 2 * dx) * c
@@ -156,7 +161,7 @@
 
     def greet(self):
         barrier = pltpu.get_barrier_semaphore()
-        partners = self.z_peers + [self.near, self.far, self.twin]
+        partners = self.z_peers + [self.x_peer, self.y_peer, self.twin]
         for partner in partners:
             pl.semaphore_signal(barrier, inc=1, device_id=partner, device_id_type=MESH)
         pl.semaphore_wait(barrier, len(partners))
@@ -198,9 +203,10 @@
 
 
 class Gather:
-    def __init__(self, wires, place, own, buf, at, wide):
+    def __init__(self, wires, place, own, buf, at, wide, turn=False):
         self.w, self.p, self.own, self.buf, self.cols = wires, place, own, buf, pl.ds(at, wide)
         self.base, self.copies = wires.slots(10), []
+        self.near, self.far = place.routes(turn)
 
     def send(self, src, dst, slot, device):
         self.copies.append(self.w.start(src, dst, self.base + slot, device))
@@ -221,20 +227,20 @@
         for j in range(3):
             self.w.arrived(self.mine(), self.base + j)
         b = self.block(p.x, p.y, p.c)
-        self.send(b, b, 3, p.near)
-        self.send(b, b, 4, p.far)
+        self.send(b, b, 3, p.on_chip(self.near))
+        self.send(b, b, 4, p.on_chip(self.far))
         self.send(b, b, 6, p.twin)
 
     def after_near(self):
         p = self.p
-        b = self.block(p.x2, p.y2, p.c)
+        b = self.block(*self.near, p.c)
         self.w.arrived(b, self.base + 3)
-        self.send(b, b, 5, p.far)
+        self.send(b, b, 5, p.on_chip(self.far))
         self.send(b, b, 7, p.twin)
 
     def after_far(self):
         p = self.p
-        b = self.block(p.x3, p.y3, p.c)
+        b = self.block(*self.far, p.c)
         self.w.arrived(b, self.base + 4)
         self.send(b, b, 8, p.twin)
         b = self.block(1 - p.x, 1 - p.y, p.c)
@@ -256,33 +262,71 @@
                 self.buf[z, x, c, h, :, self.cols] = jnp.concatenate([v[0][part], v[1][part]], 0).astype(BF16)
 
 
+class LayerFirst(Gather):
+    def begin(self):
+        for j, chip in enumerate((self.near, self.far)):
+            self.send(self.own.at[:, self.cols], self.mine(), j, self.p.on_chip(chip))
+
+    def shard(self, chip):
+        return self.buf.at[self.p.z, chip[0], self.p.c, chip[1], :, self.cols]
+
+    def layer(self, z, c):
+        return self.buf.at[z, :, c, :, :, self.cols]
+
+    def forward(self):
+        b = self.shard(self.near)
+        self.w.arrived(b, self.base)
+        self.send(b, b, 2, self.p.on_chip(self.far))
+
+    def along_z(self):
+        p = self.p
+        self.w.arrived(self.shard(self.far), self.base + 1)
+        self.w.arrived(self.shard((1 - p.x, 1 - p.y)), self.base + 2)
+        b = self.layer(p.z, p.c)
+        for j, peer in enumerate(p.z_peers):
+            self.send(b, b, 3 + j, peer)
+        self.send(b, b, 6, p.twin)
+
+    def after_z(self):
+        p = self.p
+        for j in range(3):
+            b = self.layer(lax.rem(p.z + 3 - j, Z_CHIPS), p.c)
+            self.w.arrived(b, self.base + 3 + j)
+            self.send(b, b, 7 + j, p.twin)
+        for j in range(6, 10):
+            self.w.arrived(self.layer(p.z, 1 - p.c), self.base + j)
+
+
 class Scatter:
-    def __init__(self, wires, place, rows, cols, keep, s1, r1, s2, r2, sz, rz, out, out_cols):
+    def __init__(self, wires, place, rows, cols, keep, s1, r1, s2, r2, sz, rz, out, out_cols, turn=False):
         self.w, self.p, self.rows, self.cols, self.out_cols = wires, place, rows, cols, out_cols
         self.keep, self.s1, self.r1, self.s2, self.r2, self.sz, self.rz, self.out = keep, s1, r1, s2, r2, sz, rz, out
         self.base, self.quarter, self.packed = wires.slots(5), Z_CHIPS * rows, rows % 16 != 0
         wide = cols.size // 2 if self.packed else cols.size
         self.z_cols = pl.ds(cols.start // 2 if self.packed else cols.start, wide)
+        near, far = place.routes(turn)
+        self.near, self.far = place.on_chip(near), place.on_chip(far)
+        swapped = (1 - place.c) if turn else 0
+        self.roles = (0, 1 + swapped, 2 - swapped, 3)
 
     def begin(self, left, right):
         q = self.quarter
-        for role in range(4):
-            rows = slice(role * q, role * q + q)
-            total = contract(left[0][rows], right[0], (1,), (0,)) + contract(left[1][rows], right[1], (1,), (0,))
-            at = pl.ds((role % 2) * q, q)
-            if role < 2:
+        for i, role in enumerate(self.roles):
+            total = contract(left(0, role), right[0], (1,), (0,)) + contract(left(1, role), right[1], (1,), (0,))
+            at = pl.ds((i % 2) * q, q)
+            if i < 2:
                 self.keep[at, self.cols] = total
             else:
                 self.s1[at, self.cols] = total.astype(BF16)
         both = pl.ds(0, 2 * q)
-        self.w.start(self.s1.at[both, self.cols], self.r1.at[both, self.cols], self.base, self.p.far)
+        self.w.start(self.s1.at[both, self.cols], self.r1.at[both, self.cols], self.base, self.far)
 
     def after_far(self):
         q = self.quarter
         self.w.arrived(self.r1.at[pl.ds(0, 2 * q), self.cols], self.base)
         at = pl.ds(q, q)
         self.s2[:, self.cols] = (self.keep[at, self.cols] + self.r1[at, self.cols].astype(F32)).astype(BF16)
-        self.w.start(self.s2.at[:, self.cols], self.r2.at[:, self.cols], self.base + 1, self.p.near)
+        self.w.start(self.s2.at[:, self.cols], self.r2.at[:, self.cols], self.base + 1, self.near)
 
     def after_near(self):
         q, n = self.quarter, self.rows
@@ -313,27 +357,94 @@
         self.out[:, self.out_cols] = self.out[:, self.out_cols] + total
 
 
-class Butterfly:
-    def __init__(self, wires, place, send, recv):
-        self.w, self.send, self.recv, self.base = wires, send, recv, wires.slots(5)
-        self.peers = [place.twin, place.y_peer, place.x_peer]
-        self.peers.append(place.at(place.z + 1 - 2 * (place.z % 2), place.x, place.c, place.y))
-        self.peers.append(place.at(lax.rem(place.z + 2, Z_CHIPS), place.x, place.c, place.y))
-        self.step = 0
-
-    def begin(self, value):
-        i = self.step
-        self.send[i] = value.astype(self.send.dtype)
-        self.w.start(self.send.at[i], self.recv.at[i], self.base + i, self.peers[i])
-
-    def next(self):
-        i = self.step
-        self.w.arrived(self.recv.at[i], self.base + i)
-        value = self.send[i].astype(F32) + self.recv[i].astype(F32)
-        self.step += 1
-        if self.step < 5:
-            self.begin(value)
-        return value
+class AlongZFirst(Scatter):
+    def __init__(self, *args, zs, zr):
+        super().__init__(*args)
+        self.zs, self.zr = zs, zr
+
+    def begin(self, left, right):
+        n = self.rows
+        for role in range(4):
+            total = contract(left(0, role), right[0], (1,), (0,)) + contract(left(1, role), right[1], (1,), (0,))
+            for z in range(Z_CHIPS):
+                piece = total[z * n:z * n + n]
+                self.zs[z, role] = piece.astype(BF16)
+
+                @pl.when(z == self.p.z)
+                def _():
+                    self.keep[pl.ds(role * n, n), self.cols] = piece
+
+        for j, (z, peer) in enumerate(zip(self.p.z_slots, self.p.z_peers)):
+            self.w.start(self.zs.at[z], self.zr.at[j], self.base + 2 + j, peer)
+
+    def after_z(self):
+        n = self.rows
+        for j in range(3):
+            self.w.arrived(self.zr.at[j], self.base + 2 + j)
+        for role in range(4):
+            at = pl.ds(role * n, n)
+            total = self.keep[at, self.cols]
+            for j in range(3):
+                total = total + self.zr[j, role].astype(F32)
+            if role < 2:
+                self.keep[at, self.cols] = total
+            else:
+                self.s1[pl.ds((role - 2) * n, n), self.cols] = total.astype(BF16)
+        both = pl.ds(0, 2 * n)
+        self.w.start(self.s1.at[both, self.cols], self.r1.at[both, self.cols], self.base, self.far)
+
+    def after_far(self):
+        n = self.rows
+        self.w.arrived(self.r1.at[pl.ds(0, 2 * n), self.cols], self.base)
+        at, first = pl.ds(n, n), pl.ds(0, n)
+        self.s2[first, self.cols] = (self.keep[at, self.cols] + self.r1[at, self.cols].astype(F32)).astype(BF16)
+        self.w.start(self.s2.at[first, self.cols], self.r2.at[first, self.cols], self.base + 1, self.near)
+
+    def after_near(self):
+        at = pl.ds(0, self.rows)
+        self.w.arrived(self.r2.at[at, self.cols], self.base + 1)
+        self.out[:, self.out_cols] = (
+            self.keep[at, self.cols] + self.r1[at, self.cols].astype(F32) + self.r2[at, self.cols].astype(F32))
+
+
+class SmallScatter:
+    def __init__(self, wires, place, slabs, from_twin, s1, r1, s2, r2, sz, rz, out):
+        self.w, self.p, self.slabs, self.from_twin = wires, place, slabs, from_twin
+        self.s1, self.r1, self.s2, self.r2, self.sz, self.rz, self.out = s1, r1, s2, r2, sz, rz, out
+        self.base = wires.slots(6)
+        near, far = place.routes(False)
+        self.chips = ((place.x, place.y), near, far, (1 - place.x, 1 - place.y))
+        self.near, self.far = place.on_chip(near), place.on_chip(far)
+
+    def summed(self, role):
+        x, y = self.chips[role]
+        return self.slabs[:, x, self.p.c, y] + self.from_twin[:, x, y]
+
+    def to_twin(self):
+        self.w.start(self.slabs.at[:, :, 1 - self.p.c], self.from_twin, self.base, self.p.twin)
+
+    def begin(self):
+        self.w.arrived(self.from_twin, self.base)
+        self.s1[0], self.s1[1] = self.summed(2), self.summed(3)
+        self.w.start(self.s1, self.r1, self.base + 1, self.far)
+
+    def after_far(self):
+        self.w.arrived(self.r1, self.base + 1)
+        self.s2[...] = self.summed(1) + self.r1[1]
+        self.w.start(self.s2, self.r2, self.base + 2, self.near)
+
+    def after_near(self):
+        self.w.arrived(self.r2, self.base + 2)
+        self.sz[...] = self.summed(0) + self.r1[0] + self.r2[...]
+        for j, (z, peer) in enumerate(zip(self.p.z_slots, self.p.z_peers)):
+            self.w.start(self.sz.at[z], self.rz.at[j], self.base + 3 + j, peer)
+
+    def after_z(self):
+        total = self.sz[self.p.z]
+        for j in range(3):
+            self.w.arrived(self.rz.at[j], self.base + 3 + j)
+            total = total + self.rz[j]
+        self.out[...] = total
 
 
 def merged(value):
@@ -359,8 +470,11 @@
 def scratch_table(slots):
     k, w = WIDTH // 2, WIDTH
     return [
-        ("par_send", (5,) + SMALL, BF16), ("par_recv", (5,) + SMALL, BF16), ("par", SMALL, F32),
-        ("sum_send", (5,) + SMALL, F32), ("sum_recv", (5,) + SMALL, F32), ("sums", SMALL, F32),
+        ("par", SMALL, F32), ("sums", SMALL, F32), ("bs", (4, 2, 2, 2, 16, 128), BF16),
+        ("slabs", (4, 2, 2, 2, 16, 128), F32), ("from_twin", (4, 2, 2, 16, 128), F32), ("s1_s", (2, 4, 16, 128), F32),
+        ("r1_s", (2, 4, 16, 128), F32), ("s2_s", (4, 16, 128), F32), ("r2_s", (4, 16, 128), F32),
+        ("sz_s", (4, 16, 128), F32), ("rz_s", (3, 16, 128), F32),
+        ("w1", (48, 1536), BF16), ("w2", (48, 1536), BF16), ("same", (2, 128, 128), F32), ("time", (2, 1, w), F32),
         ("b1", (4, 2, 2, 2, 48, 1536), BF16), ("b2", (4, 2, 2, 2, 48, 1536), BF16), ("b3", (4, 2, 2, 2, 96, w), BF16),
         ("x0", (2, 2, 64, w), BF16), ("cot", (2, 2, 2, 64, w), BF16),
         ("res_in", (TOKENS, w), F32), ("normed1", (TOKENS, w), BF16), ("qkv", (TOKENS, 3 * w), BF16),
@@ -371,11 +485,12 @@
         ("to", (2, k, TOKENS), BF16), ("to_send", (k, TOKENS), BF16),
         ("t2", (2, k, TOKENS), BF16), ("t2_send", (k, TOKENS), BF16),
         ("ta", (2, 4, 4, 96, TOKENS), BF16), ("ta_send", (4, 4, 96, TOKENS), BF16),
-        ("d_hid", (2, TOKENS, HIDDEN), BF16), ("d_norm", (TOKENS, w), F32), ("d_mid", (TOKENS, w), F32),
-        ("d_branch", (2, TOKENS, w), BF16), ("d_att", (TOKENS, w), BF16), ("d_proj", (2, TOKENS, 3 * w), BF16),
-        ("lo", (2, 2, 64, w), BF16), ("ig", (2, 2, 64, w), F32), ("tg", (2, 8, PART), F32),
+        ("d_hid", (2, TOKENS, HIDDEN), BF16), ("d_norm", (TOKENS, w), F32),
+        ("d_branch", (2, TOKENS, w), BF16), ("d_proj", (2, TOKENS, 3 * w), BF16),
+        ("ig", (2, 2, 64, w), F32), ("tg", (2, 8, PART), F32),
         ("keep_d", (768, w), F32), ("s1_d", (768, w), BF16), ("r1_d", (768, w), BF16), ("s2_d", (PART, w), BF16),
         ("r2_d", (PART, w), BF16), ("sz_d", (4, 96, w), BF16), ("rz_d", (3, 96, w), BF16),
+        ("zr_d", (3, 4, 96, 256), BF16), ("ig_send", (2, 64, w), BF16),
         ("keep_u", (192, HIDDEN), F32), ("s1_u", (192, HIDDEN), BF16), ("r1_u", (192, HIDDEN), BF16),
         ("s2_u", (96, HIDDEN), BF16), ("r2_u", (96, HIDDEN), BF16), ("sz_u", (4, 48, 1536), BF16), ("rz_u", (3, 48, 1536), BF16),
         ("r1_m", (192, HIDDEN), BF16),
@@ -385,10 +500,64 @@
 
 
 SLOTS = 240
-
-
-def layer_kernel(names, w1, w2, w3, small, time, ids_down, ids_along, xin, cin,
-                 o_mix, o_out, o_up, o_down, o_small, lo_out, ig_out, tg_out, *scratch):
+AHEAD = 4
+TURNED = ()
+
+
+def iota(shape, dim):
+    return lax.broadcasted_iota(jnp.int32, shape, dim)
+
+
+def piece_place(row, device):
+    block = jnp.where(row < 6, device, jnp.where(row < 8, 2 * device + row - 6, 4 * device + row - 8))
+    first = jnp.where(row < 6, row, jnp.where(row < 8, 6, 8))
+    return jnp.where(row < 12, first + (block >> 5), -1), block & 31
+
+
+def ones_where(condition):
+    return condition.astype(F32).astype(BF16)
+
+
+def lane_piece(shape):
+    return (iota(shape, 1) * 2731) >> 16
+
+
+def every_piece():
+    shape = (128, WIDTH)
+    return ones_where(iota(shape, 1) - PIECE * lane_piece(shape) == iota(shape, 0))
+
+
+def slab_rows(first, count):
+    n = iota((SMALL[0], count), 1) + first
+    return ones_where(piece_place(n & 15, n >> 4)[0] == iota((SMALL[0], count), 0))
+
+
+def slab_places(first, count):
+    n = iota((count, WIDTH), 0) + first
+    return (piece_place(n & 15, n >> 4)[1] == lane_piece((count, WIDTH))).astype(F32)
+
+
+def whole_of(ref):
+    total = 0.0
+    for z in range(Z_CHIPS):
+        wide = contract(merged(ref[z]), every_piece(), (1,), (0,)) * slab_places(128 * z, 128)
+        total = total + contract(slab_rows(128 * z, 128), wide.astype(BF16), (1,), (0,))
+    return total
+
+
+def put_slabs(ref, whole):
+    high = whole.astype(BF16)
+    parts = (high, (whole - high.astype(F32)).astype(BF16))
+    for z in range(Z_CHIPS):
+        places, total = slab_places(128 * z, 128), 0.0
+        for part in parts:
+            wide = contract(slab_rows(128 * z, 128), part, *TOKEN_SUM) * places
+            total = total + contract(wide.astype(BF16), every_piece(), *TRANSPOSED)
+        ref[z] = total.reshape(ref.shape[1:])
+
+
+def layer_kernel(names, mix, out, up, w3, small, time, ids, xin, cin,
+                 o_mix, o_out, o_up, o_down, o_small, lo_out, ig_out, ig_there, tg_out, *scratch):
     m = SimpleNamespace(**dict(zip(names, scratch)))
     p = Place()
     p.greet()
@@ -396,7 +565,18 @@
     me, twin = p.c, 1 - p.c
     scale = 1.0 / math.sqrt(HEAD_DIM)
 
-    own, bufs = (w1, w2, w3), (m.b1, m.b2, m.b3)
+    own, bufs = (m.w1, m.w2, w3), (m.b1, m.b2, m.b3)
+    for ref, target, at in ((mix, m.w1, 0), (out, m.w1, 3 * PART), (up, m.w2, 0)):
+        half = ref.shape[1] // 2
+        value = ref[...].astype(F32)
+        target[:, at:at + half] = jnp.concatenate([value[:, :half], value[:, half:]], 0).astype(BF16)
+    plan = [(0, PART * i, PART) for i in range(4)] + [(1, PART * i, PART) for i in range(4)] + [(2, 256 * i, 256) for i in range(3)]
+    gathers = [Gather(wires, p, own[w], bufs[w], at, wide, k in TURNED) for k, (w, at, wide) in enumerate(plan[:-1])]
+    last = LayerFirst(wires, p, own[2], bufs[2], *plan[-1][1:])
+    params = Gather(wires, p, small, m.bs, 0, 128)
+    params.begin()
+    for g in gathers[:AHEAD]:
+        g.begin()
     locs = [pltpu.make_async_copy(own[i], bufs[i].at[p.z, p.x, p.c, p.y], m.local_sem.at[i]) for i in range(3)]
     rows_own, rows_other = pl.ds(2 * p.y, 2), pl.ds(2 - 2 * p.y, 2)
     locs.append(pltpu.make_async_copy(xin.at[rows_own], m.x0.at[:, p.y], m.local_sem.at[3]))
@@ -404,21 +584,16 @@
     for copy in locs:
         copy.start()
     swap = wires.slots(3)
+    small_copy = pltpu.make_async_copy(small, m.bs.at[p.z, p.x, p.c, p.y], m.local_sem.at[8])
+    small_copy.start()
     wires.start(xin.at[rows_other], m.x0.at[:, p.y], swap, p.y_peer)
-    params = Butterfly(wires, p, m.par_send, m.par_recv)
-    params.begin(small[...].astype(F32))
-
-    plan = [(0, PART * i, PART) for i in range(4)] + [(1, PART * i, PART) for i in range(4)] + [(2, 256 * i, 256) for i in range(3)]
-    gathers = [Gather(wires, p, own[w], bufs[w], at, wide) for w, at, wide in plan]
-    ahead = 3
-    for g in gathers[:ahead]:
-        g.begin()
+    last.begin()
     wires.start(cin.at[rows_other], m.cot.at[me, :, p.y], swap + 1, p.y_peer)
 
     def z_step(k):
         gathers[k].after_z()
-        if k + ahead < len(gathers):
-            gathers[k + ahead].begin()
+        if k + AHEAD < len(gathers):
+            gathers[k + AHEAD].begin()
 
     def near_step(k):
         gathers[k].after_near()
@@ -440,6 +615,12 @@
         m.pick[side] = jnp.concatenate(pieces, 0).astype(BF16)
         m.pick_act[side] = (lane_a == row_a + c * 192).astype(F32).astype(BF16)
 
+    for r in (0, 1):
+        m.time[r] = jnp.where(p.y == 0, time[r:r + 1, :].astype(F32), time[r + 2:r + 3, :].astype(F32))
+        along = jnp.where(p.y == 0, ids[r:r + 1, :], ids[r + 2:r + 3, :])
+        one_hot = (lax.broadcasted_iota(jnp.int32, (8, 128), 0) == along).astype(F32).astype(BF16)
+        m.same[r] = contract(one_hot, one_hot, *TOKEN_SUM)
+
     twin_base = wires.slots(16)
 
     def transposed(value, ref, send, slot):
@@ -447,8 +628,11 @@
         send[...] = contract(m.pick[1], value, *TRANSPOSED).astype(BF16)
         wires.start(send, ref.at[me], twin_base + slot, p.twin)
 
-    def left_of(ref):
-        return [merged(ref[core]) for core in (0, 1)]
+    def left_of(ref, quarter=96):
+        return lambda core, role: ref[core, pl.ds(role * quarter, quarter), :]
+
+    def left_act(core, role):
+        return merged(m.ta[core, role])
 
     def normal(h):
         centred = h - jnp.mean(h, -1, keepdims=True)
@@ -456,14 +640,14 @@
         return centred * inv, inv
 
     def first_norm():
-        m.par[...] = params.next()
+        m.par[...] = whole_of(m.bs)
         for copy in locs[3:]:
             copy.wait()
         wires.arrived(m.x0.at[:, p.y], swap)
 
         def body(i, at):
             r, half, pos = token_block(i)
-            h = m.x0[r, half, pos, :].astype(F32) + time[r]
+            h = m.x0[r, half, pos, :].astype(F32) + m.time[r]
             m.res_in[at, :] = h
             m.normed1[at, :] = (normal(h)[0] * m.par[0:1, :] + m.par[1:2, :]).astype(BF16)
             return ()
@@ -477,7 +661,7 @@
             group, lanes = (3 * h + k) // 2, PART * ((3 * h + k) % 2)
             total = contract(m.normed1[...], weight, (1,), (0,))
             if group != 1:
-                total = total + m.par[2 + group // 2:3 + group // 2, lanes:lanes + PART]
+                total = total + m.par[6 + group // 2:7 + group // 2, lanes:lanes + PART]
             m.qkv[:, WIDTH * group + lanes:WIDTH * group + lanes + PART] = total.astype(BF16)
 
     low = (lax.broadcasted_iota(jnp.int32, (1, 128), 1) < HEAD_DIM).astype(F32)
@@ -498,7 +682,7 @@
             rows, (cq, ck, cv) = at_pair(i)
             q2, k, v = two_heads(m.qkv[rows, cq]), m.qkv[rows, ck], m.qkv[rows, cv]
             scores = contract(q2, k, *TRANSPOSED) * scale
-            same = ids_down[rows, :] == ids_along[i // 6]
+            same = m.same[i // 6] > 0.5
             masked = jnp.where(jnp.concatenate([same, same], 0), scores, NEG_FILL)
             e = jnp.exp(masked - jnp.max(masked, -1, keepdims=True))
             probs = e / jnp.sum(e, -1, keepdims=True)
@@ -515,11 +699,11 @@
         transposed(m.att[...], m.to, m.to_send, 1)
         for h in (0, 1):
             at = slice(PART * h, PART * h + PART)
-            total = contract(m.att[...], out_half(h), (1,), (0,)) + m.par[4:5, at]
+            total = contract(m.att[...], out_half(h), (1,), (0,)) + m.par[2:3, at]
             m.res_mid[:, at] = m.res_in[:, at] + total
 
         def body(i, at):
-            m.normed2[at, :] = (normal(m.res_mid[at, :])[0] * m.par[5:6, :] + m.par[6:7, :]).astype(BF16)
+            m.normed2[at, :] = (normal(m.res_mid[at, :])[0] * m.par[3:4, :] + m.par[4:5, :]).astype(BF16)
             return ()
 
         by_rows(32, body)
@@ -530,7 +714,7 @@
             first = 1536 * h + PART * k
             cols, lanes = slice(first, first + PART), first % WIDTH
             weight = merged(m.b2[:, :, :, h, :, pl.ds(PART * k, PART)])
-            bias = m.par[7 + first // WIDTH:8 + first // WIDTH, lanes:lanes + PART]
+            bias = m.par[8 + first // WIDTH:9 + first // WIDTH, lanes:lanes + PART]
             m.slope[:, cols] = contract(m.normed2[...], weight, (1,), (0,)) + bias
 
             def body(i, at):
@@ -557,13 +741,16 @@
         wires.arrived(m.cot.at[me, :, p.y], swap + 1)
         wires.start(m.cot.at[me], m.cot.at[me], twin_base + 3, p.twin)
 
+    twin_act = []
+
     def act_out():
-        wires.start(m.ta_send, m.ta.at[me], twin_base + 4, p.twin)
+        twin_act.append(wires.start(m.ta_send, m.ta.at[me], twin_base + 4, p.twin))
 
     def scatter_of(kind, first, wide, out, out_first):
         cols, out_cols = pl.ds(first, wide), pl.ds(out_first, wide)
         if kind == 0:
-            return Scatter(wires, p, 96, cols, m.keep_d, m.s1_d, m.r1_d, m.s2_d, m.r2_d, m.sz_d, m.rz_d, out, out_cols)
+            args = wires, p, 96, cols, m.keep_d, m.s1_d, m.r1_d, m.s2_d, m.r2_d, m.sz_d, m.rz_d, out, out_cols
+            return Scatter(*args) if first else AlongZFirst(*args, zs=m.ta_send, zr=m.zr_d)
         if kind == 1:
             return Scatter(wires, p, 24, cols, m.keep_u, m.s1_u, m.r1_u, m.s2_u, m.r2_u, m.sz_u, m.rz_u, out, out_cols)
         return Scatter(wires, p, 24, cols, m.slope, m.act, m.r1_m, m.s2_m, m.r2_m, m.sz_m, m.rz_m, out, out_cols)
@@ -577,10 +764,11 @@
         if i == 0:
             wires.arrived(m.cot.at[twin], twin_base + 3)
             wires.arrived(m.ta.at[twin], twin_base + 4)
+            wires.left(twin_act)
             m.sums[...] = jnp.zeros(SMALL, F32)
-            m.sums[11:12, :] = column_sums(merged(m.cot[me]))
+            m.sums[5:6, :] = column_sums(merged(m.cot[me]))
         cols = pl.ds(256 * i, 256)
-        down[i].begin(left_of(m.ta), [merged(m.cot[core, :, :, :, cols]) for core in (0, 1)])
+        down[i].begin(left_act, [merged(m.cot[core, :, :, :, cols]) for core in (0, 1)])
 
     def hidden_grad(i):
         cot = merged(m.cot[me])
@@ -590,7 +778,7 @@
             grad = (d_act * m.slope[:, cols]).astype(BF16)
             m.d_hid[me, :, cols] = grad
             lanes = PART * (part % 2)
-            m.sums[7 + i:8 + i, lanes:lanes + PART] = column_sums(grad)
+            m.sums[8 + i:9 + i, lanes:lanes + PART] = column_sums(grad)
         at = m.d_hid.at[me, :, pl.ds(WIDTH * i, WIDTH)]
         wires.start(at, at, twin_base + 5 + i, p.twin)
 
@@ -604,21 +792,21 @@
     def layer_result():
         for i in range(3):
             cols = slice(256 * i, 256 * i + 256)
-            total = contract(m.act[...], merged(m.b3[:, :, :, :, :, cols]), (1,), (0,)) + m.par[11:12, cols]
+            total = contract(m.act[...], merged(m.b3[:, :, :, :, :, cols]), (1,), (0,)) + m.par[5:6, cols]
             total = (m.res_mid[:, cols] + total).astype(BF16)
             for r in (0, 1):
                 for half in (0, 1):
                     first = r * 128 + half * 64
-                    m.lo[r, half, :, cols] = total[first:first + 64]
+                    m.x0[r, half, :, cols] = total[first:first + 64]
 
     back = wires.slots(3)
-    lo_copy = pltpu.make_async_copy(m.lo.at[:, p.y], lo_out.at[rows_own], m.local_sem.at[5])
-    ig_copy = pltpu.make_async_copy(m.ig.at[:, p.y], ig_out.at[rows_own], m.local_sem.at[6])
+    lo_copy = pltpu.make_async_copy(m.x0.at[:, p.y], lo_out.at[rows_own], m.local_sem.at[5])
+    ig_copy = pltpu.make_async_copy(m.ig.at[:, p.y], ig_out, m.local_sem.at[6])
     tg_copy = pltpu.make_async_copy(m.tg.at[p.y], tg_out.at[p.y], m.local_sem.at[7])
 
     def result_out():
         lo_copy.start()
-        wires.start(m.lo.at[:, 1 - p.y], lo_out.at[rows_own], back, p.y_peer)
+        wires.start(m.x0.at[:, 1 - p.y], lo_out.at[rows_own], back, p.y_peer)
 
     def second_norm_back():
         halves = [merged(m.b2[:, :, :, h]) for h in (0, 1)]
@@ -630,22 +818,22 @@
             norm, inv = normal(m.res_mid[at, :])
             dn = m.d_norm[at, :]
             dn_norm = dn * norm
-            g, gn = dn * m.par[5:6, :], dn_norm * m.par[5:6, :]
+            g, gn = dn * m.par[3:4, :], dn_norm * m.par[3:4, :]
             back_in = inv * (g - jnp.mean(g, -1, keepdims=True) - norm * jnp.mean(gn, -1, keepdims=True))
             d_mid = m.cot[me, r, half, pos, :].astype(F32) + back_in
-            m.d_mid[at, :] = d_mid
+            m.res_mid[at, :] = d_mid
             m.d_branch[me, at, :] = d_mid.astype(BF16)
             return gain_sum + folded(dn_norm), shift_sum + folded(dn)
 
         zero = jnp.zeros((8, WIDTH), F32)
         gain_sum, shift_sum = by_rows(32, body, zero, zero)
-        m.sums[5:6, :] = jnp.sum(gain_sum, 0, keepdims=True)
-        m.sums[6:7, :] = jnp.sum(shift_sum, 0, keepdims=True)
+        m.sums[3:4, :] = jnp.sum(gain_sum, 0, keepdims=True)
+        m.sums[4:5, :] = jnp.sum(shift_sum, 0, keepdims=True)
         wires.start(m.d_branch.at[me], m.d_branch.at[me], twin_base + 9, p.twin)
         d_branch = m.d_branch[me]
-        m.sums[4:5, :] = column_sums(d_branch)
+        m.sums[2:3, :] = column_sums(d_branch)
         d_att = contract(d_branch[:, 0:PART], out_half(0), *TRANSPOSED) + contract(d_branch[:, PART:], out_half(1), *TRANSPOSED)
-        m.d_att[...] = d_att.astype(BF16)
+        m.normed2[...] = d_att.astype(BF16)
 
     def out_grad():
         wires.arrived(m.to.at[twin], twin_base + 1)
@@ -656,7 +844,7 @@
         def body(i, _):
             rows, (cq, ck, cv) = at_pair(i)
             q2, k, v = two_heads(m.qkv[rows, cq]), m.qkv[rows, ck], m.qkv[rows, cv]
-            da2 = two_heads(m.d_att[rows, cq])
+            da2 = two_heads(m.normed2[rows, cq])
             probs = m.probs[i]
             d_probs = contract(da2, v, *TRANSPOSED)
             delta = jnp.sum(probs * d_probs, -1, keepdims=True)
@@ -678,7 +866,7 @@
             wires.arrived(m.t1.at[twin], twin_base)
         cols = pl.ds(WIDTH * i, WIDTH)
         if i != 1:
-            m.sums[2 + i // 2:3 + i // 2, :] = column_sums(m.d_proj[me, :, cols])
+            m.sums[6 + i // 2:7 + i // 2, :] = column_sums(m.d_proj[me, :, cols])
         wires.arrived(m.d_proj.at[twin, :, cols], twin_base + 10 + i)
         mixes[i].begin(left_of(m.t1), [m.d_proj[core, :, cols] for core in (0, 1)])
 
@@ -693,7 +881,7 @@
             dn = m.d_norm[at, :]
             dn_norm = dn * norm
             g, gn = dn * m.par[0:1, :], dn_norm * m.par[0:1, :]
-            grad = m.d_mid[at, :] + inv * (g - jnp.mean(g, -1, keepdims=True) - norm * jnp.mean(gn, -1, keepdims=True))
+            grad = m.res_mid[at, :] + inv * (g - jnp.mean(g, -1, keepdims=True) - norm * jnp.mean(gn, -1, keepdims=True))
             m.ig[r, half, pos, :] = grad
             sums = folded(grad)
             first = (r == 0).astype(F32)
@@ -709,23 +897,29 @@
             for half in (0, 1):
                 m.tg[half, r:r + 1, :] = total[:, PART * half:PART * half + PART]
         ig_copy.start()
-        wires.start(m.ig.at[:, 1 - p.y], ig_out.at[rows_own], back + 1, p.y_peer)
+        m.ig_send[...] = m.ig[:, 1 - p.y].astype(BF16)
+        wires.start(m.ig_send, ig_there, back + 1, p.y_peer)
         tg_copy.start()
         wires.start(m.tg.at[1 - p.y], tg_out.at[p.y], back + 2, p.y_peer)
 
-    totals = Butterfly(wires, p, m.sum_send, m.sum_recv)
-
+    totals = SmallScatter(wires, p, m.slabs, m.from_twin, m.s1_s, m.r1_s, m.s2_s, m.r2_s, m.sz_s, m.rz_s, o_small)
+
+    def small_out():
+        put_slabs(m.slabs, m.sums[...])
+        totals.to_twin()
+
+    small_copy.wait()
     for copy in locs[:3]:
         copy.wait()
+    params.after_z()
     z_step(0)
-    params.next()
+    params.after_near()
+    last.forward()
     z_step(1)
     near_step(0)
-    params.next()
+    params.after_far()
     z_step(2)
     near_step(1)
-    params.next()
-    params.next()
     first_norm()
     far_step(0)
     projected(0)
@@ -745,6 +939,7 @@
     far_step(3)
     attention(8, 12)
     z_step(6)
+    last.along_z()
     near_step(5)
     branch()
     far_step(4)
@@ -762,36 +957,33 @@
     far_step(7)
     up_part(3)
     act_out()
-    z_step(10)
+    down_grad(0)
     near_step(9)
-    down_grad(0)
+    down_grad(1)
+    down_grad(2)
     far_step(8)
-    near_step(10)
-    down_grad(1)
+    down[1].after_far()
     far_step(9)
-    down_grad(2)
-    down[0].after_far()
-    far_step(10)
+    down[2].after_far()
+    last.after_z()
     hidden_grad(0)
     hidden_grad(1)
-    down[1].after_far()
-    down[0].after_near()
     up_grad(0)
+    down[1].after_near()
     hidden_grad(2)
     up_grad(1)
     hidden_grad(3)
     up_grad(2)
-    down[2].after_far()
-    down[1].after_near()
+    down[2].after_near()
     up_grad(3)
     layer_result()
     result_out()
     second_norm_back()
+    down[1].after_z()
     ups[0].after_far()
-    down[2].after_near()
-    down[0].after_z()
     attention_back(0, 4)
     out_grad()
+    down[0].after_z()
     ups[1].after_far()
     ups[0].after_near()
     attention_back(4, 8)
@@ -802,82 +994,85 @@
     for i in range(3):
         mix_grad(i)
     first_norm_back()
+    small_out()
     ups[3].after_far()
     ups[2].after_near()
-    down[1].after_z()
-    totals.begin(m.sums[...])
+    totals.begin()
+    down[0].after_far()
     outs.after_far()
     ups[3].after_near()
     down[2].after_z()
-    totals.next()
     mixes[0].after_far()
     outs.after_near()
     ups[0].after_z()
-    totals.next()
+    down[0].after_near()
     mixes[1].after_far()
     mixes[0].after_near()
     ups[1].after_z()
-    totals.next()
     mixes[2].after_far()
+    totals.after_far()
     mixes[1].after_near()
     ups[2].after_z()
-    totals.next()
     ups[3].after_z()
     outs.after_z()
     mixes[2].after_near()
-    o_small[...] = totals.next()
+    totals.after_near()
     for s in mixes:
         s.after_z()
+    totals.after_z()
     wires.arrived(lo_out.at[rows_own], back)
-    wires.arrived(ig_out.at[rows_own], back + 1)
+    wires.arrived(ig_there, back + 1)
     wires.arrived(tg_out.at[p.y], back + 2)
     for copy in (lo_copy, ig_copy, tg_copy):
         copy.wait()
     wires.finish()
 
 
-def pack_halves(shard):
-    r, n = shard.shape
-    return shard.reshape(r, 2, n // 2).transpose(1, 0, 2).reshape(2 * r, n // 2)
-
-
-def place_in_zeros(shard, index):
-    n = shard.shape[0]
-    return lax.dynamic_update_slice(jnp.zeros((32 * n,), shard.dtype), shard, (index * n,))
+def results_kernel(mix, out, up, down, lo, ig, ig_there, tg, small, lo_out, ig_out, time_out, *rest):
+    gain1, shift1, o_mix, mbias, o_out, obias, gain2, shift2, o_up, ubias, o_down, dbias, wide, sem = rest
+    y = lax.axis_index(SEQ)
+    pairs = [(mix, o_mix), (out, o_out), (up, o_up), (down, o_down), (lo, lo_out), (ig, ig_out.at[pl.ds(2 * y, 2)])]
+    copies = [pltpu.make_async_copy(src, dst, sem.at[i]) for i, (src, dst) in enumerate(pairs)]
+    wide[...] = ig_there[...].astype(F32)
+    copies.append(pltpu.make_async_copy(wide, ig_out.at[pl.ds(2 - 2 * y, 2)], sem.at[len(pairs)]))
+    for copy in copies:
+        copy.start()
+    time_out[...] = jnp.concatenate([tg[0, 0:2], tg[1, 0:2]], 0)
+    first = 0
+    for ref in (gain1, shift1, obias, gain2, shift2, dbias, mbias, ubias):
+        count = ref.shape[0] // PIECE
+        ref[...] = jnp.concatenate([small[first + i:first + i + 1, :PIECE] for i in range(count)], 1)[0]
+        first += count
+    for copy in copies:
+        copy.wait()
 
 
 def in_one_kernel(inputs, time_embed, segment_ids, cotangent, gain1, shift1, mix, mbias, out, obias, gain2, shift2, up, ubias,
                   down, dbias):
-    y = lax.axis_index(SEQ)
-    index = lax.axis_index(BATCH) * 2 + y
-    smalls = (gain1, shift1, mbias, obias, gain2, shift2, ubias, dbias)
-    flat = jnp.concatenate([place_in_zeros(v, index) for v in smalls] + [jnp.zeros((4 * WIDTH,), BF16)]).reshape(SMALL)
-    w1 = jnp.concatenate([pack_halves(mix), pack_halves(out)], axis=1)
-    time = lax.dynamic_slice_in_dim(time_embed, 2 * y, 2, 0).astype(F32).reshape(2, 1, WIDTH)
-    ids = lax.dynamic_slice_in_dim(segment_ids, 2 * y, 2, 0)
-    ids_down = jnp.broadcast_to(ids.reshape(TOKENS, 1), (TOKENS, 128))
+    pieces = jnp.concatenate([v.reshape(-1, PIECE) for v in (gain1, shift1, obias, gain2, shift2, dbias, mbias, ubias)])
+    raw = jnp.pad(pieces, ((0, 16 - pieces.shape[0]), (0, 128 - PIECE)))
     table = scratch_table(SLOTS)
     anywhere, vmem = pl.BlockSpec(memory_space=pl.ANY), pl.BlockSpec(memory_space=pltpu.VMEM)
+    shape = jax.ShapeDtypeStruct
     tokens = inputs.shape
-    o_mix, o_out, o_up, o_down, sums, lo, ig, tg = pl.pallas_call(
+    here = (tokens[0] // 2,) + tokens[1:]
+    g_mix, g_out, g_up, g_down, small, lo, ig, ig_there, tg = pl.pallas_call(
         partial(layer_kernel, [name for name, _, _ in table]),
-        out_shape=[jax.ShapeDtypeStruct(w.shape, F32) for w in (mix, out, up, down)]
-        + [jax.ShapeDtypeStruct(SMALL, F32), jax.ShapeDtypeStruct(tokens, BF16), jax.ShapeDtypeStruct(tokens, F32),
-           jax.ShapeDtypeStruct((2, 8, PART), F32)],
+        out_shape=[shape(w.shape, F32) for w in (mix, out, up, down)]
+        + [shape((16, 128), F32), shape(tokens, BF16), shape(here, F32), shape(here, BF16), shape((2, 8, PART), F32)],
         in_specs=[vmem] * 7 + [anywhere] * 2,
-        out_specs=[vmem] * 5 + [anywhere] * 3,
+        out_specs=[vmem] * 5 + [anywhere] * 4,
         scratch_shapes=[pltpu.SemaphoreType.DMA(shape) if kind is None else pltpu.VMEM(shape, kind) for _, shape, kind in table],
         compiler_params=pltpu.CompilerParams(collective_id=0, has_side_effects=True, vmem_limit_bytes=60 * 2**20),
-    )(w1, pack_halves(up), down, flat, time, ids_down, ids.reshape(2, 1, 128), inputs, cotangent)
-    parts, at = [], 0
-    flat = sums.reshape(-1)
-    for v in smalls:
-        n = v.shape[0]
-        parts.append(lax.dynamic_slice(flat, (at + index * n,), (n,)))
-        at += 32 * n
-    time_grad = tg[:, :2].reshape(4, PART)
-    return (lo, ig, time_grad, parts[0], parts[1], o_mix, parts[2], o_out, parts[3], parts[4], parts[5], o_up, parts[6], o_down,
-            parts[7])
+    )(mix, out, up, down, raw, time_embed, segment_ids, inputs, cotangent)
+    params = (gain1, shift1, mix, mbias, out, obias, gain2, shift2, up, ubias, down, dbias)
+    return tuple(pl.pallas_call(
+        results_kernel,
+        out_shape=[shape(tokens, BF16), shape(tokens, F32), shape((tokens[0], PART), F32)] + [shape(w.shape, F32) for w in params],
+        in_specs=[vmem] * 9,
+        out_specs=[anywhere] * 2 + [vmem] + [anywhere if w.ndim == 2 else vmem for w in params],
+        scratch_shapes=[pltpu.VMEM(here, F32), pltpu.SemaphoreType.DMA((7,))],
+    )(g_mix, g_out, g_up, g_down, lo, ig, ig_there, tg, small))
 
 
 def solution(mesh):

time: 200 us -> 165 us (0.82)
  local copies, waits for them, and re-layouts: 21.4 us -> 2.06 us
  Pallas kernels: 176 us -> 162 us
    pallas_call x1, Pallas kernels: 176 us -> 158 us  [in_one_kernel(): pl.pallas_call(partial(layer_kernel, [name for name, _, _ in table]), out...]
    unnamed x50 -> x16, local copies, waits for them, and re-layouts: 12.6 us -> 1.24 us
    pallas_call x0 -> x1, Pallas kernels: none -> 3.48 us  [in_one_kernel(): pl.pallas_call(results_kernel, out_shape=[shape(tokens, BF16), shape(toke...]
    reshape x7 -> x2, local copies, waits for them, and re-layouts: 3.35 us -> 0.17 us  [in_one_kernel(): v.reshape(-1, PIECE)]
    dynamic_slice x4 -> x0, local copies, waits for them, and re-layouts: 2.34 us -> none  [the longest x3 1.77 us: in_one_kernel(): parts.append(lax.dynamic_slice(flat, (at + index * n,), (n,)))]
where the time goes in v3:
time: 165 us; the launch traced here: 164 us
  Pallas kernels  162 us (98%)
  local copies, waits for them, and re-layouts  2.06 us (1%)
    pallas_call x1, Pallas kernels, in_one_kernel(): pl.pallas_call(partial(layer_kernel, [name for name, _, _ in table]), out...  158 us
    pallas_call x1, Pallas kernels, in_one_kernel(): pl.pallas_call(results_kernel, out_shape=[shape(tokens, BF16), shape(toke...  3.48 us

profile of v3, /device:TPU:0, one launch (start us, length us, event | category | flops | bytes accessed | tf_op | source)
XLA Modules:
  0.0 164.5 jit_solution(5310096037552856256)
XLA Ops:
  0.6 0.0 copy-start.6
  0.7 0.0 copy-start.7
  0.7 0.6 copy-done.6
  1.3 0.0 copy-start.3
  1.3 0.0 copy-start.4
  1.3 0.0 copy-start.5
  1.3 0.1 reshape.60
  1.4 0.0 copy-done.7
  1.4 0.0 copy-start
  1.4 0.0 copy-start.1
  1.4 0.0 copy-start.2
  1.4 0.1 reshape.61
  1.5 0.5 copy-done.3
  2.0 0.0 copy-done.4
  2.0 0.0 copy-done.5
  2.0 0.1 copy-done
  2.1 0.0 copy-done.1
  2.1 0.0 copy-done.2
  2.1 0.1 concatenate.3
  2.1 0.6 pad.4.small
  2.7 158.1 %shard_map.271 = (f32[24,2304]{1,0:T(8,128)}, f32[24,768]{1,0:T(8,128)}, f32[24,3072]{1,0:T(8,128)}, f32[96,768]{1,0:T(8,128)}, f32[16,128]{1,0:T(8,128)}, /*ind...) custom-call(bf16[24,2304]{1,0:T(8,128)(2,1)} %mix.1, ...), custom_call_target="tpu_custom_call" | custom-call | tf_op jit(solution)/shard_map/pallas_call | solution.py:1059
  160.8 3.5 %shard_map.272 = (bf16[4,64,768]{2,1,0:T(8,128)(2,1)}, f32[4,64,768]{2,1,0:T(8,128)}, f32[4,384]{1,0:T(4,128)}, f32[24]{0:T(128)}, f32[24]{0:T(128)}, /*index=5*...) custom-call(f32[24,2304]{1,0:T(8,128)} %get-tuple-element.24.mix, ...), custom_call_target="tpu_custom_call" | custom-call | tf_op jit(solution)/shard_map/pallas_call | solution.py:1069
Async XLA Ops:
  0.6 0.7 copy-start.6
  0.7 0.7 copy-start.7
  1.3 0.7 copy-start.3
  1.3 0.7 copy-start.4
  1.3 0.7 copy-start.5
  1.4 0.7 copy-start
  1.4 0.7 copy-start.1
  1.4 0.7 copy-start.2

commit v4 on v3

--- a/solution.py
+++ b/solution.py
@@ -160,11 +160,12 @@
         return (self.x + dx) % 2, (self.y + dy) % 2
 
     def greet(self):
-        barrier = pltpu.get_barrier_semaphore()
-        partners = self.z_peers + [self.x_peer, self.y_peer, self.twin]
-        for partner in partners:
-            pl.semaphore_signal(barrier, inc=1, device_id=partner, device_id_type=MESH)
-        pl.semaphore_wait(barrier, len(partners))
+        self.partners = self.z_peers + [self.x_peer, self.y_peer, self.twin]
+        for partner in self.partners:
+            pl.semaphore_signal(pltpu.get_barrier_semaphore(), inc=1, device_id=partner, device_id_type=MESH)
+
+    def all_here(self):
+        pl.semaphore_wait(pltpu.get_barrier_semaphore(), len(self.partners))
 
 
 class Wires:
@@ -318,7 +319,8 @@
                 self.keep[at, self.cols] = total
             else:
                 self.s1[at, self.cols] = total.astype(BF16)
-        both = pl.ds(0, 2 * q)
+    def launch(self):
+        both = pl.ds(0, 2 * self.quarter)
         self.w.start(self.s1.at[both, self.cols], self.r1.at[both, self.cols], self.base, self.far)
 
     def after_far(self):
@@ -470,7 +472,7 @@
 def scratch_table(slots):
     k, w = WIDTH // 2, WIDTH
     return [
-        ("par", SMALL, F32), ("sums", SMALL, F32), ("bs", (4, 2, 2, 2, 16, 128), BF16),
+        ("par", SMALL, F32), ("sums", SMALL, F32), ("small", (16, 128), BF16), ("bs", (4, 2, 2, 2, 16, 128), BF16),
         ("slabs", (4, 2, 2, 2, 16, 128), F32), ("from_twin", (4, 2, 2, 16, 128), F32), ("s1_s", (2, 4, 16, 128), F32),
         ("r1_s", (2, 4, 16, 128), F32), ("s2_s", (4, 16, 128), F32), ("r2_s", (4, 16, 128), F32),
         ("sz_s", (4, 16, 128), F32), ("rz_s", (3, 16, 128), F32),
@@ -502,6 +504,7 @@
 SLOTS = 240
 AHEAD = 4
 TURNED = ()
+UPS_TURNED, MIX_TURNED = (), (1, 3)
 
 
 def iota(shape, dim):
@@ -556,7 +559,7 @@
         ref[z] = total.reshape(ref.shape[1:])
 
 
-def layer_kernel(names, mix, out, up, w3, small, time, ids, xin, cin,
+def layer_kernel(names, mix, out, up, w3, gain1, shift1, obias, gain2, shift2, dbias, mbias, ubias, time, ids, xin, cin,
                  o_mix, o_out, o_up, o_down, o_small, lo_out, ig_out, ig_there, tg_out, *scratch):
     m = SimpleNamespace(**dict(zip(names, scratch)))
     p = Place()
@@ -570,10 +573,17 @@
         half = ref.shape[1] // 2
         value = ref[...].astype(F32)
         target[:, at:at + half] = jnp.concatenate([value[:, :half], value[:, half:]], 0).astype(BF16)
+    pieces = []
+    for ref in (gain1, shift1, obias, gain2, shift2, dbias, mbias, ubias):
+        value = ref[...].astype(F32).reshape(1, ref.shape[0])
+        pieces += [value[:, at:at + PIECE] for at in range(0, ref.shape[0], PIECE)]
+    pieces.append(jnp.zeros((16 - len(pieces), PIECE), F32))
+    m.small[...] = jnp.concatenate([jnp.concatenate(pieces, 0), jnp.zeros((16, 128 - PIECE), F32)], 1).astype(BF16)
+    p.all_here()
     plan = [(0, PART * i, PART) for i in range(4)] + [(1, PART * i, PART) for i in range(4)] + [(2, 256 * i, 256) for i in range(3)]
     gathers = [Gather(wires, p, own[w], bufs[w], at, wide, k in TURNED) for k, (w, at, wide) in enumerate(plan[:-1])]
     last = LayerFirst(wires, p, own[2], bufs[2], *plan[-1][1:])
-    params = Gather(wires, p, small, m.bs, 0, 128)
+    params = Gather(wires, p, m.small, m.bs, 0, 128)
     params.begin()
     for g in gathers[:AHEAD]:
         g.begin()
@@ -584,7 +594,7 @@
     for copy in locs:
         copy.start()
     swap = wires.slots(3)
-    small_copy = pltpu.make_async_copy(small, m.bs.at[p.z, p.x, p.c, p.y], m.local_sem.at[8])
+    small_copy = pltpu.make_async_copy(m.small, m.bs.at[p.z, p.x, p.c, p.y], m.local_sem.at[8])
     small_copy.start()
     wires.start(xin.at[rows_other], m.x0.at[:, p.y], swap, p.y_peer)
     last.begin()
@@ -746,18 +756,19 @@
     def act_out():
         twin_act.append(wires.start(m.ta_send, m.ta.at[me], twin_base + 4, p.twin))
 
-    def scatter_of(kind, first, wide, out, out_first):
+    def scatter_of(kind, first, wide, out, out_first, turn=False):
         cols, out_cols = pl.ds(first, wide), pl.ds(out_first, wide)
         if kind == 0:
             args = wires, p, 96, cols, m.keep_d, m.s1_d, m.r1_d, m.s2_d, m.r2_d, m.sz_d, m.rz_d, out, out_cols
             return Scatter(*args) if first else AlongZFirst(*args, zs=m.ta_send, zr=m.zr_d)
         if kind == 1:
-            return Scatter(wires, p, 24, cols, m.keep_u, m.s1_u, m.r1_u, m.s2_u, m.r2_u, m.sz_u, m.rz_u, out, out_cols)
-        return Scatter(wires, p, 24, cols, m.slope, m.act, m.r1_m, m.s2_m, m.r2_m, m.sz_m, m.rz_m, out, out_cols)
+            return Scatter(wires, p, 24, cols, m.keep_u, m.s1_u, m.r1_u, m.s2_u, m.r2_u, m.sz_u, m.rz_u, out, out_cols, turn)
+        return Scatter(wires, p, 24, cols, m.slope, m.act, m.r1_m, m.s2_m, m.r2_m, m.sz_m, m.rz_m, out, out_cols, turn)
 
     down = [scatter_of(0, 256 * i, 256, o_down, 256 * i) for i in range(3)]
-    ups = [scatter_of(1, WIDTH * i, WIDTH, o_up, WIDTH * i) for i in range(4)]
-    mixes = [scatter_of(2, WIDTH * i, WIDTH, o_mix, WIDTH * i) for i in range(3)]
+    ups = [scatter_of(1, WIDTH * i, WIDTH, o_up, WIDTH * i, i in UPS_TURNED) for i in range(4)]
+    mix_plan = [(0, WIDTH), (WIDTH, WIDTH), (2 * WIDTH, 512), (2 * WIDTH + 512, 256)]
+    mixes = [scatter_of(2, at, wide, o_mix, at, i in MIX_TURNED) for i, (at, wide) in enumerate(mix_plan)]
     outs = scatter_of(2, 3 * WIDTH, WIDTH, o_out, 0)
 
     def down_grad(i):
@@ -789,8 +800,8 @@
         wires.arrived(m.d_hid.at[twin, :, cols], twin_base + 5 + i)
         ups[i].begin(left_of(m.t2), [m.d_hid[core, :, cols] for core in (0, 1)])
 
-    def layer_result():
-        for i in range(3):
+    def layer_result(*parts):
+        for i in parts:
             cols = slice(256 * i, 256 * i + 256)
             total = contract(m.act[...], merged(m.b3[:, :, :, :, :, cols]), (1,), (0,)) + m.par[5:6, cols]
             total = (m.res_mid[:, cols] + total).astype(BF16)
@@ -864,10 +875,12 @@
     def mix_grad(i):
         if i == 0:
             wires.arrived(m.t1.at[twin], twin_base)
-        cols = pl.ds(WIDTH * i, WIDTH)
-        if i != 1:
-            m.sums[6 + i // 2:7 + i // 2, :] = column_sums(m.d_proj[me, :, cols])
-        wires.arrived(m.d_proj.at[twin, :, cols], twin_base + 10 + i)
+        at, wide = mix_plan[i]
+        cols, whole = pl.ds(at, wide), pl.ds(at // WIDTH * WIDTH, WIDTH)
+        if i < 3:
+            if i != 1:
+                m.sums[6 + i // 2:7 + i // 2, :] = column_sums(m.d_proj[me, :, whole])
+            wires.arrived(m.d_proj.at[twin, :, whole], twin_base + 10 + i)
         mixes[i].begin(left_of(m.t1), [m.d_proj[core, :, cols] for core in (0, 1)])
 
     def first_norm_back():
@@ -960,64 +973,83 @@
     down_grad(0)
     near_step(9)
     down_grad(1)
+    down[1].launch()
     down_grad(2)
+    down[2].launch()
     far_step(8)
     down[1].after_far()
+    layer_result(0)
     far_step(9)
     down[2].after_far()
+    layer_result(1)
     last.after_z()
     hidden_grad(0)
     hidden_grad(1)
     up_grad(0)
+    ups[0].launch()
     down[1].after_near()
     hidden_grad(2)
     up_grad(1)
+    ups[1].launch()
     hidden_grad(3)
     up_grad(2)
+    ups[2].launch()
     down[2].after_near()
     up_grad(3)
-    layer_result()
+    layer_result(2)
     result_out()
     second_norm_back()
+    ups[0].after_far()
+    ups[3].launch()
     down[1].after_z()
-    ups[0].after_far()
-    attention_back(0, 4)
+    attention_back(0, 3)
     out_grad()
+    ups[1].after_far()
+    outs.launch()
+    attention_back(3, 6)
+    ups[0].after_near()
+    down[2].after_z()
+    attention_back(6, 9)
     down[0].after_z()
-    ups[1].after_far()
-    ups[0].after_near()
-    attention_back(4, 8)
     ups[2].after_far()
+    attention_back(9, 12)
     ups[1].after_near()
-    attention_back(8, 12)
     proj_out()
-    for i in range(3):
-        mix_grad(i)
+    mix_grad(0)
+    mixes[0].launch()
+    mix_grad(1)
+    ups[3].after_far()
+    mixes[1].launch()
+    ups[2].after_near()
+    ups[0].after_z()
+    mix_grad(2)
+    mix_grad(3)
+    down[0].after_far()
     first_norm_back()
     small_out()
-    ups[3].after_far()
-    ups[2].after_near()
+    outs.after_far()
+    mixes[2].launch()
+    ups[3].after_near()
+    ups[1].after_z()
     totals.begin()
-    down[0].after_far()
-    outs.after_far()
-    ups[3].after_near()
-    down[2].after_z()
+    down[0].after_near()
     mixes[0].after_far()
+    mixes[3].launch()
     outs.after_near()
-    ups[0].after_z()
-    down[0].after_near()
+    ups[2].after_z()
     mixes[1].after_far()
     mixes[0].after_near()
-    ups[1].after_z()
+    ups[3].after_z()
     mixes[2].after_far()
     totals.after_far()
     mixes[1].after_near()
-    ups[2].after_z()
-    ups[3].after_z()
     outs.after_z()
+    mixes[3].after_far()
     mixes[2].after_near()
+    mixes[0].after_z()
     totals.after_near()
-    for s in mixes:
+    mixes[3].after_near()
+    for s in mixes[1:]:
         s.after_z()
     totals.after_z()
     wires.arrived(lo_out.at[rows_own], back)
@@ -1049,8 +1081,6 @@
 
 def in_one_kernel(inputs, time_embed, segment_ids, cotangent, gain1, shift1, mix, mbias, out, obias, gain2, shift2, up, ubias,
                   down, dbias):
-    pieces = jnp.concatenate([v.reshape(-1, PIECE) for v in (gain1, shift1, obias, gain2, shift2, dbias, mbias, ubias)])
-    raw = jnp.pad(pieces, ((0, 16 - pieces.shape[0]), (0, 128 - PIECE)))
     table = scratch_table(SLOTS)
     anywhere, vmem = pl.BlockSpec(memory_space=pl.ANY), pl.BlockSpec(memory_space=pltpu.VMEM)
     shape = jax.ShapeDtypeStruct
@@ -1060,11 +1090,11 @@
         partial(layer_kernel, [name for name, _, _ in table]),
         out_shape=[shape(w.shape, F32) for w in (mix, out, up, down)]
         + [shape((16, 128), F32), shape(tokens, BF16), shape(here, F32), shape(here, BF16), shape((2, 8, PART), F32)],
-        in_specs=[vmem] * 7 + [anywhere] * 2,
+        in_specs=[vmem] * 14 + [anywhere] * 2,
         out_specs=[vmem] * 5 + [anywhere] * 4,
         scratch_shapes=[pltpu.SemaphoreType.DMA(shape) if kind is None else pltpu.VMEM(shape, kind) for _, shape, kind in table],
         compiler_params=pltpu.CompilerParams(collective_id=0, has_side_effects=True, vmem_limit_bytes=60 * 2**20),
-    )(mix, out, up, down, raw, time_embed, segment_ids, inputs, cotangent)
+    )(mix, out, up, down, gain1, shift1, obias, gain2, shift2, dbias, mbias, ubias, time_embed, segment_ids, inputs, cotangent)
     params = (gain1, shift1, mix, mbias, out, obias, gain2, shift2, up, ubias, down, dbias)
     return tuple(pl.pallas_call(
         results_kernel,

time: 165 us -> 161 us (0.976)
  local copies, waits for them, and re-layouts: 2.06 us -> 0 us
  Pallas kernels: 162 us -> 160 us
    pallas_call x1, Pallas kernels: 158 us -> 156 us  [in_one_kernel(): pl.pallas_call(partial(layer_kernel, [name for name, _, _ in table]), out...]
where the time goes in v4:
time: 161 us
  Pallas kernels  160 us (99%)
    pallas_call x1, Pallas kernels, in_one_kernel(): pl.pallas_call(partial(layer_kernel, [name for name, _, _ in table]), out...  156 us
    pallas_call x1, Pallas kernels, in_one_kernel(): pl.pallas_call(results_kernel, out_shape=[shape(tokens, BF16), shape(toke...  3.48 us

profile of v4, /device:TPU:0, one launch (start us, length us, event | category | flops | bytes accessed | tf_op | source)
XLA Modules:
  0.0 160.6 jit_solution(4872563311889196405)
XLA Ops:
  0.7 156.3 %shard_map.271 = (f32[24,2304]{1,0:T(8,128)}, f32[24,768]{1,0:T(8,128)}, f32[24,3072]{1,0:T(8,128)}, f32[96,768]{1,0:T(8,128)}, f32[16,128]{1,0:T(8,128)}, /*ind...) custom-call(bf16[24,2304]{1,0:T(8,128)(2,1)} %mix.1, ...), custom_call_target="tpu_custom_call" | custom-call | tf_op jit(solution)/shard_map/pallas_call | solution.py:1089
  157.0 3.5 %shard_map.272 = (bf16[4,64,768]{2,1,0:T(8,128)(2,1)}, f32[4,64,768]{2,1,0:T(8,128)}, f32[4,384]{1,0:T(4,128)}, f32[24]{0:T(128)}, f32[24]{0:T(128)}, /*index=5*...) custom-call(f32[24,2304]{1,0:T(8,128)} %get-tuple-element.24.mix, ...), custom_call_target="tpu_custom_call" | custom-call | tf_op jit(solution)/shard_map/pallas_call | solution.py:1099

commit v5 on v4

--- a/solution.py
+++ b/solution.py
@@ -769,7 +769,7 @@
     ups = [scatter_of(1, WIDTH * i, WIDTH, o_up, WIDTH * i, i in UPS_TURNED) for i in range(4)]
     mix_plan = [(0, WIDTH), (WIDTH, WIDTH), (2 * WIDTH, 512), (2 * WIDTH + 512, 256)]
     mixes = [scatter_of(2, at, wide, o_mix, at, i in MIX_TURNED) for i, (at, wide) in enumerate(mix_plan)]
-    outs = scatter_of(2, 3 * WIDTH, WIDTH, o_out, 0)
+    outs = scatter_of(2, 3 * WIDTH, WIDTH, o_out, 0, True)
 
     def down_grad(i):
         if i == 0:

time: 161 us -> 163 us (1.012)
  Pallas kernels: 160 us -> 162 us
    pallas_call x1, Pallas kernels: 156 us -> 158 us  [in_one_kernel(): pl.pallas_call(partial(layer_kernel, [name for name, _, _ in table]), out...]
where the time goes in v5:
time: 163 us
  Pallas kernels  162 us (99%)
    pallas_call x1, Pallas kernels, in_one_kernel(): pl.pallas_call(partial(layer_kernel, [name for name, _, _ in table]), out...  158 us
    pallas_call x1, Pallas kernels, in_one_kernel(): pl.pallas_call(results_kernel, out_shape=[shape(tokens, BF16), shape(toke...  3.48 us

profile of v5, /device:TPU:0, one launch (start us, length us, event | category | flops | bytes accessed | tf_op | source)
XLA Modules:
  0.0 162.6 jit_solution(9751624167322575525)
XLA Ops:
  0.7 158.2 %shard_map.271 = (f32[24,2304]{1,0:T(8,128)}, f32[24,768]{1,0:T(8,128)}, f32[24,3072]{1,0:T(8,128)}, f32[96,768]{1,0:T(8,128)}, f32[16,128]{1,0:T(8,128)}, /*ind...) custom-call(bf16[24,2304]{1,0:T(8,128)(2,1)} %mix.1, ...), custom_call_target="tpu_custom_call" | custom-call | tf_op jit(solution)/shard_map/pallas_call | solution.py:1089
  158.9 3.5 %shard_map.272 = (bf16[4,64,768]{2,1,0:T(8,128)(2,1)}, f32[4,64,768]{2,1,0:T(8,128)}, f32[4,384]{1,0:T(4,128)}, f32[24]{0:T(128)}, f32[24]{0:T(128)}, /*index=5*...) custom-call(f32[24,2304]{1,0:T(8,128)} %get-tuple-element.24.mix, ...), custom_call_target="tpu_custom_call" | custom-call | tf_op jit(solution)/shard_map/pallas_call | solution.py:1099
